TPU v7x, 512 devices: a whole 4x8x8 slice. The times are simulated.
512 devices in a mesh: tok: 16 (over z, core), voc: 32 (over x, y).
Axes of the slice: x: 4, y: 8, z: 8, core: 2. Of those that a mesh axis runs over, the one named last changes fastest.
Arguments:
- hidden: bfloat16 [8192, 3584], P('tok', 'voc'), may hold values from -30 to 30
- unembed: bfloat16 [3584, 8192], P(None, 'voc'), may hold values from -1 to 1
- teacher: bfloat16 [8192, 8192], P('tok', 'voc'), may hold values from -12 to 12
- teacher_lse: float32 [8192], P('tok'), may hold values from 14 to 18
- cotangent: float32 [8192], P('tok'), may hold values from -4 to 4
Outputs:
- loss: float32 [8192], P('tok')
- grad_hidden: bfloat16 [8192, 3584], P('tok', 'voc')
- grad_unembed: bfloat16 [3584, 8192], P(None, 'voc')
All inputs are finite; a program needn't handle non-finite values.
Results may differ from a plain program's by a relative error of at most 0.023.
Values may be sent and summed in bfloat16 or wider, within the bound.
No kernel may reach another device: no remote copies, remote signals or barrier semaphores. Data moves between devices by JAX's collectives and lax.ppermute only.
A program may use at most 64 MiB of HBM per device.

v0:
```python
import jax
import jax.numpy as jnp
from jax import lax
from jax.sharding import PartitionSpec as P


def body(hidden, unembed, teacher, teacher_lse, cotangent):
    gathered = lax.all_gather(hidden, "voc", axis=1, tiled=True)
    logits = jnp.dot(gathered, unembed, preferred_element_type=jnp.float32)
    teacher_f = teacher.astype(jnp.float32)
    shifted = teacher_f - teacher_lse[:, None]
    probs = jnp.exp(shifted)
    local_mass = jnp.sum(probs, axis=1)
    local_cross = jnp.sum(probs * (shifted - logits), axis=1)
    local_top = jnp.max(logits, axis=1)
    row_top = lax.pmax(local_top, "voc")
    local_total = jnp.sum(jnp.exp(logits - row_top[:, None]), axis=1)
    exp_total, cross_term, row_mass = lax.psum((local_total, local_cross, local_mass), "voc")
    student_lse = row_top + jnp.log(exp_total)
    loss = cross_term + row_mass * student_lse
    grad_logits = (
        cotangent[:, None] * (jnp.exp(logits - student_lse[:, None]) * row_mass[:, None] - probs)
    ).astype(jnp.bfloat16)
    hidden_terms = lax.dot_general(
        grad_logits, unembed, (((1,), (1,)), ((), ())), preferred_element_type=jnp.float32
    )
    grad_hidden = lax.psum_scatter(
        hidden_terms.astype(jnp.bfloat16), "voc", scatter_dimension=1, tiled=True
    )
    weight_terms = lax.dot_general(
        gathered, grad_logits, (((0,), (0,)), ((), ())), preferred_element_type=jnp.float32
    )
    grad_unembed = lax.psum(weight_terms.astype(jnp.bfloat16), "tok")
    return (loss, grad_hidden, grad_unembed)


def solution(mesh):
    placed = (P("tok", "voc"), P(None, "voc"), P("tok", "voc"), P("tok"), P("tok"))
    return jax.shard_map(
        body,
        mesh=mesh,
        in_specs=placed,
        out_specs=(P("tok"), P("tok", "voc"), P(None, "voc")),
        check_vma=False,
    )
```

profile of v0, /device:TPU:1, one launch (start us, length us, event | category | flops | bytes accessed | tf_op | source)
XLA Modules:
  0.0 601.6 jit_solution(18040906554612980268)
XLA Ops:
  7.2 0.0 copy-start
  7.2 0.0 all-gather.2.cloned.1.call-start
  7.2 0.7 all-gather.2.cloned.1.call-update
  7.9 0.0 all-reduce.3.cloned.1.call-start
  8.0 1.1 copy.8
  9.1 0.0 copy-start.1
  9.1 0.0 copy-start.2
  9.1 90.6 %all-gather.2.cloned.1.call-done = bf16[512,3584]{0,1:T(8,128)(2,1)} async-done(((bf16[512,112]{0,1:T(8,128)(2,1)}), bf16[512,3584]{0,1:T(8,128)(2,1)}) %all-gather.2.cloned.1.call-update) | async-done | bytes 3670032 | tf_op jit(solution)/shard_map/all_gather | solution.py:8
  99.7 0.0 copy-done
  99.7 3.2 fusion.3
  102.9 57.4 %pmax.7 = f32[512]{0:T(512)S(1)} all-reduce(f32[512]{0:T(512)S(1)} %get-tuple-element.14), channel_id=1, replica_groups=mesh['tok'=16,'voc'=32] {'voc'}, use_global_device_ids=true, to_apply=%region_5.0 | all-reduce | flops 512 | bytes 4096 | tf_op jit(solution)/shard_map/pmax | solution.py:16
  160.3 0.0 copy-done.1
  160.3 0.2 exponential_reduce_fusion
  160.5 56.7 %all-reduce = (f32[512]{0:T(512)S(1)}, f32[512]{0:T(512)S(1)}, f32[512]{0:T(512)S(1)}) all-reduce(f32[512]{0:T(512)S(1)} %get-tuple-element.7, f32[512]{0:T(512)S(1)} %get-tuple-element.8, f32[512]{0:T(512)S(1)} %get-tuple-element.6), channel_id=1, replica_groups=mesh['tok'=16,'voc'=32] {'voc'}, use_global_device_ids=true, to_apply=%region_1.0 | all-reduce | flops 1536 | bytes 12288 | tf_op jit(solution)/shard_map/psum | solution.py:18
  217.2 0.6 multiply_add_fusion
  217.8 0.0 copy-done.2
  217.8 0.2 multiply_convert_fusion
  218.0 4.4 fusion
  222.4 0.0 all-reduce.3.cloned.1.call-update
  222.5 0.0 reduce-scatter.2.cloned.1.call-start
  222.5 2.9 convolution_convert_fusion
  225.4 0.0 reduce-scatter.2.cloned.1.call-update
  225.5 144.1 %all-reduce.3.cloned.1.call-done = bf16[3584,256]{0,1:T(8,128)(2,1)} async-done(((bf16[3584,256]{0,1:T(8,128)(2,1)}), bf16[3584,256]{0,1:T(8,128)(2,1)}) %all-reduce.3.cloned.1.call-update) | async-done | bytes 1835024 | tf_op jit(solution)/shard_map/psum | solution.py:33
  369.6 3.8 copy.9
  373.4 221.7 %reduce-scatter.2.cloned.1.call-done = bf16[512,112]{0,1:T(8,128)(2,1)} async-done(((bf16[512,3584]{0,1:T(8,128)(2,1)}), bf16[512,112]{0,1:T(8,128)(2,1)}) %reduce-scatter.2.cloned.1.call-update) | async-done | bytes 114704 | tf_op jit(solution)/shard_map/reduce_scatter | solution.py:27
Async XLA Ops:
  7.2 92.5 %copy-start = (bf16[3584,256]{1,0:T(8,128)(2,1)S(1)}, bf16[3584,256]{1,0:T(8,128)(2,1)}, u32[]{:S(2)}) copy-start(bf16[3584,256]{1,0:T(8,128)(2,1)} %param.6) | copy-start | bytes 5505028
  7.2 92.5 %all-gather.2.cloned.1.call-start = ((), (), s32[]{:S(2)}) async-start(), calls=%async_computation.1 | async-start | bytes 3784704 | tf_op jit(solution)/shard_map/all_gather | solution.py:8
  7.9 361.7 %all-reduce.3.cloned.1.call-start = ((), (), s32[]{:S(2)}) async-start(), calls=%async_computation.3 | async-start | bytes 3670016 | tf_op jit(solution)/shard_map/psum | solution.py:33
  9.1 151.2 %copy-start.1 = (f32[512]{0:T(512)S(1)}, f32[512]{0:T(512)}, u32[]{:S(2)}) copy-start(f32[512]{0:T(512)} %param.8) | copy-start | bytes 6148
  9.1 208.8 %copy-start.2 = (f32[512]{0:T(512)S(1)}, f32[512]{0:T(512)}, u32[]{:S(2)}) copy-start(f32[512]{0:T(512)} %param.9) | copy-start | bytes 6148
  222.5 372.6 %reduce-scatter.2.cloned.1.call-start = ((), (), s32[]{:S(2)}) async-start(), calls=%async_computation.2 | async-start | bytes 3784704 | tf_op jit(solution)/shard_map/reduce_scatter | solution.py:27
Sparse Core Ops, SparseCore 0:
  11.2 88.4 all-gather.1
  222.6 146.9 all-reduce.2
  375.3 219.7 reduce-scatter.1
where the time goes:
time: 606 us; the launch traced here: 602 us
  waiting for transfers between devices  457 us (75%)
  blocking collectives  114 us (19%)
  between operations  13.8 us (2%)
  matrix products  10.5 us (2%)
    reduce_scatter x1, waiting for transfers between devices, body(): lax.psum_scatter(hidden_terms.astype(jnp.bfloat16), 'voc', scatter_dimens...  222 us
    psum x1, waiting for transfers between devices, body(): grad_unembed = lax.psum(weight_terms.astype(jnp.bfloat16), 'tok')  144 us
    all_gather x1, waiting for transfers between devices, body(): gathered = lax.all_gather(hidden, 'voc', axis=1, tiled=True)  90.6 us
    pmax x1, blocking collectives, body(): row_top = lax.pmax(local_top, 'voc')  57.4 us
    psum x1, blocking collectives, body(): lax.psum((local_total, local_cross, local_mass), 'voc')  56.7 us
  transfers between devices with their start and end apart: 3, of which 3 were waited for; matrix products, arithmetic and copies ran while one was open for 1% of the time, Pallas kernels for 0%

commit v1 on v0

v1 whole, which is shorter than its diff:
```python
import jax
import jax.numpy as jnp
from jax import lax
from jax.sharding import PartitionSpec as P

NX, NY, NZ, NC = 4, 8, 8, 2
Y_GROUPS = [[x * NY + y for y in range(NY)] for x in range(NX)]
X_GROUPS = [[x * NY + y for x in range(NX)] for y in range(NY)]
Z_GROUPS = [[z * NC + c for z in range(NZ)] for c in range(NC)]
CORE_SWAP = [(z * NC + c, z * NC + 1 - c) for z in range(NZ) for c in range(NC)]


def exchange(blocks, axis, groups):
    return lax.all_to_all(blocks, axis, 0, 0, tiled=True, axis_index_groups=groups)


def spread(block, axis, groups):
    copies = jnp.broadcast_to(block[None], (len(groups[0]),) + block.shape)
    return exchange(copies, axis, groups)


def merge(parts):
    top = jnp.max(parts[:, 0], axis=0)
    total = jnp.sum(parts[:, 1] * jnp.exp(parts[:, 0] - top[None]), axis=0)
    return jnp.stack([top, total, jnp.sum(parts[:, 2], axis=0), jnp.sum(parts[:, 3], axis=0)])


def add_up(blocks):
    return jnp.sum(blocks.astype(jnp.float32), axis=0).astype(jnp.bfloat16)


def body(hidden, unembed, teacher, teacher_lse, cotangent):
    tokens, columns = teacher.shape
    features = unembed.shape[0]
    mine = hidden.T
    row = spread(mine, "voc", Y_GROUPS).reshape(NY * mine.shape[0], tokens)
    gathered = spread(row, "voc", X_GROUPS).reshape(features, tokens)

    teacher_t = teacher.T.astype(jnp.float32)
    shifted = teacher_t - teacher_lse[None, :]
    probs = jnp.exp(shifted)
    logits = lax.dot_general(
        unembed, gathered, (((0,), (0,)), ((), ())), preferred_element_type=jnp.float32
    )
    top = jnp.max(logits, axis=0)
    total = jnp.sum(jnp.exp(logits - top[None, :]), axis=0)
    mass = jnp.sum(probs, axis=0)
    cross = jnp.sum(probs * (shifted - logits), axis=0)
    stats = jnp.stack([top, total, mass, cross])
    stats = merge(spread(stats, "voc", Y_GROUPS))
    stats = merge(spread(stats, "voc", X_GROUPS))
    row_mass = stats[2]
    student_lse = stats[0] + jnp.log(stats[1])
    loss = stats[3] + row_mass * student_lse
    grad_logits = (
        cotangent[None, :] * (jnp.exp(logits - student_lse[None, :]) * row_mass[None, :] - probs)
    ).astype(jnp.bfloat16)

    weight_terms = lax.dot_general(
        gathered, grad_logits, (((1,), (1,)), ((), ())), preferred_element_type=jnp.float32
    ).astype(jnp.bfloat16)
    core = lax.rem(lax.axis_index("tok"), NC)
    half = features // NC
    kept = lax.dynamic_slice_in_dim(weight_terms, core * half, half, 0)
    given = lax.dynamic_slice_in_dim(weight_terms, (1 - core) * half, half, 0)
    came = lax.ppermute(given, "tok", CORE_SWAP)
    chip_terms = add_up(jnp.stack([kept, came])).reshape(NZ, half // NZ, columns)

    hidden_terms = jnp.dot(unembed, grad_logits, preferred_element_type=jnp.float32).astype(jnp.bfloat16)
    rows = add_up(exchange(hidden_terms.reshape(NX, features // NX, tokens), "voc", X_GROUPS))
    grad_hidden = add_up(exchange(rows.reshape(NY, features // NX // NY, tokens), "voc", Y_GROUPS)).T

    summed = add_up(exchange(chip_terms, "tok", Z_GROUPS))
    own_half = spread(summed, "tok", Z_GROUPS).reshape(half, columns)
    other_half = lax.ppermute(own_half, "tok", CORE_SWAP)
    low = jnp.where(core == 0, own_half, other_half)
    high = jnp.where(core == 0, other_half, own_half)
    return (loss, grad_hidden, jnp.concatenate([low, high], axis=0))


def solution(mesh):
    placed = (P("tok", "voc"), P(None, "voc"), P("tok", "voc"), P("tok"), P("tok"))
    return jax.shard_map(
        body,
        mesh=mesh,
        in_specs=placed,
        out_specs=(P("tok"), P("tok", "voc"), P(None, "voc")),
        check_vma=False,
    )
```

time: 606 us -> 270 us (0.45)
  waiting for transfers between devices: 457 us -> 157 us
  blocking collectives: 114 us -> 41.8 us
  starting transfers between devices: 0.12 us -> 40.5 us
  between operations: 13.8 us -> 0.83 us
  other arithmetic: 1 us -> 9.83 us
  local copies, waits for them, and re-layouts: 4.9 us -> 11 us
    reduce_scatter x1 -> x0, waiting for transfers between devices: 222 us -> none  [body(): lax.psum_scatter(hidden_terms.astype(jnp.bfloat16), 'voc', scatter_dimens...]
    all_to_all x0 -> x6, waiting for transfers between devices: none -> 155 us  [exchange(): lax.all_to_all(blocks, axis, 0, 0, tiled=True, axis_index_groups=groups)]
    psum x1 -> x0, waiting for transfers between devices: 144 us -> none  [body(): grad_unembed = lax.psum(weight_terms.astype(jnp.bfloat16), 'tok')]
    all_gather x1 -> x0, waiting for transfers between devices: 90.6 us -> none  [body(): gathered = lax.all_gather(hidden, 'voc', axis=1, tiled=True)]
    pmax x1 -> x0, blocking collectives: 57.4 us -> none  [body(): row_top = lax.pmax(local_top, 'voc')]
    psum x1 -> x0, blocking collectives: 56.7 us -> none  [body(): lax.psum((local_total, local_cross, local_mass), 'voc')]
    all_to_all x0 -> x2, blocking collectives: none -> 41.8 us  [exchange(): lax.all_to_all(blocks, axis, 0, 0, tiled=True, axis_index_groups=groups)]
    all_to_all x0 -> x6, starting transfers between devices: none -> 31.5 us  [exchange(): lax.all_to_all(blocks, axis, 0, 0, tiled=True, axis_index_groups=groups)]
  transfers between devices with their start and end apart: 3 -> 8, of which waited for: 3 -> 7; matrix products, arithmetic and copies ran while one was open for 1% -> 3% of each run, Pallas kernels for 0% -> 0%
where the time goes in v1:
time: 270 us; the launch traced here: 269 us
  waiting for transfers between devices  157 us (58%)
  blocking collectives  41.8 us (15%)
  starting transfers between devices  40.5 us (15%)
  local copies, waits for them, and re-layouts  11 us (4%)
  other arithmetic  9.83 us (4%)
  matrix products  7.56 us (3%)
    all_to_all x6, waiting for transfers between devices, exchange(): lax.all_to_all(blocks, axis, 0, 0, tiled=True, axis_index_groups=groups)  155 us
    all_to_all x2, blocking collectives, exchange(): lax.all_to_all(blocks, axis, 0, 0, tiled=True, axis_index_groups=groups)  41.8 us
    all_to_all x6, starting transfers between devices, exchange(): lax.all_to_all(blocks, axis, 0, 0, tiled=True, axis_index_groups=groups)  31.5 us
    ppermute x1, starting transfers between devices, body(): came = lax.ppermute(given, 'tok', CORE_SWAP)  6.62 us
    reduce_sum x4, other arithmetic, add_up(): return jnp.sum(blocks.astype(jnp.float32), axis=0).astype(jnp.bfloat16)  5.68 us
  transfers between devices with their start and end apart: 8, of which 7 were waited for; matrix products, arithmetic and copies ran while one was open for 3% of the time, Pallas kernels for 0%

profile of v1, /device:TPU:1, one launch (start us, length us, event | category | flops | bytes accessed | tf_op | source)
XLA Modules:
  0.0 268.7 jit_solution(14450481801123976636)
XLA Ops:
  0.6 0.0 copy-start
  0.6 1.1 broadcast_in_dim.12
  1.8 30.9 %all_to_all.40 = bf16[8,112,512]{2,1,0:T(8,128)(2,1)S(1)} all-to-all(bf16[8,112,512]{2,1,0:T(8,128)(2,1)S(1)} %broadcast_in_dim.12), channel_id=1, replica_groups={{0,1,2,3,4,5,6,7},{8,9,10,11,12,13,14,15},{16,17,18,19,20,21,22,23},{24..., dimensions={0} | all-to-all | bytes 1835008 | tf_op jit(solution)/shard_map/all_to_all | solution.py:14
  32.7 2.1 broadcast_in_dim.14
  34.8 0.0 copy-start.2
  34.8 5.4 %all-to-all-start.1 = ((bf16[4,896,512]{2,1,0:T(8,128)(2,1)}), bf16[4,896,512]{2,1,0:T(8,128)(2,1)}, u32[]{:S(2)}, u32[]{:S(2)}) async-start(bf16[4,896,512]{2,1,0:T(8,128)(2,1)} %broadcast_in_dim.14), calls=%async_computation.1 | async-start | bytes 7340032 | tf_op jit(solution)/shard_map/all_to_all | solution.py:14
  40.2 0.0 copy-done.2
  40.2 0.1 copy.33
  40.4 41.3 %all-to-all-done.1 = bf16[4,896,512]{2,1,0:T(8,128)(2,1)} async-done(((bf16[4,896,512]{2,1,0:T(8,128)(2,1)}), bf16[4,896,512]{2,1,0:T(8,128)(2,1)}, u32[]{:S(2)}, u32[]{:S(2)}) %all-to-all-start.1) | async-done | bytes 3670048 | tf_op jit(solution)/shard_map/all_to_all | solution.py:14
  81.7 0.0 copy-done
  81.7 0.0 copy-start.3
  81.7 0.0 copy-start.4
  81.7 3.2 %fusion.12 = (f32[512]{0:T(512)S(1)}, f32[256,512]{1,0:T(8,128)S(1)}) fusion(bf16[3584,256]{1,0:T(8,128)(2,1)S(1)} %copy-done, bf16[3584,512]{1,0:T(8,128)(2,1)} %bitcast.2), kind=kOutput, calls=%fused_computation.37 | convolution fusion | flops 939654656 | bytes 6031360 | tf_op jit(solution)/shard_map/dot_general | solution.py:42
  84.9 0.0 copy-done.3
  84.9 0.2 exponential_reduce_fusion
  85.2 10.8 %all_to_all.41 = f32[8,4,512]{2,1,0:T(4,128)S(1)} all-to-all(f32[8,4,512]{2,1,0:T(4,128)S(1)} %broadcast_in_dim.15), channel_id=1, replica_groups={{0,1,2,3,4,5,6,7},{8,9,10,11,12,13,14,15},{16,17,18,19,20,21,22,23},{24..., dimensions={0} | all-to-all | bytes 131072 | tf_op jit(solution)/shard_map/all_to_all | solution.py:14
  96.0 0.1 slice_reduce_fusion.5
  96.2 0.6 broadcast_in_dim.16
  96.8 3.3 %all-to-all-start.3 = ((f32[4,4,512]{2,1,0:T(4,128)}), f32[4,4,512]{2,1,0:T(4,128)S(1)}, u32[]{:S(2)}, u32[]{:S(2)}) async-start(f32[4,4,512]{2,1,0:T(4,128)} %broadcast_in_dim.16), calls=%async_computation.3 | async-start | bytes 65536 | tf_op jit(solution)/shard_map/all_to_all | solution.py:14
  100.1 4.3 %all-to-all-done.3 = f32[4,4,512]{2,1,0:T(4,128)S(1)} async-done(((f32[4,4,512]{2,1,0:T(4,128)}), f32[4,4,512]{2,1,0:T(4,128)S(1)}, u32[]{:S(2)}, u32[]{:S(2)}) %all-to-all-start.3) | async-done | bytes 32800 | tf_op jit(solution)/shard_map/all_to_all | solution.py:14
  104.3 0.1 fusion.11
  104.4 0.6 multiply_add_fusion
  105.0 0.0 copy-done.4
  105.0 0.2 multiply_convert_fusion
  105.2 3.2 %convolution_convert_fusion.1 = bf16[256,3584]{1,0:T(8,128)(2,1)S(1)} fusion(bf16[256,512]{1,0:T(8,128)(2,1)S(1)} %multiply_convert_fusion, bf16[3584,512]{1,0:T(8,128)(2,1)} %bitcast.2), kind=kOutput, calls=%fused_computation.1 | convolution fusion | flops 940441600 | bytes 5767168 | tf_op jit(solution)/shard_map/dot_general | solution.py:59
  108.4 0.0 copy-start.1
  108.4 1.2 copy-done.1
  109.6 0.1 dynamic-slice_bitcast_fusion
  109.7 6.6 %collective-permute-start = (bf16[1792,256]{0,1:T(8,128)(2,1)S(1)}, bf16[1792,256]{0,1:T(8,128)(2,1)}, u32[]{:S(2)}, u32[]{:S(2)}) collective-permute-start(bf16[1792,256]{0,1:T(8,128)(2,1)S(1)} %dynamic-slice_bitcast_fusion), channel_id=1, source_target_pairs={{0,32},{32,0},{64,96},{96,64},{128,160},{160,128},{192,224},{224,1... | collective-permute-start | bytes 2752520 | tf_op jit(solution)/shard_map/ppermute | solution.py:66
  116.3 2.2 collective-permute-done
  118.5 1.7 bitcast_add_fusion
  120.2 1.3 copy.43
  121.5 10.3 %all-to-all-start.6 = ((bf16[8,224,256]{2,1,0:T(8,128)(2,1)}), bf16[8,224,256]{2,1,0:T(8,128)(2,1)S(1)}, u32[]{:S(2)}, u32[]{:S(2)}) async-start(bf16[8,224,256]{2,1,0:T(8,128)(2,1)} %bitcast.72), calls=%async_computation.6 | async-start | bytes 1835008 | tf_op jit(solution)/shard_map/all_to_all | solution.py:14
  131.7 1.2 convolution_convert_fusion
  132.9 2.1 copy.77
  135.0 23.1 %all-to-all-done.6 = bf16[8,224,256]{2,1,0:T(8,128)(2,1)S(1)} async-done(((bf16[8,224,256]{2,1,0:T(8,128)(2,1)}), bf16[8,224,256]{2,1,0:T(8,128)(2,1)S(1)}, u32[]{:S(2)}, u32[]{:S(2)}) %all-to-all-start.6) | async-done | bytes 917536 | tf_op jit(solution)/shard_map/all_to_all | solution.py:14
  158.1 4.7 %all-to-all-start.4 = ((bf16[4,896,512]{1,2,0:T(8,128)(2,1)}), bf16[4,896,512]{1,2,0:T(8,128)(2,1)}, u32[]{:S(2)}, u32[]{:S(2)}) async-start(bf16[4,896,512]{1,2,0:T(8,128)(2,1)} %bitcast.70), calls=%async_computation.4 | async-start | bytes 7340032 | tf_op jit(solution)/shard_map/all_to_all | solution.py:14
  162.9 0.1 reduce_sum.139
  163.0 42.7 %all-to-all-done.4 = bf16[4,896,512]{1,2,0:T(8,128)(2,1)} async-done(((bf16[4,896,512]{1,2,0:T(8,128)(2,1)}), bf16[4,896,512]{1,2,0:T(8,128)(2,1)}, u32[]{:S(2)}, u32[]{:S(2)}) %all-to-all-start.4) | async-done | bytes 3670048 | tf_op jit(solution)/shard_map/all_to_all | solution.py:14
  205.7 1.0 broadcast_in_dim.17
  206.7 4.2 %all-to-all-start.7 = ((bf16[8,224,256]{2,1,0:T(8,128)(2,1)}), bf16[8,224,256]{2,1,0:T(8,128)(2,1)}, u32[]{:S(2)}, u32[]{:S(2)}) async-start(bf16[8,224,256]{2,1,0:T(8,128)(2,1)} %broadcast_in_dim.17), calls=%async_computation.7 | async-start | bytes 1835008 | tf_op jit(solution)/shard_map/all_to_all | solution.py:14
  210.9 3.1 %reduce_sum.136 = bf16[896,512]{0,1:T(8,128)(2,1)S(1)} reduce(bf16[4,896,512]{1,2,0:T(8,128)(2,1)} %all-to-all-done.4, bf16[]{:T(256)} %constant.18.clone.1), dimensions={0}, to_apply=%region_12.0 | reduce | flops 1376256 | bytes 4587522 | tf_op jit(solution)/shard_map/reduce_sum | solution.py:29
  214.0 1.3 copy.42
  215.3 22.0 %all-to-all-done.7 = bf16[8,224,256]{2,1,0:T(8,128)(2,1)} async-done(((bf16[8,224,256]{2,1,0:T(8,128)(2,1)}), bf16[8,224,256]{2,1,0:T(8,128)(2,1)}, u32[]{:S(2)}, u32[]{:S(2)}) %all-to-all-start.7) | async-done | bytes 917536 | tf_op jit(solution)/shard_map/all_to_all | solution.py:14
  237.3 3.6 %all-to-all-start.5 = ((bf16[8,112,512]{2,1,0:T(8,128)(2,1)}), bf16[8,112,512]{2,1,0:T(8,128)(2,1)S(1)}, u32[]{:S(2)}, u32[]{:S(2)}) async-start(bf16[8,112,512]{2,1,0:T(8,128)(2,1)} %bitcast.71), calls=%async_computation.5 | async-start | bytes 1835008 | tf_op jit(solution)/shard_map/all_to_all | solution.py:14
  240.9 2.4 collective-permute-start.1
  243.3 21.7 %all-to-all-done.5 = bf16[8,112,512]{2,1,0:T(8,128)(2,1)S(1)} async-done(((bf16[8,112,512]{2,1,0:T(8,128)(2,1)}), bf16[8,112,512]{2,1,0:T(8,128)(2,1)S(1)}, u32[]{:S(2)}, u32[]{:S(2)}) %all-to-all-start.5) | async-done | bytes 917536 | tf_op jit(solution)/shard_map/all_to_all | solution.py:14
  265.0 0.8 reduce_sum.137
  265.7 0.0 collective-permute-done.1
  265.7 1.6 broadcast_select_fusion.1
  267.3 1.3 pad_maximum_fusion
  (5 shorter events, 0.1 us)
Async XLA Ops:
  0.6 81.1 %copy-start = (bf16[3584,256]{1,0:T(8,128)(2,1)S(1)}, bf16[3584,256]{1,0:T(8,128)(2,1)}, u32[]{:S(2)}) copy-start(bf16[3584,256]{1,0:T(8,128)(2,1)} %param.6) | copy-start | bytes 5505028
  34.8 5.4 %copy-start.2 = (bf16[512,256]{1,0:T(8,128)(2,1)S(1)}, bf16[512,256]{1,0:T(8,128)(2,1)}, u32[]{:S(2)}) copy-start(bf16[512,256]{1,0:T(8,128)(2,1)} %param.7) | copy-start | bytes 786436
  34.8 46.9 %all-to-all-start.1 = ((bf16[4,896,512]{2,1,0:T(8,128)(2,1)}), bf16[4,896,512]{2,1,0:T(8,128)(2,1)}, u32[]{:S(2)}, u32[]{:S(2)}) async-start(bf16[4,896,512]{2,1,0:T(8,128)(2,1)} %broadcast_in_dim.14), calls=%async_computation.1 | async-start | bytes 7340032 | tf_op jit(solution)/shard_map/all_to_all | solution.py:14
  81.7 3.2 %copy-start.3 = (f32[512]{0:T(512)S(1)}, f32[512]{0:T(512)}, u32[]{:S(2)}) copy-start(f32[512]{0:T(512)} %param.8) | copy-start | bytes 6148
  81.7 23.3 %copy-start.4 = (f32[512]{0:T(512)S(1)}, f32[512]{0:T(512)}, u32[]{:S(2)}) copy-start(f32[512]{0:T(512)} %param.9) | copy-start | bytes 6148
  96.8 7.5 %all-to-all-start.3 = ((f32[4,4,512]{2,1,0:T(4,128)}), f32[4,4,512]{2,1,0:T(4,128)S(1)}, u32[]{:S(2)}, u32[]{:S(2)}) async-start(f32[4,4,512]{2,1,0:T(4,128)} %broadcast_in_dim.16), calls=%async_computation.3 | async-start | bytes 65536 | tf_op jit(solution)/shard_map/all_to_all | solution.py:14
  108.4 1.2 copy-start.1
  109.7 8.8 %collective-permute-start = (bf16[1792,256]{0,1:T(8,128)(2,1)S(1)}, bf16[1792,256]{0,1:T(8,128)(2,1)}, u32[]{:S(2)}, u32[]{:S(2)}) collective-permute-start(bf16[1792,256]{0,1:T(8,128)(2,1)S(1)} %dynamic-slice_bitcast_fusion), channel_id=1, source_target_pairs={{0,32},{32,0},{64,96},{96,64},{128,160},{160,128},{192,224},{224,1... | collective-permute-start | bytes 2752520 | tf_op jit(solution)/shard_map/ppermute | solution.py:66
  121.5 36.6 %all-to-all-start.6 = ((bf16[8,224,256]{2,1,0:T(8,128)(2,1)}), bf16[8,224,256]{2,1,0:T(8,128)(2,1)S(1)}, u32[]{:S(2)}, u32[]{:S(2)}) async-start(bf16[8,224,256]{2,1,0:T(8,128)(2,1)} %bitcast.72), calls=%async_computation.6 | async-start | bytes 1835008 | tf_op jit(solution)/shard_map/all_to_all | solution.py:14
  158.1 47.6 %all-to-all-start.4 = ((bf16[4,896,512]{1,2,0:T(8,128)(2,1)}), bf16[4,896,512]{1,2,0:T(8,128)(2,1)}, u32[]{:S(2)}, u32[]{:S(2)}) async-start(bf16[4,896,512]{1,2,0:T(8,128)(2,1)} %bitcast.70), calls=%async_computation.4 | async-start | bytes 7340032 | tf_op jit(solution)/shard_map/all_to_all | solution.py:14
  206.7 30.6 %all-to-all-start.7 = ((bf16[8,224,256]{2,1,0:T(8,128)(2,1)}), bf16[8,224,256]{2,1,0:T(8,128)(2,1)}, u32[]{:S(2)}, u32[]{:S(2)}) async-start(bf16[8,224,256]{2,1,0:T(8,128)(2,1)} %broadcast_in_dim.17), calls=%async_computation.7 | async-start | bytes 1835008 | tf_op jit(solution)/shard_map/all_to_all | solution.py:14
  237.3 27.6 %all-to-all-start.5 = ((bf16[8,112,512]{2,1,0:T(8,128)(2,1)}), bf16[8,112,512]{2,1,0:T(8,128)(2,1)S(1)}, u32[]{:S(2)}, u32[]{:S(2)}) async-start(bf16[8,112,512]{2,1,0:T(8,128)(2,1)} %bitcast.71), calls=%async_computation.5 | async-start | bytes 1835008 | tf_op jit(solution)/shard_map/all_to_all | solution.py:14
  240.9 24.9 %collective-permute-start.1 = (bf16[1792,256]{1,0:T(8,128)(2,1)}, bf16[1792,256]{1,0:T(8,128)(2,1)}, u32[]{:S(2)}, u32[]{:S(2)}) collective-permute-start(bf16[1792,256]{1,0:T(8,128)(2,1)} %bitcast.20), channel_id=1, source_target_pairs={{0,32},{32,0},{64,96},{96,64},{128,160},{160,128},{192,224},{224,1... | collective-permute-start | bytes 2752520 | tf_op jit(solution)/shard_map/ppermute | solution.py:75

commit v2 on v1

v2 whole, which is shorter than its diff:
```python
import jax
import jax.numpy as jnp
from jax import lax
from jax.sharding import PartitionSpec as P

NX, NY, NZ, NC = 4, 8, 8, 2
Y_GROUPS = [[x * NY + y for y in range(NY)] for x in range(NX)]
X_GROUPS = [[x * NY + y for x in range(NX)] for y in range(NY)]
Z_GROUPS = [[z * NC + c for z in range(NZ)] for c in range(NC)]
CORE_SWAP = [(z * NC + c, z * NC + 1 - c) for z in range(NZ) for c in range(NC)]
ROWS_B = 64


def exchange(blocks, axis, groups):
    return lax.all_to_all(blocks, axis, 0, 0, tiled=True, axis_index_groups=groups)


def spread(block, axis, groups):
    copies = jnp.broadcast_to(block[None], (len(groups[0]),) + block.shape)
    return exchange(copies, axis, groups)


def merge(parts):
    top = jnp.max(parts[:, 0], axis=0)
    total = jnp.sum(parts[:, 1] * jnp.exp(parts[:, 0] - top[None]), axis=0)
    return jnp.stack([top, total, jnp.sum(parts[:, 2], axis=0), jnp.sum(parts[:, 3], axis=0)])


def add_up(blocks):
    return jnp.sum(blocks.astype(jnp.float32), axis=0).astype(jnp.bfloat16)


def contract(left, right, dims):
    return lax.dot_general(left, right, (dims, ((), ())), preferred_element_type=jnp.float32)


def body(hidden, unembed, teacher, teacher_lse, cotangent):
    tokens, columns = teacher.shape
    features = unembed.shape[0]
    shard = features // (NX * NY)
    rows_a = shard - ROWS_B
    mine = hidden.T

    line = spread(mine[:ROWS_B], "voc", X_GROUPS).reshape(NX * ROWS_B, tokens)
    gathered_b = lax.all_gather(line, "voc", axis_index_groups=Y_GROUPS, axis=0, tiled=True)
    part_a = lax.optimization_barrier((mine[ROWS_B:], line))[0]
    row = spread(part_a, "voc", Y_GROUPS).reshape(NY * rows_a, tokens)
    gathered_a = spread(row, "voc", X_GROUPS).reshape(NX * NY * rows_a, tokens)

    by_shard = unembed.reshape(NX, NY, shard, columns)
    unembed_b = by_shard[:, :, :ROWS_B].transpose(1, 0, 2, 3).reshape(-1, columns)
    unembed_a = by_shard[:, :, ROWS_B:].reshape(-1, columns)

    teacher_t = teacher.T.astype(jnp.float32)
    shifted = teacher_t - teacher_lse[None, :]
    probs = jnp.exp(shifted)
    logits = contract(unembed_b, gathered_b, ((0,), (0,))) + contract(unembed_a, gathered_a, ((0,), (0,)))
    top = jnp.max(logits, axis=0)
    total = jnp.sum(jnp.exp(logits - top[None, :]), axis=0)
    mass = jnp.sum(probs, axis=0)
    cross = jnp.sum(probs * (shifted - logits), axis=0)
    stats = jnp.stack([top, total, mass, cross])
    stats = merge(spread(stats, "voc", Y_GROUPS))
    stats = merge(spread(stats, "voc", X_GROUPS))
    row_mass = stats[2]
    student_lse = stats[0] + jnp.log(stats[1])
    loss = stats[3] + row_mass * student_lse
    grad_logits = (
        cotangent[None, :] * (jnp.exp(logits - student_lse[None, :]) * row_mass[None, :] - probs)
    ).astype(jnp.bfloat16)

    natural = jnp.concatenate(
        [
            gathered_b.reshape(NY, NX, ROWS_B, tokens).transpose(1, 0, 2, 3),
            gathered_a.reshape(NX, NY, rows_a, tokens),
        ],
        axis=2,
    ).reshape(NZ, NC, features // NZ // NC, tokens)
    core = lax.rem(lax.axis_index("tok"), NC)
    rows_kept = lax.dynamic_slice_in_dim(natural, core, 1, 1).reshape(-1, tokens)
    rows_given = lax.dynamic_slice_in_dim(natural, 1 - core, 1, 1).reshape(-1, tokens)
    given = contract(rows_given, grad_logits, ((1,), (1,))).astype(jnp.bfloat16)
    came = lax.ppermute(given, "tok", CORE_SWAP)

    terms_b = jnp.dot(unembed_b, grad_logits, preferred_element_type=jnp.float32).astype(jnp.bfloat16)
    line_b = lax.psum_scatter(
        terms_b, "voc", axis_index_groups=Y_GROUPS, scatter_dimension=0, tiled=True
    )
    chip_terms = (contract(rows_kept, grad_logits, ((1,), (1,))) + came.astype(jnp.float32)).astype(jnp.bfloat16)
    summed = add_up(exchange(chip_terms.reshape(NZ, -1, columns), "tok", Z_GROUPS))
    grad_unembed = lax.all_gather(summed, "tok", axis=0, tiled=True)

    terms_a = jnp.dot(unembed_a, grad_logits, preferred_element_type=jnp.float32).astype(jnp.bfloat16)
    row_a = add_up(exchange(terms_a.reshape(NX, -1, tokens), "voc", X_GROUPS))
    out_a = add_up(exchange(row_a.reshape(NY, -1, tokens), "voc", Y_GROUPS))
    out_b = add_up(exchange(line_b.reshape(NX, -1, tokens), "voc", X_GROUPS))
    grad_hidden = jnp.concatenate([out_b, out_a], axis=0).T
    return (loss, grad_hidden, grad_unembed)


def solution(mesh):
    placed = (P("tok", "voc"), P(None, "voc"), P("tok", "voc"), P("tok"), P("tok"))
    return jax.shard_map(
        body,
        mesh=mesh,
        in_specs=placed,
        out_specs=(P("tok"), P("tok", "voc"), P(None, "voc")),
        check_vma=False,
    )
```

time: 270 us -> 197 us (0.73)
  waiting for transfers between devices: 157 us -> 32.9 us
  blocking collectives: 41.8 us -> 101 us
  starting transfers between devices: 40.5 us -> 20.1 us
  between operations: 0.83 us -> 14 us
  other arithmetic: 9.83 us -> 5.14 us
    all_to_all x6 -> x3, waiting for transfers between devices: 155 us -> 29.3 us  [exchange(): lax.all_to_all(blocks, axis, 0, 0, tiled=True, axis_index_groups=groups)]
    all_to_all x2 -> x6, blocking collectives: 41.8 us -> 101 us  [exchange(): lax.all_to_all(blocks, axis, 0, 0, tiled=True, axis_index_groups=groups)]
    all_to_all x6 -> x3, starting transfers between devices: 31.5 us -> 10.6 us  [exchange(): lax.all_to_all(blocks, axis, 0, 0, tiled=True, axis_index_groups=groups)]
    reduce_sum x4, other arithmetic: 5.68 us -> 1.31 us  [add_up(): return jnp.sum(blocks.astype(jnp.float32), axis=0).astype(jnp.bfloat16)]
    broadcast_in_dim x5, local copies, waits for them, and re-layouts: 4.85 us -> 1.33 us  [spread(): copies = jnp.broadcast_to(block[None], (len(groups[0]),) + block.shape)]
    ppermute x1, starting transfers between devices: 6.62 us -> 9.38 us  [body(): came = lax.ppermute(given, 'tok', CORE_SWAP)]
    dot_general x3 -> x6, matrix products: 7.56 us -> 9.08 us  [the longest x4 6.34 us: contract(): lax.dot_general(left, right, (dims, ((), ())), preferred_element_type=jnp...]
  transfers between devices with their start and end apart: 8 -> 7, of which waited for: 7 -> 5; matrix products, arithmetic and copies ran while one was open for 3% -> 8% of each run, Pallas kernels for 0% -> 0%
where the time goes in v2:
time: 197 us; the launch traced here: 194 us
  blocking collectives  101 us (51%)
  waiting for transfers between devices  32.9 us (17%)
  starting transfers between devices  20.1 us (10%)
  between operations  14 us (7%)
  local copies, waits for them, and re-layouts  11.5 us (6%)
  matrix products  9.08 us (5%)
  other arithmetic  5.14 us (3%)
    all_to_all x6, blocking collectives, exchange(): lax.all_to_all(blocks, axis, 0, 0, tiled=True, axis_index_groups=groups)  101 us
    all_to_all x3, waiting for transfers between devices, exchange(): lax.all_to_all(blocks, axis, 0, 0, tiled=True, axis_index_groups=groups)  29.3 us
    all_to_all x3, starting transfers between devices, exchange(): lax.all_to_all(blocks, axis, 0, 0, tiled=True, axis_index_groups=groups)  10.6 us
    ppermute x1, starting transfers between devices, body(): came = lax.ppermute(given, 'tok', CORE_SWAP)  9.38 us
    dot_general x4, matrix products, contract(): lax.dot_general(left, right, (dims, ((), ())), preferred_element_type=jnp...  6.34 us
  transfers between devices with their start and end apart: 7, of which 5 were waited for; matrix products, arithmetic and copies ran while one was open for 8% of the time, Pallas kernels for 0%

profile of v2, /device:TPU:1, one launch (start us, length us, event | category | flops | bytes accessed | tf_op | source)
XLA Modules:
  0.0 193.9 jit_solution(16017170076207870032)
XLA Ops:
  7.2 0.0 all-gather.3.cloned.1.call-start
  7.2 0.8 slice.51
  8.1 10.3 %all_to_all.45 = bf16[4,64,512]{2,1,0:T(8,128)(2,1)} all-to-all(bf16[4,64,512]{2,1,0:T(8,128)(2,1)S(1)} %broadcast_in_dim.12), channel_id=1, replica_groups={{0,8,16,24},{1,9,17,25},{2,10,18,26},{3,11,19,27},{4,12,20,28},{5,13,21..., dimensions={0} | all-to-all | bytes 524288 | tf_op jit(solution)/shard_map/all_to_all | solution.py:15
  18.4 0.0 all-gather.3.cloned.1.call-update
  18.4 0.8 slice.52
  19.2 18.2 %all_to_all.46 = bf16[8,48,512]{2,1,0:T(8,128)(2,1)S(1)} all-to-all(bf16[8,48,512]{2,1,0:T(8,128)(2,1)S(1)} %broadcast_in_dim.13), channel_id=1, replica_groups={{0,1,2,3,4,5,6,7},{8,9,10,11,12,13,14,15},{16,17,18,19,20,21,22,23},{24..., dimensions={0} | all-to-all | bytes 786432 | tf_op jit(solution)/shard_map/all_to_all | solution.py:15
  37.4 1.3 broadcast_in_dim.15
  38.7 0.0 copy-start.1
  38.7 3.7 %all-to-all-start.2 = ((bf16[4,384,512]{2,1,0:T(8,128)(2,1)}), bf16[4,384,512]{2,1,0:T(8,128)(2,1)S(1)}, u32[]{:S(2)}, u32[]{:S(2)}) async-start(bf16[4,384,512]{2,1,0:T(8,128)(2,1)} %broadcast_in_dim.15), calls=%async_computation.2 | async-start | bytes 3145728 | tf_op jit(solution)/shard_map/all_to_all | solution.py:15
  42.4 0.0 reduce-scatter.2.cloned.1.call-start
  42.5 0.0 copy-done.1
  42.5 0.9 slice.53
  43.4 0.1 slice_bitcast_fusion
  43.5 0.0 copy-start.2
  43.6 0.1 copy.49
  43.7 0.8 copy-done.2
  44.5 0.1 copy.50
  44.7 14.1 %all-to-all-done.2 = bf16[4,384,512]{2,1,0:T(8,128)(2,1)S(1)} async-done(((bf16[4,384,512]{2,1,0:T(8,128)(2,1)}), bf16[4,384,512]{2,1,0:T(8,128)(2,1)S(1)}, u32[]{:S(2)}, u32[]{:S(2)}) %all-to-all-start.2) | async-done | bytes 1572896 | tf_op jit(solution)/shard_map/all_to_all | solution.py:15
  58.7 2.6 %convolution_bitcast_fusion = f32[256,512]{1,0:T(8,128)} fusion(bf16[1536,512]{1,0:T(8,128)(2,1)S(1)} %bitcast.90, bf16[1536,256]{1,0:T(8,128)(2,1)} %bitcast.97), kind=kOutput, calls=%fused_computation.8 | convolution fusion | flops 402653184 | bytes 2883584 | tf_op jit(solution)/shard_map/dot_general | solution.py:34
  61.3 1.4 all-gather.3.cloned.1.call-done
  62.7 0.0 copy-start.3
  62.7 0.0 copy-start.4
  62.7 2.4 %fusion.13 = (f32[512]{0:T(512)S(1)}, f32[256,512]{1,0:T(8,128)S(1)}) fusion(f32[256,512]{1,0:T(8,128)} %convolution_bitcast_fusion, bf16[2048,256]{1,0:T(8,128)(2,1)S(1)} %bitcast.94, bf16[2048,512]{1,0:T(8,128)(2,1)} %all-gather.3.cloned.1.call-done), kind=kOutput, calls=%fused_computation.42 | convolution fusion | flops 537132544 | bytes 4196352 | tf_op jit(solution)/shard_map/dot_general | solution.py:34
  65.1 0.0 copy-done.3
  65.1 0.2 exponential_reduce_fusion
  65.4 11.1 %all_to_all.47 = f32[8,4,512]{2,1,0:T(4,128)S(1)} all-to-all(f32[8,4,512]{2,1,0:T(4,128)S(1)} %broadcast_in_dim.16), channel_id=1, replica_groups={{0,1,2,3,4,5,6,7},{8,9,10,11,12,13,14,15},{16,17,18,19,20,21,22,23},{24..., dimensions={0} | all-to-all | bytes 131072 | tf_op jit(solution)/shard_map/all_to_all | solution.py:15
  76.5 0.1 slice_reduce_fusion.5
  76.7 8.0 %all_to_all.48 = f32[4,4,512]{2,1,0:T(4,128)S(1)} all-to-all(f32[4,4,512]{2,1,0:T(4,128)S(1)} %broadcast_in_dim.17), channel_id=1, replica_groups={{0,8,16,24},{1,9,17,25},{2,10,18,26},{3,11,19,27},{4,12,20,28},{5,13,21..., dimensions={0} | all-to-all | bytes 65536 | tf_op jit(solution)/shard_map/all_to_all | solution.py:15
  84.7 0.1 fusion.12
  84.8 0.6 multiply_add_fusion
  85.4 0.0 copy-done.4
  85.4 0.2 multiply_convert_fusion
  85.5 2.1 %fusion = bf16[2048,512]{0,1:T(8,128)(2,1)} fusion(bf16[256,512]{1,0:T(8,128)(2,1)S(1)} %multiply_convert_fusion, bf16[2048,256]{1,0:T(8,128)(2,1)S(1)} %bitcast.95), kind=kOutput, calls=%fused_computation.3 | convolution fusion | flops 537919488 | bytes 3407872 | tf_op jit(solution)/shard_map/dot_general | solution.py:85
  87.7 0.0 reduce-scatter.2.cloned.1.call-update
  87.7 0.0 all-gather.5.cloned.1.call-start
  87.7 2.0 %pad_maximum_fusion = bf16[4,8,112,512]{3,2,0,1:T(8,128)(2,1)S(1)} fusion(bf16[4,8,64,512]{3,2,0,1:T(8,128)(2,1)} %bitcast.99, bf16[4,8,48,512]{3,2,1,0:T(8,128)(2,1)S(1)} %bitcast.91), kind=kLoop, calls=%fused_computation | loop fusion | flops 7340032 | bytes 7340032 | tf_op jit(solution)/shard_map/concatenate | solution.py:72
  89.7 0.3 copy.62
  90.0 0.3 constant_dynamic-slice_fusion
  90.4 0.7 convolution_convert_fusion.2
  91.1 9.4 %collective-permute-start = (bf16[1792,256]{1,0:T(8,128)(2,1)S(1)}, bf16[1792,256]{1,0:T(8,128)(2,1)S(1)}, u32[]{:S(2)}, u32[]{:S(2)}) collective-permute-start(bf16[1792,256]{1,0:T(8,128)(2,1)S(1)} %convolution_convert_fusion.2), channel_id=1, source_target_pairs={{0,32},{32,0},{64,96},{96,64},{128,160},{160,128},{192,224},{224,1... | collective-permute-start | bytes 2752520 | tf_op jit(solution)/shard_map/ppermute | solution.py:83
  100.4 2.1 %collective-permute-done = bf16[1792,256]{1,0:T(8,128)(2,1)S(1)} collective-permute-done((bf16[1792,256]{1,0:T(8,128)(2,1)S(1)}, bf16[1792,256]{1,0:T(8,128)(2,1)S(1)}, u32[]{:S(2)}, u32[]{:S(2)}) %collective-permute-start) | collective-permute-done | bytes 917536 | tf_op jit(solution)/shard_map/ppermute | solution.py:83
  102.5 0.7 add_convert_fusion
  103.2 0.0 copy-start
  103.2 32.2 %all_to_all.49 = bf16[8,224,256]{2,1,0:T(8,128)(2,1)S(1)} all-to-all(bf16[8,224,256]{2,1,0:T(8,128)(2,1)S(1)} %bitcast.96), channel_id=1, replica_groups={{0,64,128,192,256,320,384,448},{32,96,160,224,288,352,416,480},{1,65,12..., dimensions={0} | all-to-all | bytes 1835008 | tf_op jit(solution)/shard_map/all_to_all | solution.py:15
  135.4 0.8 reduce_sum.141
  136.2 0.0 all-gather.5.cloned.1.call-update
  136.2 0.0 copy-done
  136.2 0.6 convolution_convert_fusion.1
  136.8 0.2 copy.98
  137.0 21.5 %all_to_all.50 = bf16[4,384,512]{1,2,0:T(8,128)(2,1)S(1)} all-to-all(bf16[4,384,512]{1,2,0:T(8,128)(2,1)S(1)} %bitcast.93), channel_id=1, replica_groups={{0,8,16,24},{1,9,17,25},{2,10,18,26},{3,11,19,27},{4,12,20,28},{5,13,21..., dimensions={0} | all-to-all | bytes 3145728 | tf_op jit(solution)/shard_map/all_to_all | solution.py:15
  158.4 0.4 reduce_sum.139
  158.9 0.9 copy.60
  159.8 3.5 %all-to-all-start.7 = ((bf16[8,48,512]{2,1,0:T(8,128)(2,1)}), bf16[8,48,512]{2,1,0:T(8,128)(2,1)S(1)}, u32[]{:S(2)}, u32[]{:S(2)}) async-start(bf16[8,48,512]{2,1,0:T(8,128)(2,1)} %bitcast.23), calls=%async_computation.8 | async-start | bytes 786432 | tf_op jit(solution)/shard_map/all_to_all | solution.py:15
  163.3 0.0 reduce-scatter.2.cloned.1.call-done
  163.3 1.8 copy.57
  165.1 9.8 %all-to-all-done.7 = bf16[8,48,512]{2,1,0:T(8,128)(2,1)S(1)} async-done(((bf16[8,48,512]{2,1,0:T(8,128)(2,1)}), bf16[8,48,512]{2,1,0:T(8,128)(2,1)S(1)}, u32[]{:S(2)}, u32[]{:S(2)}) %all-to-all-start.7) | async-done | bytes 393248 | tf_op jit(solution)/shard_map/all_to_all | solution.py:15
  175.0 3.4 %all-to-all-start.5 = ((bf16[4,64,512]{2,1,0:T(8,128)(2,1)}), bf16[4,64,512]{2,1,0:T(8,128)(2,1)S(1)}, u32[]{:S(2)}, u32[]{:S(2)}) async-start(bf16[4,64,512]{2,1,0:T(8,128)(2,1)} %bitcast.21), calls=%async_computation.6 | async-start | bytes 524288 | tf_op jit(solution)/shard_map/all_to_all | solution.py:15
  178.4 0.1 reduce_sum.140
  178.4 5.4 %all-to-all-done.5 = bf16[4,64,512]{2,1,0:T(8,128)(2,1)S(1)} async-done(((bf16[4,64,512]{2,1,0:T(8,128)(2,1)}), bf16[4,64,512]{2,1,0:T(8,128)(2,1)S(1)}, u32[]{:S(2)}, u32[]{:S(2)}) %all-to-all-start.5) | async-done | bytes 262176 | tf_op jit(solution)/shard_map/all_to_all | solution.py:15
  183.9 0.7 maximum_bitcast_fusion
  184.6 0.0 all-gather.5.cloned.1.call-done
  184.6 2.8 %copy.100 = bf16[3584,256]{1,0:T(8,128)(2,1)} copy(bf16[3584,256]{1,0:T(8,128)(2,1)} %all-gather.5.cloned.1.call-done) | data formatting | bytes 3670016
  (9 shorter events, 0.2 us)
Async XLA Ops:
  7.2 55.5 %all-gather.3.cloned.1.call-start = ((), (), s32[]{:S(2)}) async-start(), calls=%async_computation.10 | async-start | bytes 2359296 | tf_op jit(solution)/shard_map/all_gather | solution.py:45
  38.7 3.8 %copy-start.1 = (bf16[3584,256]{1,0:T(8,128)(2,1)S(1)}, bf16[3584,256]{1,0:T(8,128)(2,1)}, u32[]{:S(2)}) copy-start(bf16[3584,256]{1,0:T(8,128)(2,1)} %param.6) | copy-start | bytes 5505028
  38.7 20.0 %all-to-all-start.2 = ((bf16[4,384,512]{2,1,0:T(8,128)(2,1)}), bf16[4,384,512]{2,1,0:T(8,128)(2,1)S(1)}, u32[]{:S(2)}, u32[]{:S(2)}) async-start(bf16[4,384,512]{2,1,0:T(8,128)(2,1)} %broadcast_in_dim.15), calls=%async_computation.2 | async-start | bytes 3145728 | tf_op jit(solution)/shard_map/all_to_all | solution.py:15
  42.4 120.9 %reduce-scatter.2.cloned.1.call-start = ((), (), s32[]{:S(2)}) async-start(), calls=%async_computation.11 | async-start | bytes 2359296 | tf_op jit(solution)/shard_map/reduce_scatter | solution.py:86
  43.5 1.0 copy-start.2
  62.7 2.4 %copy-start.3 = (f32[512]{0:T(512)S(1)}, f32[512]{0:T(512)}, u32[]{:S(2)}) copy-start(f32[512]{0:T(512)} %param.8) | copy-start | bytes 6148
  62.7 22.7 %copy-start.4 = (f32[512]{0:T(512)S(1)}, f32[512]{0:T(512)}, u32[]{:S(2)}) copy-start(f32[512]{0:T(512)} %param.9) | copy-start | bytes 6148
  87.7 96.9 %all-gather.5.cloned.1.call-start = ((), (), s32[]{:S(2)}) async-start(), calls=%async_computation.12 | async-start | bytes 1949696 | tf_op jit(solution)/shard_map/all_gather | solution.py:91
  91.1 11.5 %collective-permute-start = (bf16[1792,256]{1,0:T(8,128)(2,1)S(1)}, bf16[1792,256]{1,0:T(8,128)(2,1)S(1)}, u32[]{:S(2)}, u32[]{:S(2)}) collective-permute-start(bf16[1792,256]{1,0:T(8,128)(2,1)S(1)} %convolution_convert_fusion.2), channel_id=1, source_target_pairs={{0,32},{32,0},{64,96},{96,64},{128,160},{160,128},{192,224},{224,1... | collective-permute-start | bytes 2752520 | tf_op jit(solution)/shard_map/ppermute | solution.py:83
  103.2 33.0 %copy-start = (bf16[4,8,48,256]{3,2,1,0:T(8,128)(2,1)S(1)}, bf16[4,8,48,256]{3,2,1,0:T(8,128)(2,1)}, u32[]{:S(2)}) copy-start(bf16[4,8,48,256]{3,2,1,0:T(8,128)(2,1)} %slice.53) | copy-start | bytes 2359300
  159.8 15.1 %all-to-all-start.7 = ((bf16[8,48,512]{2,1,0:T(8,128)(2,1)}), bf16[8,48,512]{2,1,0:T(8,128)(2,1)S(1)}, u32[]{:S(2)}, u32[]{:S(2)}) async-start(bf16[8,48,512]{2,1,0:T(8,128)(2,1)} %bitcast.23), calls=%async_computation.8 | async-start | bytes 786432 | tf_op jit(solution)/shard_map/all_to_all | solution.py:15
  175.0 8.9 %all-to-all-start.5 = ((bf16[4,64,512]{2,1,0:T(8,128)(2,1)}), bf16[4,64,512]{2,1,0:T(8,128)(2,1)S(1)}, u32[]{:S(2)}, u32[]{:S(2)}) async-start(bf16[4,64,512]{2,1,0:T(8,128)(2,1)} %bitcast.21), calls=%async_computation.6 | async-start | bytes 524288 | tf_op jit(solution)/shard_map/all_to_all | solution.py:15
Sparse Core Ops, SparseCore 0:
  18.5 44.1 all-gather.2
  87.8 41.8 reduce-scatter.1
  136.3 41.9 all-gather.4

commit v3 on v2

--- a/solution.py
+++ b/solution.py
@@ -8,7 +8,8 @@
 X_GROUPS = [[x * NY + y for x in range(NX)] for y in range(NY)]
 Z_GROUPS = [[z * NC + c for z in range(NZ)] for c in range(NC)]
 CORE_SWAP = [(z * NC + c, z * NC + 1 - c) for z in range(NZ) for c in range(NC)]
-ROWS_B = 64
+X_SHIFTS = [[(x * NY + y, (x + k) % NX * NY + y) for x in range(NX) for y in range(NY)] for k in range(NX)]
+ROWS_B = 48
 
 
 def exchange(blocks, axis, groups):
@@ -41,15 +42,26 @@
     rows_a = shard - ROWS_B
     mine = hidden.T
 
-    line = spread(mine[:ROWS_B], "voc", X_GROUPS).reshape(NX * ROWS_B, tokens)
-    gathered_b = lax.all_gather(line, "voc", axis_index_groups=Y_GROUPS, axis=0, tiled=True)
-    part_a = lax.optimization_barrier((mine[ROWS_B:], line))[0]
-    row = spread(part_a, "voc", Y_GROUPS).reshape(NY * rows_a, tokens)
+    x = lax.axis_index("voc") // NY
+    part_b = mine[:ROWS_B]
+    came_from = [part_b] + [lax.ppermute(part_b, "voc", X_SHIFTS[k]) for k in range(1, NX)]
+    place = lax.broadcasted_iota(jnp.int32, (NX, ROWS_B, tokens), 0)
+    line = jnp.broadcast_to(came_from[-1][None], place.shape)
+    for k in range(NX - 1):
+        line = jnp.where(place == lax.rem(x + NX - k, NX), came_from[k][None], line)
+    gathered_b = lax.all_gather(
+        line.reshape(NX * ROWS_B, tokens), "voc", axis_index_groups=Y_GROUPS, axis=0, tiled=True
+    )
+    row = spread(mine[ROWS_B:], "voc", Y_GROUPS).reshape(NY * rows_a, tokens)
     gathered_a = spread(row, "voc", X_GROUPS).reshape(NX * NY * rows_a, tokens)
 
     by_shard = unembed.reshape(NX, NY, shard, columns)
     unembed_b = by_shard[:, :, :ROWS_B].transpose(1, 0, 2, 3).reshape(-1, columns)
     unembed_a = by_shard[:, :, ROWS_B:].reshape(-1, columns)
+    to_x = [
+        lax.dynamic_slice_in_dim(by_shard[:, :, ROWS_B:], lax.rem(x + k, NX), 1, 0).reshape(-1, columns)
+        for k in range(NX)
+    ]
 
     teacher_t = teacher.T.astype(jnp.float32)
     shifted = teacher_t - teacher_lse[None, :]
@@ -60,15 +72,7 @@
     mass = jnp.sum(probs, axis=0)
     cross = jnp.sum(probs * (shifted - logits), axis=0)
     stats = jnp.stack([top, total, mass, cross])
-    stats = merge(spread(stats, "voc", Y_GROUPS))
-    stats = merge(spread(stats, "voc", X_GROUPS))
-    row_mass = stats[2]
-    student_lse = stats[0] + jnp.log(stats[1])
-    loss = stats[3] + row_mass * student_lse
-    grad_logits = (
-        cotangent[None, :] * (jnp.exp(logits - student_lse[None, :]) * row_mass[None, :] - probs)
-    ).astype(jnp.bfloat16)
-
+    every = lax.all_to_all(jnp.broadcast_to(stats[None], (NX * NY,) + stats.shape), "voc", 0, 0, tiled=True)
     natural = jnp.concatenate(
         [
             gathered_b.reshape(NY, NX, ROWS_B, tokens).transpose(1, 0, 2, 3),
@@ -79,19 +83,31 @@
     core = lax.rem(lax.axis_index("tok"), NC)
     rows_kept = lax.dynamic_slice_in_dim(natural, core, 1, 1).reshape(-1, tokens)
     rows_given = lax.dynamic_slice_in_dim(natural, 1 - core, 1, 1).reshape(-1, tokens)
+    every, rows_kept, rows_given, to_x = lax.optimization_barrier((every, rows_kept, rows_given, to_x))
+    stats = merge(every)
+    row_mass = stats[2]
+    student_lse = stats[0] + jnp.log(stats[1])
+    loss = stats[3] + row_mass * student_lse
+    grad_logits = (
+        cotangent[None, :] * (jnp.exp(logits - student_lse[None, :]) * row_mass[None, :] - probs)
+    ).astype(jnp.bfloat16)
+
     given = contract(rows_given, grad_logits, ((1,), (1,))).astype(jnp.bfloat16)
     came = lax.ppermute(given, "tok", CORE_SWAP)
 
     terms_b = jnp.dot(unembed_b, grad_logits, preferred_element_type=jnp.float32).astype(jnp.bfloat16)
+    chip_terms = (contract(rows_kept, grad_logits, ((1,), (1,))) + came.astype(jnp.float32)).astype(jnp.bfloat16)
+    chip_terms, terms_b, grad_later = lax.optimization_barrier((chip_terms, terms_b, grad_logits))
     line_b = lax.psum_scatter(
         terms_b, "voc", axis_index_groups=Y_GROUPS, scatter_dimension=0, tiled=True
     )
-    chip_terms = (contract(rows_kept, grad_logits, ((1,), (1,))) + came.astype(jnp.float32)).astype(jnp.bfloat16)
     summed = add_up(exchange(chip_terms.reshape(NZ, -1, columns), "tok", Z_GROUPS))
     grad_unembed = lax.all_gather(summed, "tok", axis=0, tiled=True)
-
-    terms_a = jnp.dot(unembed_a, grad_logits, preferred_element_type=jnp.float32).astype(jnp.bfloat16)
-    row_a = add_up(exchange(terms_a.reshape(NX, -1, tokens), "voc", X_GROUPS))
+    row_a = jnp.dot(to_x[0], grad_later, preferred_element_type=jnp.float32)
+    for k in range(1, NX):
+        term = jnp.dot(to_x[k], grad_later, preferred_element_type=jnp.float32).astype(jnp.bfloat16)
+        row_a = row_a + lax.ppermute(term, "voc", X_SHIFTS[k]).astype(jnp.float32)
+    row_a = row_a.astype(jnp.bfloat16)
     out_a = add_up(exchange(row_a.reshape(NY, -1, tokens), "voc", Y_GROUPS))
     out_b = add_up(exchange(line_b.reshape(NX, -1, tokens), "voc", X_GROUPS))
     grad_hidden = jnp.concatenate([out_b, out_a], axis=0).T

time: 197 us -> 215 us (1.091)
  blocking collectives: 101 us -> 74 us
  starting transfers between devices: 20.1 us -> 44.4 us
  waiting for transfers between devices: 32.9 us -> 48.5 us
  local copies, waits for them, and re-layouts: 11.5 us -> 17.3 us
    all_to_all x6 -> x3, blocking collectives: 101 us -> 74 us  [exchange(): lax.all_to_all(blocks, axis, 0, 0, tiled=True, axis_index_groups=groups)]
    all_to_all x3 -> x2, waiting for transfers between devices: 29.3 us -> 6.14 us  [exchange(): lax.all_to_all(blocks, axis, 0, 0, tiled=True, axis_index_groups=groups)]
    ppermute x0 -> x6, waiting for transfers between devices: none -> 22.5 us  [the longest x3 20.3 us: body(): row_a = row_a + lax.ppermute(term, 'voc', X_SHIFTS[k]).astype(jnp.float32)]
    ppermute x0 -> x6, starting transfers between devices: none -> 20 us  [the longest x3 10.8 us: body(): lax.ppermute(part_b, 'voc', X_SHIFTS[k])]
    all_gather x1, waiting for transfers between devices: 1.41 us -> 13.3 us  [body(): lax.all_gather(line.reshape(NX * ROWS_B, tokens), 'voc', axis_index_group...]
    all_to_all x0 -> x1, starting transfers between devices: none -> 6.45 us  [body(): lax.all_to_all(jnp.broadcast_to(stats[None], (NX * NY,) + stats.shape), '...]
    all_to_all x0 -> x1, waiting for transfers between devices: none -> 6.22 us  [body(): lax.all_to_all(jnp.broadcast_to(stats[None], (NX * NY,) + stats.shape), '...]
    unnamed x12 -> x25, local copies, waits for them, and re-layouts: 3.85 us -> 6.77 us
  transfers between devices with their start and end apart: 7 -> 13, of which waited for: 5 -> 9; matrix products, arithmetic and copies ran while one was open for 8% -> 9% of each run, Pallas kernels for 0% -> 0%
where the time goes in v3:
time: 215 us; the launch traced here: 213 us
  blocking collectives  74 us (34%)
  waiting for transfers between devices  48.5 us (23%)
  starting transfers between devices  44.4 us (21%)
  local copies, waits for them, and re-layouts  17.3 us (8%)
  between operations  14.1 us (7%)
  matrix products  9.17 us (4%)
  other arithmetic  5.41 us (3%)
    all_to_all x3, blocking collectives, exchange(): lax.all_to_all(blocks, axis, 0, 0, tiled=True, axis_index_groups=groups)  74 us
    ppermute x3, waiting for transfers between devices, body(): row_a = row_a + lax.ppermute(term, 'voc', X_SHIFTS[k]).astype(jnp.float32)  20.3 us
    all_gather x1, waiting for transfers between devices, body(): lax.all_gather(line.reshape(NX * ROWS_B, tokens), 'voc', axis_index_group...  13.3 us
    ppermute x3, starting transfers between devices, body(): lax.ppermute(part_b, 'voc', X_SHIFTS[k])  10.8 us
    all_to_all x2, starting transfers between devices, exchange(): lax.all_to_all(blocks, axis, 0, 0, tiled=True, axis_index_groups=groups)  10.7 us
    ppermute x3, starting transfers between devices, body(): row_a = row_a + lax.ppermute(term, 'voc', X_SHIFTS[k]).astype(jnp.float32)  9.29 us
    ppermute x1, starting transfers between devices, body(): came = lax.ppermute(given, 'tok', CORE_SWAP)  7.09 us
    unnamed x25, local copies, waits for them, and re-layouts  6.77 us
  transfers between devices with their start and end apart: 13, of which 9 were waited for; matrix products, arithmetic and copies ran while one was open for 9% of the time, Pallas kernels for 0%

profile of v3, /device:TPU:1, one launch (start us, length us, event | category | flops | bytes accessed | tf_op | source)
XLA Modules:
  0.0 212.8 jit_solution(6745365677297458593)
XLA Ops:
  7.2 0.0 all-gather.3.cloned.1.call-start
  7.2 0.8 slice.37
  8.0 5.2 %collective-permute-start.2 = (bf16[48,512]{1,0:T(8,128)(2,1)S(1)}, bf16[48,512]{1,0:T(8,128)(2,1)S(1)}, u32[]{:S(2)}, u32[]{:S(2)}) collective-permute-start(bf16[48,512]{1,0:T(8,128)(2,1)S(1)} %slice.37), channel_id=1, source_target_pairs={{0,24},{1,25},{2,26},{3,27},{4,28},{5,29},{6,30},{7,31},{8,0},{9,1... | collective-permute-start | bytes 147464 | tf_op jit(solution)/shard_map/ppermute | solution.py:47
  13.2 1.9 collective-permute-start.1
  15.2 3.6 %collective-permute-start = (bf16[48,512]{1,0:T(8,128)(2,1)S(1)}, bf16[48,512]{1,0:T(8,128)(2,1)S(1)}, u32[]{:S(2)}, u32[]{:S(2)}) collective-permute-start(bf16[48,512]{1,0:T(8,128)(2,1)S(1)} %slice.37), channel_id=1, source_target_pairs={{0,16},{1,17},{2,18},{3,19},{4,20},{5,21},{6,22},{7,23},{8,24},{9,... | collective-permute-start | bytes 147464 | tf_op jit(solution)/shard_map/ppermute | solution.py:47
  18.9 0.1 iota.27
  18.9 0.1 iota.28
  19.0 0.1 iota.31
  19.1 0.1 iota.32
  19.2 0.1 iota.35
  19.3 0.1 iota.36
  19.4 2.1 %collective-permute-done = bf16[48,512]{1,0:T(8,128)(2,1)S(1)} collective-permute-done((bf16[48,512]{1,0:T(8,128)(2,1)S(1)}, bf16[48,512]{1,0:T(8,128)(2,1)S(1)}, u32[]{:S(2)}, u32[]{:S(2)}) %collective-permute-start) | collective-permute-done | bytes 49184 | tf_op jit(solution)/shard_map/ppermute | solution.py:47
  21.5 0.8 fusion.5
  22.3 0.8 slice.40
  23.2 21.1 %all_to_all.30 = bf16[8,64,512]{2,1,0:T(8,128)(2,1)S(1)} all-to-all(bf16[8,64,512]{2,1,0:T(8,128)(2,1)S(1)} %broadcast_in_dim.67), channel_id=1, replica_groups={{0,1,2,3,4,5,6,7},{8,9,10,11,12,13,14,15},{16,17,18,19,20,21,22,23},{24..., dimensions={0} | all-to-all | bytes 1048576 | tf_op jit(solution)/shard_map/all_to_all | solution.py:16
  44.3 1.5 broadcast_in_dim.69
  45.8 4.0 %all-to-all-start.1 = ((bf16[4,512,512]{2,1,0:T(8,128)(2,1)}), bf16[4,512,512]{2,1,0:T(8,128)(2,1)S(1)}, u32[]{:S(2)}, u32[]{:S(2)}) async-start(bf16[4,512,512]{2,1,0:T(8,128)(2,1)} %broadcast_in_dim.69), calls=%async_computation.1 | async-start | bytes 4194304 | tf_op jit(solution)/shard_map/all_to_all | solution.py:16
  49.8 0.1 copy.30
  49.9 1.3 slice.39
  51.2 1.2 slice_bitcast_fusion
  52.4 0.9 copy.29
  53.4 1.0 constant_dynamic-slice_fusion
  54.4 13.3 %all-gather.3.cloned.1.call-done = bf16[1536,512]{1,0:T(8,128)(2,1)} async-done(((bf16[192,512]{1,0:T(8,128)(2,1)}), bf16[1536,512]{1,0:T(8,128)(2,1)}) %all-gather.3.cloned.1.call-update) | async-done | bytes 1572880 | tf_op jit(solution)/shard_map/all_gather | solution.py:52
  67.7 3.0 %convolution_bitcast_fusion = f32[256,512]{1,0:T(8,128)} fusion(bf16[1536,512]{1,0:T(8,128)(2,1)} %all-gather.3.cloned.1.call-done, bf16[1536,256]{1,0:T(8,128)(2,1)} %bitcast.93), kind=kOutput, calls=%fused_computation.9 | convolution fusion | flops 402653184 | bytes 2883584 | tf_op jit(solution)/shard_map/dot_general | solution.py:35
  70.7 1.0 all-to-all-done.1
  71.7 1.8 fusion.8
  73.5 0.8 copy-done.2
  74.3 0.2 exponential_reduce_fusion
  74.6 0.7 broadcast_in_dim.70
  75.3 6.4 %all-to-all-start.2 = ((f32[32,4,512]{2,1,0:T(4,128)}), f32[32,4,512]{2,1,0:T(4,128)S(1)}, u32[]{:S(2)}, u32[]{:S(2)}) async-start(f32[32,4,512]{2,1,0:T(4,128)} %broadcast_in_dim.70), calls=%async_computation.2 | async-start | bytes 524288 | tf_op jit(solution)/shard_map/all_to_all | solution.py:75
  81.8 0.0 reduce-scatter.4.cloned.1.call-start
  81.8 1.8 pad_maximum_fusion
  83.6 1.6 constant_dynamic-slice_fusion.4
  85.2 6.2 %all-to-all-done.2 = f32[32,4,512]{2,1,0:T(4,128)S(1)} async-done(((f32[32,4,512]{2,1,0:T(4,128)}), f32[32,4,512]{2,1,0:T(4,128)S(1)}, u32[]{:S(2)}, u32[]{:S(2)}) %all-to-all-start.2) | async-done | bytes 262176 | tf_op jit(solution)/shard_map/all_to_all | solution.py:75
  91.4 0.2 slice_reduce_fusion
  91.6 0.1 copy.34
  91.7 0.6 multiply_add_fusion
  92.3 0.2 multiply_convert_fusion
  92.5 0.4 copy-done
  92.9 0.7 convolution_convert_fusion.1
  93.6 7.1 %collective-permute-start.3 = (bf16[1792,256]{1,0:T(8,128)(2,1)S(1)}, bf16[1792,256]{1,0:T(8,128)(2,1)S(1)}, u32[]{:S(2)}, u32[]{:S(2)}) collective-permute-start(bf16[1792,256]{1,0:T(8,128)(2,1)S(1)} %convolution_convert_fusion.1), channel_id=1, source_target_pairs={{0,32},{32,0},{64,96},{96,64},{128,160},{160,128},{192,224},{224,1... | collective-permute-start | bytes 2752520 | tf_op jit(solution)/shard_map/ppermute | solution.py:96
  100.7 1.8 fusion
  102.5 0.3 collective-permute-done.3
  102.8 0.7 add_convert_fusion
  103.4 2.6 %copy.36 = bf16[1536,512]{1,0:T(8,128)(2,1)} copy(bf16[1536,512]{0,1:T(8,128)(2,1)} %fusion) | data formatting | bytes 3145728
  106.1 0.0 all-gather.5.cloned.1.call-start
  106.1 35.1 %all_to_all.31 = bf16[8,224,256]{2,1,0:T(8,128)(2,1)S(1)} all-to-all(bf16[8,224,256]{2,1,0:T(8,128)(2,1)S(1)} %bitcast.92), channel_id=1, replica_groups={{0,64,128,192,256,320,384,448},{32,96,160,224,288,352,416,480},{1,65,12..., dimensions={0} | all-to-all | bytes 1835008 | tf_op jit(solution)/shard_map/all_to_all | solution.py:16
  141.2 0.8 reduce_sum.98
  142.0 0.3 convolution_convert_fusion.2
  142.3 0.3 convolution_convert_fusion.3
  142.6 0.3 convolution_convert_fusion.4
  142.9 2.2 %collective-permute-start.4 = (bf16[512,512]{1,0:T(8,128)(2,1)S(1)}, bf16[512,512]{1,0:T(8,128)(2,1)S(1)}, u32[]{:S(2)}, u32[]{:S(2)}) collective-permute-start(bf16[512,512]{1,0:T(8,128)(2,1)S(1)} %convolution_convert_fusion.4), channel_id=1, source_target_pairs={{0,8},{1,9},{2,10},{3,11},{4,12},{5,13},{6,14},{7,15},{8,16},{9,17... | collective-permute-start | bytes 1572872 | tf_op jit(solution)/shard_map/ppermute | solution.py:109
  145.2 3.9 %collective-permute-start.5 = (bf16[512,512]{1,0:T(8,128)(2,1)S(1)}, bf16[512,512]{1,0:T(8,128)(2,1)S(1)}, u32[]{:S(2)}, u32[]{:S(2)}) collective-permute-start(bf16[512,512]{1,0:T(8,128)(2,1)S(1)} %convolution_convert_fusion.3), channel_id=1, source_target_pairs={{0,16},{1,17},{2,18},{3,19},{4,20},{5,21},{6,22},{7,23},{8,24},{9,... | collective-permute-start | bytes 1572872 | tf_op jit(solution)/shard_map/ppermute | solution.py:109
  149.1 3.1 %collective-permute-start.6 = (bf16[512,512]{1,0:T(8,128)(2,1)S(1)}, bf16[512,512]{1,0:T(8,128)(2,1)S(1)}, u32[]{:S(2)}, u32[]{:S(2)}) collective-permute-start(bf16[512,512]{1,0:T(8,128)(2,1)S(1)} %convolution_convert_fusion.2), channel_id=1, source_target_pairs={{0,24},{1,25},{2,26},{3,27},{4,28},{5,29},{6,30},{7,31},{8,0},{9,1... | collective-permute-start | bytes 1572872 | tf_op jit(solution)/shard_map/ppermute | solution.py:109
  152.2 5.6 %collective-permute-done.4 = bf16[512,512]{1,0:T(8,128)(2,1)S(1)} collective-permute-done((bf16[512,512]{1,0:T(8,128)(2,1)S(1)}, bf16[512,512]{1,0:T(8,128)(2,1)S(1)}, u32[]{:S(2)}, u32[]{:S(2)}) %collective-permute-start.4) | collective-permute-done | bytes 524320 | tf_op jit(solution)/shard_map/ppermute | solution.py:109
  157.8 10.9 %collective-permute-done.5 = bf16[512,512]{1,0:T(8,128)(2,1)S(1)} collective-permute-done((bf16[512,512]{1,0:T(8,128)(2,1)S(1)}, bf16[512,512]{1,0:T(8,128)(2,1)S(1)}, u32[]{:S(2)}, u32[]{:S(2)}) %collective-permute-start.5) | collective-permute-done | bytes 524320 | tf_op jit(solution)/shard_map/ppermute | solution.py:109
  168.7 3.9 %collective-permute-done.6 = bf16[512,512]{1,0:T(8,128)(2,1)S(1)} collective-permute-done((bf16[512,512]{1,0:T(8,128)(2,1)S(1)}, bf16[512,512]{1,0:T(8,128)(2,1)S(1)}, u32[]{:S(2)}, u32[]{:S(2)}) %collective-permute-start.6) | collective-permute-done | bytes 524320 | tf_op jit(solution)/shard_map/ppermute | solution.py:109
  172.6 0.4 add_convert_fusion.1
  173.0 17.9 %all_to_all.32 = bf16[8,64,512]{2,1,0:T(8,128)(2,1)S(1)} all-to-all(bf16[8,64,512]{2,1,0:T(8,128)(2,1)S(1)} %bitcast.95), channel_id=1, replica_groups={{0,1,2,3,4,5,6,7},{8,9,10,11,12,13,14,15},{16,17,18,19,20,21,22,23},{24..., dimensions={0} | all-to-all | bytes 1048576 | tf_op jit(solution)/shard_map/all_to_all | solution.py:16
  190.8 6.7 %all-to-all-start.3 = ((bf16[4,48,512]{2,1,0:T(8,128)(2,1)}), bf16[4,48,512]{2,1,0:T(8,128)(2,1)S(1)}, u32[]{:S(2)}, u32[]{:S(2)}) async-start(bf16[4,48,512]{2,1,0:T(8,128)(2,1)} %bitcast.104), calls=%async_computation.3 | async-start | bytes 393216 | tf_op jit(solution)/shard_map/all_to_all | solution.py:16
  197.5 0.1 reduce_sum.97
  197.6 5.1 %all-to-all-done.3 = bf16[4,48,512]{2,1,0:T(8,128)(2,1)S(1)} async-done(((bf16[4,48,512]{2,1,0:T(8,128)(2,1)}), bf16[4,48,512]{2,1,0:T(8,128)(2,1)S(1)}, u32[]{:S(2)}, u32[]{:S(2)}) %all-to-all-start.3) | async-done | bytes 196640 | tf_op jit(solution)/shard_map/all_to_all | solution.py:16
  202.7 0.7 maximum_bitcast_fusion
  203.4 2.8 %copy.45 = bf16[3584,256]{1,0:T(8,128)(2,1)} copy(bf16[3584,256]{1,0:T(8,128)(2,1)} %all-gather.5.cloned.1.call-done) | data formatting | bytes 3670016
  (35 shorter events, 0.3 us)
Async XLA Ops:
  7.2 60.5 %all-gather.3.cloned.1.call-start = ((), (), s32[]{:S(2)}) async-start(), calls=%async_computation.7 | async-start | bytes 1769472 | tf_op jit(solution)/shard_map/all_gather | solution.py:52
  8.0 11.3 %collective-permute-start.2 = (bf16[48,512]{1,0:T(8,128)(2,1)S(1)}, bf16[48,512]{1,0:T(8,128)(2,1)S(1)}, u32[]{:S(2)}, u32[]{:S(2)}) collective-permute-start(bf16[48,512]{1,0:T(8,128)(2,1)S(1)} %slice.37), channel_id=1, source_target_pairs={{0,24},{1,25},{2,26},{3,27},{4,28},{5,29},{6,30},{7,31},{8,0},{9,1... | collective-permute-start | bytes 147464 | tf_op jit(solution)/shard_map/ppermute | solution.py:47
  13.2 6.1 %collective-permute-start.1 = (bf16[48,512]{1,0:T(8,128)(2,1)S(1)}, bf16[48,512]{1,0:T(8,128)(2,1)S(1)}, u32[]{:S(2)}, u32[]{:S(2)}) collective-permute-start(bf16[48,512]{1,0:T(8,128)(2,1)S(1)} %slice.37), channel_id=1, source_target_pairs={{0,8},{1,9},{2,10},{3,11},{4,12},{5,13},{6,14},{7,15},{8,16},{9,17... | collective-permute-start | bytes 147464 | tf_op jit(solution)/shard_map/ppermute | solution.py:47
  15.2 6.3 %collective-permute-start = (bf16[48,512]{1,0:T(8,128)(2,1)S(1)}, bf16[48,512]{1,0:T(8,128)(2,1)S(1)}, u32[]{:S(2)}, u32[]{:S(2)}) collective-permute-start(bf16[48,512]{1,0:T(8,128)(2,1)S(1)} %slice.37), channel_id=1, source_target_pairs={{0,16},{1,17},{2,18},{3,19},{4,20},{5,21},{6,22},{7,23},{8,24},{9,... | collective-permute-start | bytes 147464 | tf_op jit(solution)/shard_map/ppermute | solution.py:47
  45.8 4.0 %copy-start.8 = (bf16[512,256]{1,0:T(8,128)(2,1)S(1)}, bf16[512,256]{1,0:T(8,128)(2,1)}, u32[]{:S(2)}) copy-start(bf16[512,256]{1,0:T(8,128)(2,1)} %param.7) | copy-start | bytes 786436
  45.8 25.9 %all-to-all-start.1 = ((bf16[4,512,512]{2,1,0:T(8,128)(2,1)}), bf16[4,512,512]{2,1,0:T(8,128)(2,1)S(1)}, u32[]{:S(2)}, u32[]{:S(2)}) async-start(bf16[4,512,512]{2,1,0:T(8,128)(2,1)} %broadcast_in_dim.69), calls=%async_computation.1 | async-start | bytes 4194304 | tf_op jit(solution)/shard_map/all_to_all | solution.py:16
  71.7 2.6 %copy-start.9 = (f32[512]{0:T(512)S(1)}, f32[512]{0:T(512)}, u32[]{:S(2)}) copy-start(f32[512]{0:T(512)} %param.8) | copy-start | bytes 6148
  73.5 0.8 copy-start.2
  75.3 16.1 %all-to-all-start.2 = ((f32[32,4,512]{2,1,0:T(4,128)}), f32[32,4,512]{2,1,0:T(4,128)S(1)}, u32[]{:S(2)}, u32[]{:S(2)}) async-start(f32[32,4,512]{2,1,0:T(4,128)} %broadcast_in_dim.70), calls=%async_computation.2 | async-start | bytes 524288 | tf_op jit(solution)/shard_map/all_to_all | solution.py:75
  81.8 109.1 %reduce-scatter.4.cloned.1.call-start = ((), (), s32[]{:S(2)}) async-start(), calls=%async_computation.9 | async-start | bytes 1769472 | tf_op jit(solution)/shard_map/reduce_scatter | solution.py:101
  83.6 8.8 %copy-start.3 = (f32[256,512]{1,0:T(8,128)S(1)}, f32[256,512]{1,0:T(8,128)}, u32[]{:S(2)}) copy-start(f32[256,512]{1,0:T(8,128)} %copy-done.2) | copy-start | bytes 1572868
  83.6 8.8 %copy-start.10 = (f32[512]{0:T(512)S(1)}, f32[512]{0:T(512)}, u32[]{:S(2)}) copy-start(f32[512]{0:T(512)} %param.9) | copy-start | bytes 6148
  91.4 1.5 copy-start
  92.3 8.3 %copy-start.1 = (bf16[8,4,48,256]{3,2,1,0:T(8,128)(2,1)S(1)}, bf16[8,4,48,256]{3,2,1,0:T(8,128)(2,1)}, u32[]{:S(2)}) copy-start(bf16[8,4,48,256]{3,2,1,0:T(8,128)(2,1)} %copy.29) | copy-start | bytes 2359300
  93.6 9.2 %collective-permute-start.3 = (bf16[1792,256]{1,0:T(8,128)(2,1)S(1)}, bf16[1792,256]{1,0:T(8,128)(2,1)S(1)}, u32[]{:S(2)}, u32[]{:S(2)}) collective-permute-start(bf16[1792,256]{1,0:T(8,128)(2,1)S(1)} %convolution_convert_fusion.1), channel_id=1, source_target_pairs={{0,32},{32,0},{64,96},{96,64},{128,160},{160,128},{192,224},{224,1... | collective-permute-start | bytes 2752520 | tf_op jit(solution)/shard_map/ppermute | solution.py:96
  106.1 36.0 %copy-start.7 = (bf16[1,8,64,256]{3,2,1,0:T(8,128)(2,1)S(1)}, bf16[1,8,64,256]{3,2,1,0:T(8,128)(2,1)}, u32[]{:S(2)}) copy-start(bf16[1,8,64,256]{3,2,1,0:T(8,128)(2,1)} %get-tuple-element.32) | copy-start | bytes 786436
  106.1 97.3 %all-gather.5.cloned.1.call-start = ((), (), s32[]{:S(2)}) async-start(), calls=%async_computation.8 | async-start | bytes 1949696 | tf_op jit(solution)/shard_map/all_gather | solution.py:105
  106.1 36.2 %copy-start.6 = (bf16[1,8,64,256]{3,2,1,0:T(8,128)(2,1)S(1)}, bf16[1,8,64,256]{3,2,1,0:T(8,128)(2,1)}, u32[]{:S(2)}) copy-start(bf16[1,8,64,256]{3,2,1,0:T(8,128)(2,1)} %get-tuple-element.33) | copy-start | bytes 786436
  141.2 1.4 copy-start.5
  142.0 30.6 %copy-start.4 = (bf16[1,8,64,256]{3,2,1,0:T(8,128)(2,1)S(1)}, bf16[1,8,64,256]{3,2,1,0:T(8,128)(2,1)}, u32[]{:S(2)}) copy-start(bf16[1,8,64,256]{3,2,1,0:T(8,128)(2,1)} %get-tuple-element.35) | copy-start | bytes 786436
  142.9 14.9 %collective-permute-start.4 = (bf16[512,512]{1,0:T(8,128)(2,1)S(1)}, bf16[512,512]{1,0:T(8,128)(2,1)S(1)}, u32[]{:S(2)}, u32[]{:S(2)}) collective-permute-start(bf16[512,512]{1,0:T(8,128)(2,1)S(1)} %convolution_convert_fusion.4), channel_id=1, source_target_pairs={{0,8},{1,9},{2,10},{3,11},{4,12},{5,13},{6,14},{7,15},{8,16},{9,17... | collective-permute-start | bytes 1572872 | tf_op jit(solution)/shard_map/ppermute | solution.py:109
  145.2 23.5 %collective-permute-start.5 = (bf16[512,512]{1,0:T(8,128)(2,1)S(1)}, bf16[512,512]{1,0:T(8,128)(2,1)S(1)}, u32[]{:S(2)}, u32[]{:S(2)}) collective-permute-start(bf16[512,512]{1,0:T(8,128)(2,1)S(1)} %convolution_convert_fusion.3), channel_id=1, source_target_pairs={{0,16},{1,17},{2,18},{3,19},{4,20},{5,21},{6,22},{7,23},{8,24},{9,... | collective-permute-start | bytes 1572872 | tf_op jit(solution)/shard_map/ppermute | solution.py:109
  149.1 23.5 %collective-permute-start.6 = (bf16[512,512]{1,0:T(8,128)(2,1)S(1)}, bf16[512,512]{1,0:T(8,128)(2,1)S(1)}, u32[]{:S(2)}, u32[]{:S(2)}) collective-permute-start(bf16[512,512]{1,0:T(8,128)(2,1)S(1)} %convolution_convert_fusion.2), channel_id=1, source_target_pairs={{0,24},{1,25},{2,26},{3,27},{4,28},{5,29},{6,30},{7,31},{8,0},{9,1... | collective-permute-start | bytes 1572872 | tf_op jit(solution)/shard_map/ppermute | solution.py:109
  190.8 11.9 %all-to-all-start.3 = ((bf16[4,48,512]{2,1,0:T(8,128)(2,1)}), bf16[4,48,512]{2,1,0:T(8,128)(2,1)S(1)}, u32[]{:S(2)}, u32[]{:S(2)}) async-start(bf16[4,48,512]{2,1,0:T(8,128)(2,1)} %bitcast.104), calls=%async_computation.3 | async-start | bytes 393216 | tf_op jit(solution)/shard_map/all_to_all | solution.py:16
Sparse Core Ops, SparseCore 0:
  22.5 45.1 all-gather.2
  106.2 38.0 reduce-scatter.3
  147.0 45.9 all-gather.4

commit v4 on v2

--- a/solution.py
+++ b/solution.py
@@ -1,6 +1,7 @@
 import jax
 import jax.numpy as jnp
 from jax import lax
+from jax.experimental import pallas as pl
 from jax.sharding import PartitionSpec as P
 
 NX, NY, NZ, NC = 4, 8, 8, 2
@@ -8,7 +9,8 @@
 X_GROUPS = [[x * NY + y for x in range(NX)] for y in range(NY)]
 Z_GROUPS = [[z * NC + c for z in range(NZ)] for c in range(NC)]
 CORE_SWAP = [(z * NC + c, z * NC + 1 - c) for z in range(NZ) for c in range(NC)]
-ROWS_B = 64
+GATHER_B = 64
+SCATTER_B = 80
 
 
 def exchange(blocks, axis, groups):
@@ -34,22 +36,47 @@
     return lax.dot_general(left, right, (dims, ((), ())), preferred_element_type=jnp.float32)
 
 
+def product_kernel(left, right, out):
+    out[...] = jnp.dot(left[...], right[...], preferred_element_type=jnp.float32).astype(out.dtype)
+
+
+def product(left, right, rows=512):
+    (count, depth), columns = left.shape, right.shape[1]
+    return pl.pallas_call(
+        product_kernel,
+        grid=(count // rows,),
+        in_specs=[
+            pl.BlockSpec((rows, depth), lambda i: (i, 0)),
+            pl.BlockSpec((depth, columns), lambda i: (0, 0)),
+        ],
+        out_specs=pl.BlockSpec((rows, columns), lambda i: (i, 0)),
+        out_shape=jax.ShapeDtypeStruct((count, columns), jnp.bfloat16),
+        cost_estimate=pl.CostEstimate(
+            flops=2 * count * depth * columns,
+            bytes_accessed=2 * (count * depth + depth * columns + count * columns),
+            transcendentals=0,
+        ),
+    )(left, right)
+
+
 def body(hidden, unembed, teacher, teacher_lse, cotangent):
     tokens, columns = teacher.shape
     features = unembed.shape[0]
     shard = features // (NX * NY)
-    rows_a = shard - ROWS_B
+    rows_a = shard - GATHER_B
     mine = hidden.T
 
-    line = spread(mine[:ROWS_B], "voc", X_GROUPS).reshape(NX * ROWS_B, tokens)
+    line = spread(mine[:GATHER_B], "voc", X_GROUPS).reshape(NX * GATHER_B, tokens)
     gathered_b = lax.all_gather(line, "voc", axis_index_groups=Y_GROUPS, axis=0, tiled=True)
-    part_a = lax.optimization_barrier((mine[ROWS_B:], line))[0]
+    part_a = lax.optimization_barrier((mine[GATHER_B:], line))[0]
     row = spread(part_a, "voc", Y_GROUPS).reshape(NY * rows_a, tokens)
     gathered_a = spread(row, "voc", X_GROUPS).reshape(NX * NY * rows_a, tokens)
 
     by_shard = unembed.reshape(NX, NY, shard, columns)
-    unembed_b = by_shard[:, :, :ROWS_B].transpose(1, 0, 2, 3).reshape(-1, columns)
-    unembed_a = by_shard[:, :, ROWS_B:].reshape(-1, columns)
+    unembed_b = by_shard[:, :, :GATHER_B].transpose(1, 0, 2, 3).reshape(-1, columns)
+    unembed_a = by_shard[:, :, GATHER_B:].reshape(-1, columns)
+    scatter_b = by_shard[:, :, :SCATTER_B].transpose(1, 0, 2, 3).reshape(-1, columns)
+    scatter_a = by_shard[:, :, SCATTER_B:].reshape(-1, columns)
 
     teacher_t = teacher.T.astype(jnp.float32)
     shifted = teacher_t - teacher_lse[None, :]
@@ -60,8 +87,21 @@
     mass = jnp.sum(probs, axis=0)
     cross = jnp.sum(probs * (shifted - logits), axis=0)
     stats = jnp.stack([top, total, mass, cross])
-    stats = merge(spread(stats, "voc", Y_GROUPS))
-    stats = merge(spread(stats, "voc", X_GROUPS))
+    every = lax.all_to_all(jnp.broadcast_to(stats[None], (NX * NY,) + stats.shape), "voc", 0, 0, tiled=True)
+    natural = jnp.concatenate(
+        [
+            gathered_b.reshape(NY, NX, GATHER_B, tokens).transpose(1, 0, 2, 3),
+            gathered_a.reshape(NX, NY, rows_a, tokens),
+        ],
+        axis=2,
+    ).reshape(NZ, NC, features // NZ // NC, tokens)
+    core = lax.rem(lax.axis_index("tok"), NC)
+    rows_kept = lax.dynamic_slice_in_dim(natural, core, 1, 1).reshape(-1, tokens)
+    rows_given = lax.dynamic_slice_in_dim(natural, 1 - core, 1, 1).reshape(-1, tokens)
+    every, rows_kept, rows_given, scatter_a, scatter_b = lax.optimization_barrier(
+        (every, rows_kept, rows_given, scatter_a, scatter_b)
+    )
+    stats = merge(every)
     row_mass = stats[2]
     student_lse = stats[0] + jnp.log(stats[1])
     loss = stats[3] + row_mass * student_lse
@@ -69,20 +109,10 @@
         cotangent[None, :] * (jnp.exp(logits - student_lse[None, :]) * row_mass[None, :] - probs)
     ).astype(jnp.bfloat16)
 
-    natural = jnp.concatenate(
-        [
-            gathered_b.reshape(NY, NX, ROWS_B, tokens).transpose(1, 0, 2, 3),
-            gathered_a.reshape(NX, NY, rows_a, tokens),
-        ],
-        axis=2,
-    ).reshape(NZ, NC, features // NZ // NC, tokens)
-    core = lax.rem(lax.axis_index("tok"), NC)
-    rows_kept = lax.dynamic_slice_in_dim(natural, core, 1, 1).reshape(-1, tokens)
-    rows_given = lax.dynamic_slice_in_dim(natural, 1 - core, 1, 1).reshape(-1, tokens)
     given = contract(rows_given, grad_logits, ((1,), (1,))).astype(jnp.bfloat16)
     came = lax.ppermute(given, "tok", CORE_SWAP)
 
-    terms_b = jnp.dot(unembed_b, grad_logits, preferred_element_type=jnp.float32).astype(jnp.bfloat16)
+    terms_b = product(scatter_b, grad_logits)
     line_b = lax.psum_scatter(
         terms_b, "voc", axis_index_groups=Y_GROUPS, scatter_dimension=0, tiled=True
     )
@@ -90,7 +120,7 @@
     summed = add_up(exchange(chip_terms.reshape(NZ, -1, columns), "tok", Z_GROUPS))
     grad_unembed = lax.all_gather(summed, "tok", axis=0, tiled=True)
 
-    terms_a = jnp.dot(unembed_a, grad_logits, preferred_element_type=jnp.float32).astype(jnp.bfloat16)
+    terms_a = product(scatter_a, grad_logits)
     row_a = add_up(exchange(terms_a.reshape(NX, -1, tokens), "voc", X_GROUPS))
     out_a = add_up(exchange(row_a.reshape(NY, -1, tokens), "voc", Y_GROUPS))
     out_b = add_up(exchange(line_b.reshape(NX, -1, tokens), "voc", X_GROUPS))

time: 197 us -> 194 us (0.985)
  blocking collectives: 101 us -> 89.8 us
  Pallas kernels: 0 us -> 7.48 us
  local copies, waits for them, and re-layouts: 11.5 us -> 15.4 us
  matrix products: 9.08 us -> 6.13 us
  starting transfers between devices: 20.1 us -> 22.1 us
    all_to_all x3 -> x2, waiting for transfers between devices: 29.3 us -> 15.9 us  [exchange(): lax.all_to_all(blocks, axis, 0, 0, tiled=True, axis_index_groups=groups)]
    all_to_all x6 -> x5, blocking collectives: 101 us -> 89.8 us  [exchange(): lax.all_to_all(blocks, axis, 0, 0, tiled=True, axis_index_groups=groups)]
    pallas_call x0 -> x2, Pallas kernels: none -> 7.48 us  [product(): pl.pallas_call(product_kernel, grid=(count // rows,), in_specs=[pl.BlockS...]
    all_to_all x0 -> x1, starting transfers between devices: none -> 6.84 us  [body(): lax.all_to_all(jnp.broadcast_to(stats[None], (NX * NY,) + stats.shape), '...]
    all_to_all x0 -> x1, waiting for transfers between devices: none -> 5.95 us  [body(): lax.all_to_all(jnp.broadcast_to(stats[None], (NX * NY,) + stats.shape), '...]
    all_gather x1, waiting for transfers between devices: 0.01 us -> 5.06 us  [body(): grad_unembed = lax.all_gather(summed, 'tok', axis=0, tiled=True)]
    all_to_all x3 -> x2, starting transfers between devices: 10.6 us -> 7.15 us  [exchange(): lax.all_to_all(blocks, axis, 0, 0, tiled=True, axis_index_groups=groups)]
    dot_general x2 -> x0, matrix products: 2.74 us -> none  [the longest x1 2.12 us: body(): jnp.dot(unembed_b, grad_logits, preferred_element_type=jnp.float32)]
  transfers between devices with their start and end apart: 7 -> 7, of which waited for: 5 -> 6; matrix products, arithmetic and copies ran while one was open for 8% -> 9% of each run, Pallas kernels for 0% -> 1%
where the time goes in v4:
time: 194 us; the launch traced here: 193 us
  blocking collectives  89.8 us (46%)
  waiting for transfers between devices  32.4 us (17%)
  starting transfers between devices  22.1 us (11%)
  local copies, waits for them, and re-layouts  15.4 us (8%)
  between operations  13.9 us (7%)
  Pallas kernels  7.48 us (4%)
  matrix products  6.13 us (3%)
  other arithmetic  5.58 us (3%)
    all_to_all x5, blocking collectives, exchange(): lax.all_to_all(blocks, axis, 0, 0, tiled=True, axis_index_groups=groups)  89.8 us
    all_to_all x2, waiting for transfers between devices, exchange(): lax.all_to_all(blocks, axis, 0, 0, tiled=True, axis_index_groups=groups)  15.9 us
    ppermute x1, starting transfers between devices, body(): came = lax.ppermute(given, 'tok', CORE_SWAP)  7.95 us
    pallas_call x2, Pallas kernels, product(): pl.pallas_call(product_kernel, grid=(count // rows,), in_specs=[pl.BlockS...  7.48 us
    all_to_all x2, starting transfers between devices, exchange(): lax.all_to_all(blocks, axis, 0, 0, tiled=True, axis_index_groups=groups)  7.15 us
    all_to_all x1, starting transfers between devices, body(): lax.all_to_all(jnp.broadcast_to(stats[None], (NX * NY,) + stats.shape), '...  6.84 us
    dot_general x4, matrix products, contract(): lax.dot_general(left, right, (dims, ((), ())), preferred_element_type=jnp...  6.13 us
    all_to_all x1, waiting for transfers between devices, body(): lax.all_to_all(jnp.broadcast_to(stats[None], (NX * NY,) + stats.shape), '...  5.95 us
  transfers between devices with their start and end apart: 7, of which 6 were waited for; matrix products, arithmetic and copies ran while one was open for 9% of the time, Pallas kernels for 1%

profile of v4, /device:TPU:1, one launch (start us, length us, event | category | flops | bytes accessed | tf_op | source)
XLA Modules:
  0.0 192.8 jit_solution(1802906924752756865)
XLA Ops:
  7.2 0.0 all-gather.3.cloned.1.call-start
  7.2 0.8 slice.42
  8.1 10.3 %all_to_all.40 = bf16[4,64,512]{2,1,0:T(8,128)(2,1)} all-to-all(bf16[4,64,512]{2,1,0:T(8,128)(2,1)S(1)} %broadcast_in_dim.10), channel_id=1, replica_groups={{0,8,16,24},{1,9,17,25},{2,10,18,26},{3,11,19,27},{4,12,20,28},{5,13,21..., dimensions={0} | all-to-all | bytes 524288 | tf_op jit(solution)/shard_map/all_to_all | solution.py:17
  18.4 0.0 all-gather.3.cloned.1.call-update
  18.4 0.8 slice.43
  19.2 18.2 %all_to_all.41 = bf16[8,48,512]{2,1,0:T(8,128)(2,1)S(1)} all-to-all(bf16[8,48,512]{2,1,0:T(8,128)(2,1)S(1)} %broadcast_in_dim.11), channel_id=1, replica_groups={{0,1,2,3,4,5,6,7},{8,9,10,11,12,13,14,15},{16,17,18,19,20,21,22,23},{24..., dimensions={0} | all-to-all | bytes 786432 | tf_op jit(solution)/shard_map/all_to_all | solution.py:17
  37.4 1.3 broadcast_in_dim.13
  38.7 0.0 copy-start
  38.7 3.7 %all-to-all-start.2 = ((bf16[4,384,512]{2,1,0:T(8,128)(2,1)}), bf16[4,384,512]{2,1,0:T(8,128)(2,1)S(1)}, u32[]{:S(2)}, u32[]{:S(2)}) async-start(bf16[4,384,512]{2,1,0:T(8,128)(2,1)} %broadcast_in_dim.13), calls=%async_computation.2 | async-start | bytes 3145728 | tf_op jit(solution)/shard_map/all_to_all | solution.py:17
  42.4 0.0 copy-done
  42.4 1.0 slice.44
  43.4 0.9 slice.45
  44.3 0.1 slice_bitcast_fusion.1
  44.4 1.1 copy.25
  45.5 1.8 copy.26
  47.3 0.1 slice_bitcast_fusion
  47.4 0.0 copy-start.3
  47.4 1.2 copy.29
  48.6 10.1 %all-to-all-done.2 = bf16[4,384,512]{2,1,0:T(8,128)(2,1)S(1)} async-done(((bf16[4,384,512]{2,1,0:T(8,128)(2,1)}), bf16[4,384,512]{2,1,0:T(8,128)(2,1)S(1)}, u32[]{:S(2)}, u32[]{:S(2)}) %all-to-all-start.2) | async-done | bytes 1572896 | tf_op jit(solution)/shard_map/all_to_all | solution.py:17
  58.7 0.0 copy-done.3
  58.7 0.6 convolution_bitcast_fusion
  59.3 3.3 %all-gather.3.cloned.1.call-done = bf16[2048,512]{1,0:T(8,128)(2,1)} async-done(((bf16[256,512]{1,0:T(8,128)(2,1)}), bf16[2048,512]{1,0:T(8,128)(2,1)}) %all-gather.3.cloned.1.call-update) | async-done | bytes 2097168 | tf_op jit(solution)/shard_map/all_gather | solution.py:70
  62.7 0.0 copy-start.2
  62.7 0.0 copy-start.4
  62.7 2.7 %fusion.5 = (f32[512]{0:T(512)S(1)}, f32[256,512]{1,0:T(8,128)S(1)}) fusion(f32[256,512]{1,0:T(8,128)S(1)} %convolution_bitcast_fusion, bf16[2048,256]{1,0:T(8,128)(2,1)} %bitcast.79, bf16[2048,512]{1,0:T(8,128)(2,1)} %all-gather.3.cloned.1.call-done), kind=kOutput, calls=%fused_computation.28 | convolution fusion | flops 537132544 | bytes 4196352 | tf_op jit(solution)/shard_map/dot_general | solution.py:36
  65.4 0.0 copy-done.2
  65.4 0.0 copy-done.4
  65.4 0.2 exponential_reduce_fusion
  65.6 0.8 broadcast_in_dim.14
  66.4 6.8 %all-to-all-start.3 = ((f32[32,4,512]{2,1,0:T(4,128)}), f32[32,4,512]{2,1,0:T(4,128)S(1)}, u32[]{:S(2)}, u32[]{:S(2)}) async-start(f32[32,4,512]{2,1,0:T(4,128)} %broadcast_in_dim.14), calls=%async_computation.3 | async-start | bytes 524288 | tf_op jit(solution)/shard_map/all_to_all | solution.py:90
  73.3 0.0 reduce-scatter.2.cloned.1.call-start
  73.3 1.8 pad_maximum_fusion
  75.1 0.3 copy.28
  75.5 0.0 copy-start.5
  75.5 1.5 constant_dynamic-slice_fusion
  77.0 6.0 %all-to-all-done.3 = f32[32,4,512]{2,1,0:T(4,128)S(1)} async-done(((f32[32,4,512]{2,1,0:T(4,128)}), f32[32,4,512]{2,1,0:T(4,128)S(1)}, u32[]{:S(2)}, u32[]{:S(2)}) %all-to-all-start.3) | async-done | bytes 262176 | tf_op jit(solution)/shard_map/all_to_all | solution.py:90
  82.9 0.2 slice_reduce_fusion
  83.1 0.1 copy.32
  83.3 0.6 multiply_add_fusion
  83.8 0.0 copy-done.5
  83.9 0.9 multiply_convert_fusion.right
  84.7 5.0 %shard_map.76 = bf16[2560,512]{1,0:T(8,128)(2,1)} custom-call(bf16[2560,256]{1,0:T(8,128)(2,1)} %bitcast.72, bf16[256,512]{1,0:T(8,128)(2,1)} %multiply_convert_fusion.right), custom_call_target="tpu_custom_call" | custom-call | flops 671088640 | bytes 4194304 | tf_op jit(solution)/shard_map/pallas_call | solution.py:45
  89.8 0.0 copy-start.1
  89.8 0.0 reduce-scatter.2.cloned.1.call-update
  89.8 0.0 all-gather.5.cloned.1.call-start
  89.8 0.9 copy-done.1
  90.7 2.2 %convolution_convert_fusion = bf16[1792,256]{1,0:T(8,128)(2,1)S(1)} fusion(bf16[1792,512]{1,0:T(8,128)(2,1)} %bitcast.69, bf16[256,512]{1,0:T(8,128)(2,1)S(1)} %copy-done.1), kind=kOutput, calls=%fused_computation.1 | convolution fusion | flops 470220800 | bytes 3014656 | tf_op jit(solution)/shard_map/dot_general | solution.py:36
  92.9 7.9 %collective-permute-start = (bf16[1792,256]{1,0:T(8,128)(2,1)S(1)}, bf16[1792,256]{1,0:T(8,128)(2,1)S(1)}, u32[]{:S(2)}, u32[]{:S(2)}) collective-permute-start(bf16[1792,256]{1,0:T(8,128)(2,1)S(1)} %convolution_convert_fusion), channel_id=1, source_target_pairs={{0,32},{32,0},{64,96},{96,64},{128,160},{160,128},{192,224},{224,1... | collective-permute-start | bytes 2752520 | tf_op jit(solution)/shard_map/ppermute | solution.py:113
  100.8 2.1 %collective-permute-done = bf16[1792,256]{1,0:T(8,128)(2,1)S(1)} collective-permute-done((bf16[1792,256]{1,0:T(8,128)(2,1)S(1)}, bf16[1792,256]{1,0:T(8,128)(2,1)S(1)}, u32[]{:S(2)}, u32[]{:S(2)}) %collective-permute-start) | collective-permute-done | bytes 917536 | tf_op jit(solution)/shard_map/ppermute | solution.py:113
  102.9 0.7 add_convert_fusion
  103.6 32.0 %all_to_all.42 = bf16[8,224,256]{2,1,0:T(8,128)(2,1)S(1)} all-to-all(bf16[8,224,256]{2,1,0:T(8,128)(2,1)S(1)} %bitcast.74), channel_id=1, replica_groups={{0,64,128,192,256,320,384,448},{32,96,160,224,288,352,416,480},{1,65,12..., dimensions={0} | all-to-all | bytes 1835008 | tf_op jit(solution)/shard_map/all_to_all | solution.py:17
  135.6 0.8 reduce_sum.111
  136.4 0.0 all-gather.5.cloned.1.call-update
  136.5 2.4 %shard_map.77 = bf16[1024,512]{1,0:T(8,128)(2,1)} custom-call(bf16[1024,256]{1,0:T(8,128)(2,1)} %bitcast.76, bf16[256,512]{1,0:T(8,128)(2,1)} %multiply_convert_fusion.right), custom_call_target="tpu_custom_call" | custom-call | flops 268435456 | bytes 1835008 | tf_op jit(solution)/shard_map/pallas_call | solution.py:45
  138.9 16.9 %all_to_all.43 = bf16[4,256,512]{2,1,0:T(8,128)(2,1)S(1)} all-to-all(bf16[4,256,512]{2,1,0:T(8,128)(2,1)} %bitcast.73), channel_id=1, replica_groups={{0,8,16,24},{1,9,17,25},{2,10,18,26},{3,11,19,27},{4,12,20,28},{5,13,21..., dimensions={0} | all-to-all | bytes 2097152 | tf_op jit(solution)/shard_map/all_to_all | solution.py:17
  155.8 0.2 reduce_sum.109
  156.0 12.3 %all_to_all.44 = bf16[8,32,512]{2,1,0:T(8,128)(2,1)S(1)} all-to-all(bf16[8,32,512]{2,1,0:T(8,128)(2,1)S(1)} %bitcast.78), channel_id=1, replica_groups={{0,1,2,3,4,5,6,7},{8,9,10,11,12,13,14,15},{16,17,18,19,20,21,22,23},{24..., dimensions={0} | all-to-all | bytes 524288 | tf_op jit(solution)/shard_map/all_to_all | solution.py:17
  168.4 0.0 reduce-scatter.2.cloned.1.call-done
  168.4 3.5 %all-to-all-start.4 = ((bf16[4,80,512]{2,1,0:T(8,128)(2,1)}), bf16[4,80,512]{2,1,0:T(8,128)(2,1)S(1)}, u32[]{:S(2)}, u32[]{:S(2)}) async-start(bf16[4,80,512]{2,1,0:T(8,128)(2,1)} %bitcast.82), calls=%async_computation.5 | async-start | bytes 655360 | tf_op jit(solution)/shard_map/all_to_all | solution.py:17
  171.9 5.8 %all-to-all-done.4 = bf16[4,80,512]{2,1,0:T(8,128)(2,1)S(1)} async-done(((bf16[4,80,512]{2,1,0:T(8,128)(2,1)}), bf16[4,80,512]{2,1,0:T(8,128)(2,1)S(1)}, u32[]{:S(2)}, u32[]{:S(2)}) %all-to-all-start.4) | async-done | bytes 327712 | tf_op jit(solution)/shard_map/all_to_all | solution.py:17
  177.7 0.7 maximum_bitcast_fusion
  178.4 5.1 %all-gather.5.cloned.1.call-done = bf16[3584,256]{1,0:T(8,128)(2,1)} async-done(((bf16[224,256]{1,0:T(8,128)(2,1)}), bf16[3584,256]{1,0:T(8,128)(2,1)}) %all-gather.5.cloned.1.call-update) | async-done | bytes 1835024 | tf_op jit(solution)/shard_map/all_gather | solution.py:121
  183.4 2.8 %copy.40 = bf16[3584,256]{1,0:T(8,128)(2,1)} copy(bf16[3584,256]{1,0:T(8,128)(2,1)} %all-gather.5.cloned.1.call-done) | data formatting | bytes 3670016
  (7 shorter events, 0.2 us)
Async XLA Ops:
  7.2 55.5 %all-gather.3.cloned.1.call-start = ((), (), s32[]{:S(2)}) async-start(), calls=%async_computation.9 | async-start | bytes 2359296 | tf_op jit(solution)/shard_map/all_gather | solution.py:70
  38.7 3.7 %copy-start = (bf16[3584,256]{1,0:T(8,128)(2,1)S(1)}, bf16[3584,256]{1,0:T(8,128)(2,1)}, u32[]{:S(2)}) copy-start(bf16[3584,256]{1,0:T(8,128)(2,1)} %param.6) | copy-start | bytes 5505028
  38.7 20.0 %all-to-all-start.2 = ((bf16[4,384,512]{2,1,0:T(8,128)(2,1)}), bf16[4,384,512]{2,1,0:T(8,128)(2,1)S(1)}, u32[]{:S(2)}, u32[]{:S(2)}) async-start(bf16[4,384,512]{2,1,0:T(8,128)(2,1)} %broadcast_in_dim.13), calls=%async_computation.2 | async-start | bytes 3145728 | tf_op jit(solution)/shard_map/all_to_all | solution.py:17
  47.4 11.3 %copy-start.3 = (bf16[4,8,48,256]{3,2,1,0:T(8,128)(2,1)S(1)}, bf16[4,8,48,256]{3,2,1,0:T(8,128)(2,1)}, u32[]{:S(2)}) copy-start(bf16[4,8,48,256]{3,2,1,0:T(8,128)(2,1)} %slice.44) | copy-start | bytes 2359300
  62.7 2.7 %copy-start.2 = (bf16[512,256]{0,1:T(8,128)(2,1)S(1)}, bf16[512,256]{0,1:T(8,128)(2,1)}, u32[]{:S(2)}) copy-start(bf16[512,256]{0,1:T(8,128)(2,1)} %copy.26) | copy-start | bytes 786436
  62.7 2.7 %copy-start.4 = (f32[512]{0:T(512)S(1)}, f32[512]{0:T(512)}, u32[]{:S(2)}) copy-start(f32[512]{0:T(512)} %param.8) | copy-start | bytes 6148
  66.4 16.5 %all-to-all-start.3 = ((f32[32,4,512]{2,1,0:T(4,128)}), f32[32,4,512]{2,1,0:T(4,128)S(1)}, u32[]{:S(2)}, u32[]{:S(2)}) async-start(f32[32,4,512]{2,1,0:T(4,128)} %broadcast_in_dim.14), calls=%async_computation.3 | async-start | bytes 524288 | tf_op jit(solution)/shard_map/all_to_all | solution.py:90
  73.3 95.1 %reduce-scatter.2.cloned.1.call-start = ((), (), s32[]{:S(2)}) async-start(), calls=%async_computation.10 | async-start | bytes 2949120 | tf_op jit(solution)/shard_map/reduce_scatter | solution.py:116
  75.5 8.4 %copy-start.5 = (f32[512]{0:T(512)S(1)}, f32[512]{0:T(512)}, u32[]{:S(2)}) copy-start(f32[512]{0:T(512)} %param.9) | copy-start | bytes 6148
  89.8 0.9 copy-start.1
  89.8 93.6 %all-gather.5.cloned.1.call-start = ((), (), s32[]{:S(2)}) async-start(), calls=%async_computation.11 | async-start | bytes 1949696 | tf_op jit(solution)/shard_map/all_gather | solution.py:121
  92.9 10.0 %collective-permute-start = (bf16[1792,256]{1,0:T(8,128)(2,1)S(1)}, bf16[1792,256]{1,0:T(8,128)(2,1)S(1)}, u32[]{:S(2)}, u32[]{:S(2)}) collective-permute-start(bf16[1792,256]{1,0:T(8,128)(2,1)S(1)} %convolution_convert_fusion), channel_id=1, source_target_pairs={{0,32},{32,0},{64,96},{96,64},{128,160},{160,128},{192,224},{224,1... | collective-permute-start | bytes 2752520 | tf_op jit(solution)/shard_map/ppermute | solution.py:113
  168.4 9.3 %all-to-all-start.4 = ((bf16[4,80,512]{2,1,0:T(8,128)(2,1)}), bf16[4,80,512]{2,1,0:T(8,128)(2,1)S(1)}, u32[]{:S(2)}, u32[]{:S(2)}) async-start(bf16[4,80,512]{2,1,0:T(8,128)(2,1)} %bitcast.82), calls=%async_computation.5 | async-start | bytes 655360 | tf_op jit(solution)/shard_map/all_to_all | solution.py:17
Sparse Core Ops, SparseCore 0:
  18.5 44.1 all-gather.2
  89.9 44.4 reduce-scatter.1
  136.6 46.8 all-gather.4

commit v5 on v4

--- a/solution.py
+++ b/solution.py
@@ -10,7 +10,6 @@
 Z_GROUPS = [[z * NC + c for z in range(NZ)] for c in range(NC)]
 CORE_SWAP = [(z * NC + c, z * NC + 1 - c) for z in range(NZ) for c in range(NC)]
 GATHER_B = 64
-SCATTER_B = 80
 
 
 def exchange(blocks, axis, groups):
@@ -40,7 +39,7 @@
     out[...] = jnp.dot(left[...], right[...], preferred_element_type=jnp.float32).astype(out.dtype)
 
 
-def product(left, right, rows=512):
+def product(left, right, rows=896):
     (count, depth), columns = left.shape, right.shape[1]
     return pl.pallas_call(
         product_kernel,
@@ -75,8 +74,7 @@
     by_shard = unembed.reshape(NX, NY, shard, columns)
     unembed_b = by_shard[:, :, :GATHER_B].transpose(1, 0, 2, 3).reshape(-1, columns)
     unembed_a = by_shard[:, :, GATHER_B:].reshape(-1, columns)
-    scatter_b = by_shard[:, :, :SCATTER_B].transpose(1, 0, 2, 3).reshape(-1, columns)
-    scatter_a = by_shard[:, :, SCATTER_B:].reshape(-1, columns)
+    by_y = by_shard.transpose(1, 0, 2, 3).reshape(features, columns)
 
     teacher_t = teacher.T.astype(jnp.float32)
     shifted = teacher_t - teacher_lse[None, :]
@@ -98,9 +96,7 @@
     core = lax.rem(lax.axis_index("tok"), NC)
     rows_kept = lax.dynamic_slice_in_dim(natural, core, 1, 1).reshape(-1, tokens)
     rows_given = lax.dynamic_slice_in_dim(natural, 1 - core, 1, 1).reshape(-1, tokens)
-    every, rows_kept, rows_given, scatter_a, scatter_b = lax.optimization_barrier(
-        (every, rows_kept, rows_given, scatter_a, scatter_b)
-    )
+    every, rows_kept, rows_given, by_y = lax.optimization_barrier((every, rows_kept, rows_given, by_y))
     stats = merge(every)
     row_mass = stats[2]
     student_lse = stats[0] + jnp.log(stats[1])
@@ -112,19 +108,19 @@
     given = contract(rows_given, grad_logits, ((1,), (1,))).astype(jnp.bfloat16)
     came = lax.ppermute(given, "tok", CORE_SWAP)
 
-    terms_b = product(scatter_b, grad_logits)
-    line_b = lax.psum_scatter(
-        terms_b, "voc", axis_index_groups=Y_GROUPS, scatter_dimension=0, tiled=True
+    grad_later = lax.optimization_barrier((grad_logits, given))[0]
+    line = lax.psum_scatter(
+        product(by_y, grad_later), "voc", axis_index_groups=Y_GROUPS, scatter_dimension=0, tiled=True
     )
     chip_terms = (contract(rows_kept, grad_logits, ((1,), (1,))) + came.astype(jnp.float32)).astype(jnp.bfloat16)
     summed = add_up(exchange(chip_terms.reshape(NZ, -1, columns), "tok", Z_GROUPS))
-    grad_unembed = lax.all_gather(summed, "tok", axis=0, tiled=True)
-
-    terms_a = product(scatter_a, grad_logits)
-    row_a = add_up(exchange(terms_a.reshape(NX, -1, tokens), "voc", X_GROUPS))
-    out_a = add_up(exchange(row_a.reshape(NY, -1, tokens), "voc", Y_GROUPS))
-    out_b = add_up(exchange(line_b.reshape(NX, -1, tokens), "voc", X_GROUPS))
-    grad_hidden = jnp.concatenate([out_b, out_a], axis=0).T
+    own = spread(summed, "tok", Z_GROUPS)
+    other = lax.ppermute(own, "tok", CORE_SWAP)
+    line = lax.optimization_barrier((line, own))[0]
+    grad_hidden = add_up(exchange(line.reshape(NX, -1, tokens), "voc", X_GROUPS)).T
+    by_core = (NZ, NC) + own.shape[1:]
+    mine_here = lax.broadcasted_iota(jnp.int32, by_core, 1) == core
+    grad_unembed = jnp.where(mine_here, own[:, None], other[:, None]).reshape(features, columns)
     return (loss, grad_hidden, grad_unembed)
 
 

time: 194 us -> 185 us (0.954)
  starting transfers between devices: 22.1 us -> 27.4 us
  waiting for transfers between devices: 32.4 us -> 28.2 us
  local copies, waits for them, and re-layouts: 15.4 us -> 11.6 us
  blocking collectives: 89.8 us -> 86.4 us
  Pallas kernels: 7.48 us -> 4.82 us
    ppermute x0 -> x1, starting transfers between devices: none -> 5.26 us  [body(): other = lax.ppermute(own, 'tok', CORE_SWAP)]
    all_gather x1 -> x0, waiting for transfers between devices: 5.06 us -> none  [body(): grad_unembed = lax.all_gather(summed, 'tok', axis=0, tiled=True)]
    all_to_all x5 -> x4, blocking collectives: 89.8 us -> 86.4 us  [exchange(): lax.all_to_all(blocks, axis, 0, 0, tiled=True, axis_index_groups=groups)]
    unnamed x14 -> x15, local copies, waits for them, and re-layouts: 5.54 us -> 2.22 us
    pallas_call x2 -> x1, Pallas kernels: 7.48 us -> 4.82 us  [product(): pl.pallas_call(product_kernel, grid=(count // rows,), in_specs=[pl.BlockS...]
    all_to_all x2, waiting for transfers between devices: 15.9 us -> 17.9 us  [exchange(): lax.all_to_all(blocks, axis, 0, 0, tiled=True, axis_index_groups=groups)]
  transfers between devices with their start and end apart: 7 -> 7, of which waited for: 6 -> 5; matrix products, arithmetic and copies ran while one was open for 9% -> 8% of each run, Pallas kernels for 1% -> 0%
where the time goes in v5:
time: 185 us; the launch traced here: 184 us
  blocking collectives  86.4 us (47%)
  waiting for transfers between devices  28.2 us (15%)
  starting transfers between devices  27.4 us (15%)
  between operations  14.2 us (8%)
  local copies, waits for them, and re-layouts  11.6 us (6%)
  matrix products  5.79 us (3%)
  other arithmetic  5.73 us (3%)
  Pallas kernels  4.82 us (3%)
    all_to_all x4, blocking collectives, exchange(): lax.all_to_all(blocks, axis, 0, 0, tiled=True, axis_index_groups=groups)  86.4 us
    all_to_all x2, waiting for transfers between devices, exchange(): lax.all_to_all(blocks, axis, 0, 0, tiled=True, axis_index_groups=groups)  17.9 us
    ppermute x1, starting transfers between devices, body(): came = lax.ppermute(given, 'tok', CORE_SWAP)  8.08 us
    all_to_all x2, starting transfers between devices, exchange(): lax.all_to_all(blocks, axis, 0, 0, tiled=True, axis_index_groups=groups)  7.17 us
    all_to_all x1, starting transfers between devices, body(): lax.all_to_all(jnp.broadcast_to(stats[None], (NX * NY,) + stats.shape), '...  6.84 us
    all_to_all x1, waiting for transfers between devices, body(): lax.all_to_all(jnp.broadcast_to(stats[None], (NX * NY,) + stats.shape), '...  5.93 us
    dot_general x4, matrix products, contract(): lax.dot_general(left, right, (dims, ((), ())), preferred_element_type=jnp...  5.79 us
    ppermute x1, starting transfers between devices, body(): other = lax.ppermute(own, 'tok', CORE_SWAP)  5.26 us
  transfers between devices with their start and end apart: 7, of which 5 were waited for; matrix products, arithmetic and copies ran while one was open for 8% of the time, Pallas kernels for 0%

profile of v5, /device:TPU:1, one launch (start us, length us, event | category | flops | bytes accessed | tf_op | source)
XLA Modules:
  0.0 184.1 jit_solution(12428394413093694083)
XLA Ops:
  7.2 0.0 all-gather.2.cloned.1.call-start
  7.2 0.8 slice.34
  8.1 10.3 %all_to_all.35 = bf16[4,64,512]{2,1,0:T(8,128)(2,1)} all-to-all(bf16[4,64,512]{2,1,0:T(8,128)(2,1)S(1)} %broadcast_in_dim.26), channel_id=1, replica_groups={{0,8,16,24},{1,9,17,25},{2,10,18,26},{3,11,19,27},{4,12,20,28},{5,13,21..., dimensions={0} | all-to-all | bytes 524288 | tf_op jit(solution)/shard_map/all_to_all | solution.py:16
  18.4 0.0 all-gather.2.cloned.1.call-update
  18.4 0.8 slice.35
  19.2 18.2 %all_to_all.36 = bf16[8,48,512]{2,1,0:T(8,128)(2,1)S(1)} all-to-all(bf16[8,48,512]{2,1,0:T(8,128)(2,1)S(1)} %broadcast_in_dim.27), channel_id=1, replica_groups={{0,1,2,3,4,5,6,7},{8,9,10,11,12,13,14,15},{16,17,18,19,20,21,22,23},{24..., dimensions={0} | all-to-all | bytes 786432 | tf_op jit(solution)/shard_map/all_to_all | solution.py:16
  37.4 1.3 broadcast_in_dim.29
  38.7 0.0 copy-start
  38.7 3.7 %all-to-all-start.2 = ((bf16[4,384,512]{2,1,0:T(8,128)(2,1)}), bf16[4,384,512]{2,1,0:T(8,128)(2,1)S(1)}, u32[]{:S(2)}, u32[]{:S(2)}) async-start(bf16[4,384,512]{2,1,0:T(8,128)(2,1)} %broadcast_in_dim.29), calls=%async_computation.2 | async-start | bytes 3145728 | tf_op jit(solution)/shard_map/all_to_all | solution.py:16
  42.4 0.0 copy-done
  42.4 0.9 slice.36
  43.4 0.1 slice_bitcast_fusion
  43.5 1.0 copy.24
  44.6 1.8 copy.25
  46.4 1.4 copy.28
  47.8 11.0 %all-to-all-done.2 = bf16[4,384,512]{2,1,0:T(8,128)(2,1)S(1)} async-done(((bf16[4,384,512]{2,1,0:T(8,128)(2,1)}), bf16[4,384,512]{2,1,0:T(8,128)(2,1)S(1)}, u32[]{:S(2)}, u32[]{:S(2)}) %all-to-all-start.2) | async-done | bytes 1572896 | tf_op jit(solution)/shard_map/all_to_all | solution.py:16
  58.7 1.8 convolution_bitcast_fusion
  60.5 2.2 %all-gather.2.cloned.1.call-done = bf16[2048,512]{1,0:T(8,128)(2,1)} async-done(((bf16[256,512]{1,0:T(8,128)(2,1)}), bf16[2048,512]{1,0:T(8,128)(2,1)}) %all-gather.2.cloned.1.call-update) | async-done | bytes 2097168 | tf_op jit(solution)/shard_map/all_gather | solution.py:69
  62.7 0.0 copy-start.4
  62.7 0.0 copy-start.5
  62.7 2.7 %fusion.5 = (f32[512]{0:T(512)S(1)}, f32[256,512]{1,0:T(8,128)S(1)}) fusion(f32[256,512]{1,0:T(8,128)S(1)} %convolution_bitcast_fusion, bf16[2048,256]{1,0:T(8,128)(2,1)} %bitcast.75, bf16[2048,512]{1,0:T(8,128)(2,1)} %all-gather.2.cloned.1.call-done), kind=kOutput, calls=%fused_computation.28 | convolution fusion | flops 537132544 | bytes 4196352 | tf_op jit(solution)/shard_map/dot_general | solution.py:35
  65.4 0.0 copy-done.4
  65.4 0.0 copy-done.5
  65.4 0.2 exponential_reduce_fusion
  65.7 0.8 broadcast_in_dim.30
  66.4 6.8 %all-to-all-start.3 = ((f32[32,4,512]{2,1,0:T(4,128)}), f32[32,4,512]{2,1,0:T(4,128)S(1)}, u32[]{:S(2)}, u32[]{:S(2)}) async-start(f32[32,4,512]{2,1,0:T(4,128)} %broadcast_in_dim.30), calls=%async_computation.3 | async-start | bytes 524288 | tf_op jit(solution)/shard_map/all_to_all | solution.py:88
  73.3 0.0 reduce-scatter.2.cloned.1.call-start
  73.3 1.8 pad_maximum_fusion
  75.1 0.3 copy.27
  75.5 0.0 copy-start.6
  75.5 1.5 constant_dynamic-slice_fusion
  77.0 5.9 %all-to-all-done.3 = f32[32,4,512]{2,1,0:T(4,128)S(1)} async-done(((f32[32,4,512]{2,1,0:T(4,128)}), f32[32,4,512]{2,1,0:T(4,128)S(1)}, u32[]{:S(2)}, u32[]{:S(2)}) %all-to-all-start.3) | async-done | bytes 262176 | tf_op jit(solution)/shard_map/all_to_all | solution.py:88
  82.9 0.0 copy-start.1
  82.9 0.2 slice_reduce_fusion
  83.1 0.1 copy.31
  83.3 0.6 multiply_add_fusion
  83.8 0.0 copy-done.6
  83.8 0.2 multiply_convert_fusion.right
  84.0 0.4 copy-done.1
  84.4 0.0 copy-start.2
  84.4 0.7 convolution_convert_fusion
  85.1 0.0 copy-done.2
  85.1 4.8 %shard_map.76 = bf16[3584,512]{1,0:T(8,128)(2,1)} custom-call(bf16[3584,256]{1,0:T(8,128)(2,1)} %bitcast.67, bf16[256,512]{1,0:T(8,128)(2,1)} %copy-done.2), custom_call_target="tpu_custom_call" | custom-call | flops 939524096 | bytes 5767168 | tf_op jit(solution)/shard_map/pallas_call | solution.py:44
  89.9 0.0 copy-start.3
  89.9 0.0 reduce-scatter.2.cloned.1.call-update
  90.0 8.1 %collective-permute-start = (bf16[1792,256]{1,0:T(8,128)(2,1)S(1)}, bf16[1792,256]{1,0:T(8,128)(2,1)S(1)}, u32[]{:S(2)}, u32[]{:S(2)}) collective-permute-start(bf16[1792,256]{1,0:T(8,128)(2,1)S(1)} %convolution_convert_fusion), channel_id=1, source_target_pairs={{0,32},{32,0},{64,96},{96,64},{128,160},{160,128},{192,224},{224,1... | collective-permute-start | bytes 2752520 | tf_op jit(solution)/shard_map/ppermute | solution.py:109
  98.0 2.1 %collective-permute-done = bf16[1792,256]{1,0:T(8,128)(2,1)S(1)} collective-permute-done((bf16[1792,256]{1,0:T(8,128)(2,1)S(1)}, bf16[1792,256]{1,0:T(8,128)(2,1)S(1)}, u32[]{:S(2)}, u32[]{:S(2)}) %collective-permute-start) | collective-permute-done | bytes 917536 | tf_op jit(solution)/shard_map/ppermute | solution.py:109
  100.1 0.0 copy-done.3
  100.1 0.7 add_convert_fusion
  100.8 32.0 %all_to_all.37 = bf16[8,224,256]{2,1,0:T(8,128)(2,1)S(1)} all-to-all(bf16[8,224,256]{2,1,0:T(8,128)(2,1)S(1)} %bitcast.72), channel_id=1, replica_groups={{0,64,128,192,256,320,384,448},{32,96,160,224,288,352,416,480},{1,65,12..., dimensions={0} | all-to-all | bytes 1835008 | tf_op jit(solution)/shard_map/all_to_all | solution.py:16
  132.8 0.1 reduce_sum.84
  132.9 0.1 broadcast_in_dim.31
  133.0 25.9 %all_to_all.38 = bf16[8,224,256]{2,1,0:T(8,128)(2,1)S(1)} all-to-all(bf16[8,224,256]{2,1,0:T(8,128)(2,1)S(1)} %broadcast_in_dim.31), channel_id=1, replica_groups={{0,64,128,192,256,320,384,448},{32,96,160,224,288,352,416,480},{1,65,12..., dimensions={0} | all-to-all | bytes 1835008 | tf_op jit(solution)/shard_map/all_to_all | solution.py:16
  158.9 5.3 %collective-permute-start.1 = (bf16[8,224,256]{2,1,0:T(8,128)(2,1)S(1)}, bf16[8,224,256]{2,1,0:T(8,128)(2,1)S(1)}, u32[]{:S(2)}, u32[]{:S(2)}) collective-permute-start(bf16[8,224,256]{2,1,0:T(8,128)(2,1)S(1)} %all_to_all.38), channel_id=1, source_target_pairs={{0,32},{32,0},{64,96},{96,64},{128,160},{160,128},{192,224},{224,1... | collective-permute-start | bytes 2752520 | tf_op jit(solution)/shard_map/ppermute | solution.py:118
  164.1 0.0 reduce-scatter.2.cloned.1.call-done
  164.2 3.5 %all-to-all-start.6 = ((bf16[4,112,512]{2,1,0:T(8,128)(2,1)}), bf16[4,112,512]{2,1,0:T(8,128)(2,1)S(1)}, u32[]{:S(2)}, u32[]{:S(2)}) async-start(bf16[4,112,512]{2,1,0:T(8,128)(2,1)} %bitcast.78), calls=%async_computation.7 | async-start | bytes 917504 | tf_op jit(solution)/shard_map/all_to_all | solution.py:16
  167.7 0.1 iota.11
  167.7 0.1 iota.12
  167.8 0.0 collective-permute-done.1
  167.8 1.8 bitcast_select_fusion
  169.6 6.9 %all-to-all-done.6 = bf16[4,112,512]{2,1,0:T(8,128)(2,1)S(1)} async-done(((bf16[4,112,512]{2,1,0:T(8,128)(2,1)}), bf16[4,112,512]{2,1,0:T(8,128)(2,1)S(1)}, u32[]{:S(2)}, u32[]{:S(2)}) %all-to-all-start.6) | async-done | bytes 458784 | tf_op jit(solution)/shard_map/all_to_all | solution.py:16
  176.5 0.7 reduce_sum.85
  (6 shorter events, 0.1 us)
Async XLA Ops:
  7.2 55.5 %all-gather.2.cloned.1.call-start = ((), (), s32[]{:S(2)}) async-start(), calls=%async_computation.8 | async-start | bytes 2359296 | tf_op jit(solution)/shard_map/all_gather | solution.py:69
  38.7 3.7 %copy-start = (bf16[3584,256]{1,0:T(8,128)(2,1)S(1)}, bf16[3584,256]{1,0:T(8,128)(2,1)}, u32[]{:S(2)}) copy-start(bf16[3584,256]{1,0:T(8,128)(2,1)} %param.6) | copy-start | bytes 5505028
  38.7 20.0 %all-to-all-start.2 = ((bf16[4,384,512]{2,1,0:T(8,128)(2,1)}), bf16[4,384,512]{2,1,0:T(8,128)(2,1)S(1)}, u32[]{:S(2)}, u32[]{:S(2)}) async-start(bf16[4,384,512]{2,1,0:T(8,128)(2,1)} %broadcast_in_dim.29), calls=%async_computation.2 | async-start | bytes 3145728 | tf_op jit(solution)/shard_map/all_to_all | solution.py:16
  62.7 2.7 %copy-start.4 = (bf16[512,256]{0,1:T(8,128)(2,1)S(1)}, bf16[512,256]{0,1:T(8,128)(2,1)}, u32[]{:S(2)}) copy-start(bf16[512,256]{0,1:T(8,128)(2,1)} %copy.25) | copy-start | bytes 786436
  62.7 2.7 %copy-start.5 = (f32[512]{0:T(512)S(1)}, f32[512]{0:T(512)}, u32[]{:S(2)}) copy-start(f32[512]{0:T(512)} %param.8) | copy-start | bytes 6148
  66.4 16.5 %all-to-all-start.3 = ((f32[32,4,512]{2,1,0:T(4,128)}), f32[32,4,512]{2,1,0:T(4,128)S(1)}, u32[]{:S(2)}, u32[]{:S(2)}) async-start(f32[32,4,512]{2,1,0:T(4,128)} %broadcast_in_dim.30), calls=%async_computation.3 | async-start | bytes 524288 | tf_op jit(solution)/shard_map/all_to_all | solution.py:88
  73.3 90.9 %reduce-scatter.2.cloned.1.call-start = ((), (), s32[]{:S(2)}) async-start(), calls=%async_computation.9 | async-start | bytes 4128768 | tf_op jit(solution)/shard_map/reduce_scatter | solution.py:112
  75.5 8.4 %copy-start.6 = (f32[512]{0:T(512)S(1)}, f32[512]{0:T(512)}, u32[]{:S(2)}) copy-start(f32[512]{0:T(512)} %param.9) | copy-start | bytes 6148
  82.9 1.5 copy-start.1
  84.4 0.7 copy-start.2
  89.9 10.2 %copy-start.3 = (bf16[256,512]{1,0:T(8,128)(2,1)S(1)}, bf16[256,512]{1,0:T(8,128)(2,1)}, u32[]{:S(2)}) copy-start(bf16[256,512]{1,0:T(8,128)(2,1)} %copy-done.2) | copy-start | bytes 786436
  90.0 10.2 %collective-permute-start = (bf16[1792,256]{1,0:T(8,128)(2,1)S(1)}, bf16[1792,256]{1,0:T(8,128)(2,1)S(1)}, u32[]{:S(2)}, u32[]{:S(2)}) collective-permute-start(bf16[1792,256]{1,0:T(8,128)(2,1)S(1)} %convolution_convert_fusion), channel_id=1, source_target_pairs={{0,32},{32,0},{64,96},{96,64},{128,160},{160,128},{192,224},{224,1... | collective-permute-start | bytes 2752520 | tf_op jit(solution)/shard_map/ppermute | solution.py:109
  158.9 9.0 %collective-permute-start.1 = (bf16[8,224,256]{2,1,0:T(8,128)(2,1)S(1)}, bf16[8,224,256]{2,1,0:T(8,128)(2,1)S(1)}, u32[]{:S(2)}, u32[]{:S(2)}) collective-permute-start(bf16[8,224,256]{2,1,0:T(8,128)(2,1)S(1)} %all_to_all.38), channel_id=1, source_target_pairs={{0,32},{32,0},{64,96},{96,64},{128,160},{160,128},{192,224},{224,1... | collective-permute-start | bytes 2752520 | tf_op jit(solution)/shard_map/ppermute | solution.py:118
  164.2 12.4 %all-to-all-start.6 = ((bf16[4,112,512]{2,1,0:T(8,128)(2,1)}), bf16[4,112,512]{2,1,0:T(8,128)(2,1)S(1)}, u32[]{:S(2)}, u32[]{:S(2)}) async-start(bf16[4,112,512]{2,1,0:T(8,128)(2,1)} %bitcast.78), calls=%async_computation.7 | async-start | bytes 917504 | tf_op jit(solution)/shard_map/all_to_all | solution.py:16
Sparse Core Ops, SparseCore 0:
  18.5 44.1 all-gather.1
  90.1 54.4 reduce-scatter.1

commit v6 on v5

--- a/solution.py
+++ b/solution.py
@@ -9,6 +9,7 @@
 X_GROUPS = [[x * NY + y for x in range(NX)] for y in range(NY)]
 Z_GROUPS = [[z * NC + c for z in range(NZ)] for c in range(NC)]
 CORE_SWAP = [(z * NC + c, z * NC + 1 - c) for z in range(NZ) for c in range(NC)]
+X_SHIFTS = [[(x * NY + y, (x + k) % NX * NY + y) for x in range(NX) for y in range(NY)] for k in range(NX)]
 GATHER_B = 64
 
 
@@ -115,9 +116,13 @@
     chip_terms = (contract(rows_kept, grad_logits, ((1,), (1,))) + came.astype(jnp.float32)).astype(jnp.bfloat16)
     summed = add_up(exchange(chip_terms.reshape(NZ, -1, columns), "tok", Z_GROUPS))
     own = spread(summed, "tok", Z_GROUPS)
+    x = lax.axis_index("voc") // NY
+    for_x = line.reshape(NX, -1, tokens)
+    blocks = [lax.dynamic_index_in_dim(for_x, lax.rem(x + k, NX), 0, False) for k in range(NX)]
+    arrived = blocks[:1] + [lax.ppermute(blocks[k], "voc", X_SHIFTS[k]) for k in range(1, NX)]
+    own, arrived = lax.optimization_barrier((own, arrived))
     other = lax.ppermute(own, "tok", CORE_SWAP)
-    line = lax.optimization_barrier((line, own))[0]
-    grad_hidden = add_up(exchange(line.reshape(NX, -1, tokens), "voc", X_GROUPS)).T
+    grad_hidden = sum(block.astype(jnp.float32) for block in arrived).astype(jnp.bfloat16).T
     by_core = (NZ, NC) + own.shape[1:]
     mine_here = lax.broadcasted_iota(jnp.int32, by_core, 1) == core
     grad_unembed = jnp.where(mine_here, own[:, None], other[:, None]).reshape(features, columns)

time: 185 us -> 178 us (0.962)
  blocking collectives: 86.4 us -> 60.4 us
  waiting for transfers between devices: 28.2 us -> 37 us
  starting transfers between devices: 27.4 us -> 35.1 us
  local copies, waits for them, and re-layouts: 11.6 us -> 13.7 us
    all_to_all x4 -> x3, blocking collectives: 86.4 us -> 60.4 us  [exchange(): lax.all_to_all(blocks, axis, 0, 0, tiled=True, axis_index_groups=groups)]
    ppermute x0 -> x3, starting transfers between devices: none -> 10.5 us  [body(): lax.ppermute(blocks[k], 'voc', X_SHIFTS[k])]
    reduce_scatter x1, waiting for transfers between devices: 0.02 us -> 7.14 us  [body(): lax.psum_scatter(product(by_y, grad_later), 'voc', axis_index_groups=Y_GR...]
    ppermute x1, starting transfers between devices: 5.26 us -> 2.4 us  [body(): other = lax.ppermute(own, 'tok', CORE_SWAP)]
  transfers between devices with their start and end apart: 7 -> 10, of which waited for: 5 -> 7; matrix products, arithmetic and copies ran while one was open for 8% -> 9% of each run, Pallas kernels for 0% -> 0%
where the time goes in v6:
time: 178 us; the launch traced here: 177 us
  blocking collectives  60.4 us (34%)
  waiting for transfers between devices  37 us (21%)
  starting transfers between devices  35.1 us (20%)
  between operations  14.3 us (8%)
  local copies, waits for them, and re-layouts  13.7 us (8%)
  matrix products  5.78 us (3%)
  other arithmetic  5.71 us (3%)
  Pallas kernels  4.82 us (3%)
    all_to_all x3, blocking collectives, exchange(): lax.all_to_all(blocks, axis, 0, 0, tiled=True, axis_index_groups=groups)  60.4 us
    all_to_all x2, waiting for transfers between devices, exchange(): lax.all_to_all(blocks, axis, 0, 0, tiled=True, axis_index_groups=groups)  18.4 us
    ppermute x3, starting transfers between devices, body(): lax.ppermute(blocks[k], 'voc', X_SHIFTS[k])  10.5 us
    ppermute x1, starting transfers between devices, body(): came = lax.ppermute(given, 'tok', CORE_SWAP)  8.08 us
    all_to_all x2, starting transfers between devices, exchange(): lax.all_to_all(blocks, axis, 0, 0, tiled=True, axis_index_groups=groups)  7.25 us
    reduce_scatter x1, waiting for transfers between devices, body(): lax.psum_scatter(product(by_y, grad_later), 'voc', axis_index_groups=Y_GR...  7.14 us
    all_to_all x1, starting transfers between devices, body(): lax.all_to_all(jnp.broadcast_to(stats[None], (NX * NY,) + stats.shape), '...  6.84 us
    all_to_all x1, waiting for transfers between devices, body(): lax.all_to_all(jnp.broadcast_to(stats[None], (NX * NY,) + stats.shape), '...  5.92 us
  transfers between devices with their start and end apart: 10, of which 7 were waited for; matrix products, arithmetic and copies ran while one was open for 9% of the time, Pallas kernels for 0%

profile of v6, /device:TPU:1, one launch (start us, length us, event | category | flops | bytes accessed | tf_op | source)
XLA Modules:
  0.0 176.8 jit_solution(3425054540286857766)
XLA Ops:
  7.2 0.0 all-gather.2.cloned.1.call-start
  7.2 0.8 slice.34
  8.1 10.3 %all_to_all.30 = bf16[4,64,512]{2,1,0:T(8,128)(2,1)} all-to-all(bf16[4,64,512]{2,1,0:T(8,128)(2,1)S(1)} %broadcast_in_dim.26), channel_id=1, replica_groups={{0,8,16,24},{1,9,17,25},{2,10,18,26},{3,11,19,27},{4,12,20,28},{5,13,21..., dimensions={0} | all-to-all | bytes 524288 | tf_op jit(solution)/shard_map/all_to_all | solution.py:17
  18.4 0.0 all-gather.2.cloned.1.call-update
  18.4 0.8 slice.35
  19.2 18.2 %all_to_all.31 = bf16[8,48,512]{2,1,0:T(8,128)(2,1)S(1)} all-to-all(bf16[8,48,512]{2,1,0:T(8,128)(2,1)S(1)} %broadcast_in_dim.27), channel_id=1, replica_groups={{0,1,2,3,4,5,6,7},{8,9,10,11,12,13,14,15},{16,17,18,19,20,21,22,23},{24..., dimensions={0} | all-to-all | bytes 786432 | tf_op jit(solution)/shard_map/all_to_all | solution.py:17
  37.4 1.3 broadcast_in_dim.29
  38.7 0.0 copy-start
  38.7 3.7 %all-to-all-start.2 = ((bf16[4,384,512]{2,1,0:T(8,128)(2,1)}), bf16[4,384,512]{2,1,0:T(8,128)(2,1)S(1)}, u32[]{:S(2)}, u32[]{:S(2)}) async-start(bf16[4,384,512]{2,1,0:T(8,128)(2,1)} %broadcast_in_dim.29), calls=%async_computation.2 | async-start | bytes 3145728 | tf_op jit(solution)/shard_map/all_to_all | solution.py:17
  42.4 0.0 copy-done
  42.4 1.0 slice.36
  43.4 0.1 slice_bitcast_fusion
  43.5 1.0 copy.24
  44.6 1.8 %copy.25 = bf16[512,256]{0,1:T(8,128)(2,1)} copy(bf16[512,256]{1,0:T(8,128)(2,1)} %param.7) | data formatting | bytes 524288 | tf_op args[2]
  46.4 1.4 copy.28
  47.8 10.9 %all-to-all-done.2 = bf16[4,384,512]{2,1,0:T(8,128)(2,1)S(1)} async-done(((bf16[4,384,512]{2,1,0:T(8,128)(2,1)}), bf16[4,384,512]{2,1,0:T(8,128)(2,1)S(1)}, u32[]{:S(2)}, u32[]{:S(2)}) %all-to-all-start.2) | async-done | bytes 1572896 | tf_op jit(solution)/shard_map/all_to_all | solution.py:17
  58.7 1.8 convolution_bitcast_fusion
  60.5 2.2 %all-gather.2.cloned.1.call-done = bf16[2048,512]{1,0:T(8,128)(2,1)} async-done(((bf16[256,512]{1,0:T(8,128)(2,1)}), bf16[2048,512]{1,0:T(8,128)(2,1)}) %all-gather.2.cloned.1.call-update) | async-done | bytes 2097168 | tf_op jit(solution)/shard_map/all_gather | solution.py:70
  62.7 0.0 copy-start.4
  62.7 2.7 %fusion.6 = (f32[512]{0:T(512)S(1)}, f32[256,512]{1,0:T(8,128)S(1)}) fusion(f32[256,512]{1,0:T(8,128)S(1)} %convolution_bitcast_fusion, bf16[2048,256]{1,0:T(8,128)(2,1)} %bitcast.84, bf16[2048,512]{1,0:T(8,128)(2,1)} %all-gather.2.cloned.1.call-done), kind=kOutput, calls=%fused_computation.34 | convolution fusion | flops 537132544 | bytes 4196352 | tf_op jit(solution)/shard_map/dot_general | solution.py:36
  65.4 0.0 copy-done.4
  65.4 0.0 copy-done.5
  65.4 0.2 exponential_reduce_fusion
  65.7 0.8 broadcast_in_dim.30
  66.4 6.8 %all-to-all-start.3 = ((f32[32,4,512]{2,1,0:T(4,128)}), f32[32,4,512]{2,1,0:T(4,128)S(1)}, u32[]{:S(2)}, u32[]{:S(2)}) async-start(f32[32,4,512]{2,1,0:T(4,128)} %broadcast_in_dim.30), calls=%async_computation.3 | async-start | bytes 524288 | tf_op jit(solution)/shard_map/all_to_all | solution.py:89
  73.3 0.0 reduce-scatter.2.cloned.1.call-start
  73.3 1.8 %pad_maximum_fusion = bf16[4,8,112,512]{3,2,0,1:T(8,128)(2,1)S(1)} fusion(bf16[4,8,64,512]{3,2,0,1:T(8,128)(2,1)} %bitcast.82, bf16[4,8,48,512]{3,2,1,0:T(8,128)(2,1)S(1)} %bitcast.80), kind=kLoop, calls=%fused_computation | loop fusion | flops 7340032 | bytes 7340032 | tf_op jit(solution)/shard_map/concatenate | solution.py:90
  75.2 0.3 copy.27
  75.5 0.0 copy-start.6
  75.5 1.5 constant_dynamic-slice_fusion
  77.0 5.9 %all-to-all-done.3 = f32[32,4,512]{2,1,0:T(4,128)S(1)} async-done(((f32[32,4,512]{2,1,0:T(4,128)}), f32[32,4,512]{2,1,0:T(4,128)S(1)}, u32[]{:S(2)}, u32[]{:S(2)}) %all-to-all-start.3) | async-done | bytes 262176 | tf_op jit(solution)/shard_map/all_to_all | solution.py:89
  82.9 0.2 slice_reduce_fusion
  83.1 0.1 copy.31
  83.3 0.6 multiply_add_fusion
  83.9 0.0 copy-done.6
  83.9 0.2 multiply_convert_fusion.right
  84.1 0.4 copy-done.1
  84.4 0.7 convolution_convert_fusion
  85.1 0.0 copy-done.2
  85.1 4.8 %shard_map.76 = bf16[3584,512]{1,0:T(8,128)(2,1)} custom-call(bf16[3584,256]{1,0:T(8,128)(2,1)} %bitcast.76, bf16[256,512]{1,0:T(8,128)(2,1)} %copy-done.2), custom_call_target="tpu_custom_call" | custom-call | flops 939524096 | bytes 5767168 | tf_op jit(solution)/shard_map/pallas_call | solution.py:45
  89.9 0.0 reduce-scatter.2.cloned.1.call-update
  90.0 8.1 %collective-permute-start = (bf16[1792,256]{1,0:T(8,128)(2,1)S(1)}, bf16[1792,256]{1,0:T(8,128)(2,1)S(1)}, u32[]{:S(2)}, u32[]{:S(2)}) collective-permute-start(bf16[1792,256]{1,0:T(8,128)(2,1)S(1)} %convolution_convert_fusion), channel_id=1, source_target_pairs={{0,32},{32,0},{64,96},{96,64},{128,160},{160,128},{192,224},{224,1... | collective-permute-start | bytes 2752520 | tf_op jit(solution)/shard_map/ppermute | solution.py:110
  98.0 2.1 %collective-permute-done = bf16[1792,256]{1,0:T(8,128)(2,1)S(1)} collective-permute-done((bf16[1792,256]{1,0:T(8,128)(2,1)S(1)}, bf16[1792,256]{1,0:T(8,128)(2,1)S(1)}, u32[]{:S(2)}, u32[]{:S(2)}) %collective-permute-start) | collective-permute-done | bytes 917536 | tf_op jit(solution)/shard_map/ppermute | solution.py:110
  100.1 0.0 copy-done.3
  100.1 0.7 add_convert_fusion
  100.8 31.9 %all_to_all.32 = bf16[8,224,256]{2,1,0:T(8,128)(2,1)S(1)} all-to-all(bf16[8,224,256]{2,1,0:T(8,128)(2,1)S(1)} %bitcast.81), channel_id=1, replica_groups={{0,64,128,192,256,320,384,448},{32,96,160,224,288,352,416,480},{1,65,12..., dimensions={0} | all-to-all | bytes 1835008 | tf_op jit(solution)/shard_map/all_to_all | solution.py:17
  132.7 0.1 reduce_sum.72
  132.9 1.0 broadcast_in_dim.31
  133.8 3.6 %all-to-all-start.5 = ((bf16[8,224,256]{2,1,0:T(8,128)(2,1)}), bf16[8,224,256]{2,1,0:T(8,128)(2,1)S(1)}, u32[]{:S(2)}, u32[]{:S(2)}) async-start(bf16[8,224,256]{2,1,0:T(8,128)(2,1)} %broadcast_in_dim.31), calls=%async_computation.5 | async-start | bytes 1835008 | tf_op jit(solution)/shard_map/all_to_all | solution.py:17
  137.5 7.1 %reduce-scatter.2.cloned.1.call-done = bf16[448,512]{1,0:T(8,128)(2,1)} async-done(((bf16[3584,512]{1,0:T(8,128)(2,1)}), bf16[448,512]{1,0:T(8,128)(2,1)}) %reduce-scatter.2.cloned.1.call-update) | async-done | bytes 458768 | tf_op jit(solution)/shard_map/reduce_scatter | solution.py:113
  144.6 1.1 dynamic-slice_bitcast_fusion
  145.7 3.1 %collective-permute-start.1 = (bf16[112,512]{1,0:T(8,128)(2,1)S(1)}, bf16[112,512]{1,0:T(8,128)(2,1)S(1)}, u32[]{:S(2)}, u32[]{:S(2)}) collective-permute-start(bf16[112,512]{1,0:T(8,128)(2,1)S(1)} %get-tuple-element.36), channel_id=1, source_target_pairs={{0,8},{1,9},{2,10},{3,11},{4,12},{5,13},{6,14},{7,15},{8,16},{9,17... | collective-permute-start | bytes 344072 | tf_op jit(solution)/shard_map/ppermute | solution.py:122
  148.8 4.3 %collective-permute-start.2 = (bf16[112,512]{1,0:T(8,128)(2,1)S(1)}, bf16[112,512]{1,0:T(8,128)(2,1)S(1)}, u32[]{:S(2)}, u32[]{:S(2)}) collective-permute-start(bf16[112,512]{1,0:T(8,128)(2,1)S(1)} %get-tuple-element.35), channel_id=1, source_target_pairs={{0,16},{1,17},{2,18},{3,19},{4,20},{5,21},{6,22},{7,23},{8,24},{9,... | collective-permute-start | bytes 344072 | tf_op jit(solution)/shard_map/ppermute | solution.py:122
  153.2 3.1 %collective-permute-start.3 = (bf16[112,512]{1,0:T(8,128)(2,1)S(1)}, bf16[112,512]{1,0:T(8,128)(2,1)S(1)}, u32[]{:S(2)}, u32[]{:S(2)}) collective-permute-start(bf16[112,512]{1,0:T(8,128)(2,1)S(1)} %get-tuple-element.34), channel_id=1, source_target_pairs={{0,24},{1,25},{2,26},{3,27},{4,28},{5,29},{6,30},{7,31},{8,0},{9,1... | collective-permute-start | bytes 344072 | tf_op jit(solution)/shard_map/ppermute | solution.py:122
  156.2 7.5 %all-to-all-done.5 = bf16[8,224,256]{2,1,0:T(8,128)(2,1)S(1)} async-done(((bf16[8,224,256]{2,1,0:T(8,128)(2,1)}), bf16[8,224,256]{2,1,0:T(8,128)(2,1)S(1)}, u32[]{:S(2)}, u32[]{:S(2)}) %all-to-all-start.5) | async-done | bytes 917536 | tf_op jit(solution)/shard_map/all_to_all | solution.py:17
  163.7 0.0 collective-permute-done.1
  163.7 0.0 collective-permute-done.2
  163.7 0.0 collective-permute-done.3
  163.7 2.4 %collective-permute-start.4 = (bf16[8,224,256]{2,1,0:T(8,128)(2,1)S(1)}, bf16[8,224,256]{2,1,0:T(8,128)(2,1)S(1)}, u32[]{:S(2)}, u32[]{:S(2)}) collective-permute-start(bf16[8,224,256]{2,1,0:T(8,128)(2,1)S(1)} %all-to-all-done.5), channel_id=1, source_target_pairs={{0,32},{32,0},{64,96},{96,64},{128,160},{160,128},{192,224},{224,1... | collective-permute-start | bytes 2752520 | tf_op jit(solution)/shard_map/ppermute | solution.py:124
  166.1 0.1 iota.11
  166.2 0.1 iota.12
  166.3 0.7 fusion.3
  167.0 1.2 collective-permute-done.4
  168.2 1.8 %bitcast_select_fusion = bf16[3584,256]{1,0:T(8,128)(2,1)} fusion(pred[3584]{0:T(1024)(128)(4,1)S(1)} %iota.12, bf16[8,224,256]{2,1,0:T(8,128)(2,1)S(1)} %collective-permute-done.4, bf16[8,224,256]{2,1,0:T(8,128)(2,1)S(1)} %all-to-all-done.5), kind=kLoop, calls=%fused_computation.2 | loop fusion | flops 917504 | bytes 3673600 | tf_op jit(solution)/shard_map/jit(_where)/select_n | solution.py:128
  (10 shorter events, 0.1 us)
Async XLA Ops:
  7.2 55.5 %all-gather.2.cloned.1.call-start = ((), (), s32[]{:S(2)}) async-start(), calls=%async_computation.7 | async-start | bytes 2359296 | tf_op jit(solution)/shard_map/all_gather | solution.py:70
  38.7 3.7 %copy-start = (bf16[3584,256]{1,0:T(8,128)(2,1)S(1)}, bf16[3584,256]{1,0:T(8,128)(2,1)}, u32[]{:S(2)}) copy-start(bf16[3584,256]{1,0:T(8,128)(2,1)} %param.6) | copy-start | bytes 5505028
  38.7 20.0 %all-to-all-start.2 = ((bf16[4,384,512]{2,1,0:T(8,128)(2,1)}), bf16[4,384,512]{2,1,0:T(8,128)(2,1)S(1)}, u32[]{:S(2)}, u32[]{:S(2)}) async-start(bf16[4,384,512]{2,1,0:T(8,128)(2,1)} %broadcast_in_dim.29), calls=%async_computation.2 | async-start | bytes 3145728 | tf_op jit(solution)/shard_map/all_to_all | solution.py:17
  62.7 2.7 %copy-start.4 = (bf16[512,256]{0,1:T(8,128)(2,1)S(1)}, bf16[512,256]{0,1:T(8,128)(2,1)}, u32[]{:S(2)}) copy-start(bf16[512,256]{0,1:T(8,128)(2,1)} %copy.25) | copy-start | bytes 786436
  62.7 2.7 %copy-start.5 = (f32[512]{0:T(512)S(1)}, f32[512]{0:T(512)}, u32[]{:S(2)}) copy-start(f32[512]{0:T(512)} %param.8) | copy-start | bytes 6148
  66.4 16.5 %all-to-all-start.3 = ((f32[32,4,512]{2,1,0:T(4,128)}), f32[32,4,512]{2,1,0:T(4,128)S(1)}, u32[]{:S(2)}, u32[]{:S(2)}) async-start(f32[32,4,512]{2,1,0:T(4,128)} %broadcast_in_dim.30), calls=%async_computation.3 | async-start | bytes 524288 | tf_op jit(solution)/shard_map/all_to_all | solution.py:89
  73.3 71.3 %reduce-scatter.2.cloned.1.call-start = ((), (), s32[]{:S(2)}) async-start(), calls=%async_computation.8 | async-start | bytes 4128768 | tf_op jit(solution)/shard_map/reduce_scatter | solution.py:113
  75.5 8.4 %copy-start.6 = (f32[512]{0:T(512)S(1)}, f32[512]{0:T(512)}, u32[]{:S(2)}) copy-start(f32[512]{0:T(512)} %param.9) | copy-start | bytes 6148
  82.9 1.5 copy-start.1
  84.4 0.7 copy-start.2
  89.9 10.2 %copy-start.3 = (bf16[256,512]{1,0:T(8,128)(2,1)S(1)}, bf16[256,512]{1,0:T(8,128)(2,1)}, u32[]{:S(2)}) copy-start(bf16[256,512]{1,0:T(8,128)(2,1)} %copy-done.2) | copy-start | bytes 786436
  90.0 10.2 %collective-permute-start = (bf16[1792,256]{1,0:T(8,128)(2,1)S(1)}, bf16[1792,256]{1,0:T(8,128)(2,1)S(1)}, u32[]{:S(2)}, u32[]{:S(2)}) collective-permute-start(bf16[1792,256]{1,0:T(8,128)(2,1)S(1)} %convolution_convert_fusion), channel_id=1, source_target_pairs={{0,32},{32,0},{64,96},{96,64},{128,160},{160,128},{192,224},{224,1... | collective-permute-start | bytes 2752520 | tf_op jit(solution)/shard_map/ppermute | solution.py:110
  133.8 29.9 %all-to-all-start.5 = ((bf16[8,224,256]{2,1,0:T(8,128)(2,1)}), bf16[8,224,256]{2,1,0:T(8,128)(2,1)S(1)}, u32[]{:S(2)}, u32[]{:S(2)}) async-start(bf16[8,224,256]{2,1,0:T(8,128)(2,1)} %broadcast_in_dim.31), calls=%async_computation.5 | async-start | bytes 1835008 | tf_op jit(solution)/shard_map/all_to_all | solution.py:17
  145.7 18.0 %collective-permute-start.1 = (bf16[112,512]{1,0:T(8,128)(2,1)S(1)}, bf16[112,512]{1,0:T(8,128)(2,1)S(1)}, u32[]{:S(2)}, u32[]{:S(2)}) collective-permute-start(bf16[112,512]{1,0:T(8,128)(2,1)S(1)} %get-tuple-element.36), channel_id=1, source_target_pairs={{0,8},{1,9},{2,10},{3,11},{4,12},{5,13},{6,14},{7,15},{8,16},{9,17... | collective-permute-start | bytes 344072 | tf_op jit(solution)/shard_map/ppermute | solution.py:122
  148.8 14.9 %collective-permute-start.2 = (bf16[112,512]{1,0:T(8,128)(2,1)S(1)}, bf16[112,512]{1,0:T(8,128)(2,1)S(1)}, u32[]{:S(2)}, u32[]{:S(2)}) collective-permute-start(bf16[112,512]{1,0:T(8,128)(2,1)S(1)} %get-tuple-element.35), channel_id=1, source_target_pairs={{0,16},{1,17},{2,18},{3,19},{4,20},{5,21},{6,22},{7,23},{8,24},{9,... | collective-permute-start | bytes 344072 | tf_op jit(solution)/shard_map/ppermute | solution.py:122
  153.2 10.6 %collective-permute-start.3 = (bf16[112,512]{1,0:T(8,128)(2,1)S(1)}, bf16[112,512]{1,0:T(8,128)(2,1)S(1)}, u32[]{:S(2)}, u32[]{:S(2)}) collective-permute-start(bf16[112,512]{1,0:T(8,128)(2,1)S(1)} %get-tuple-element.34), channel_id=1, source_target_pairs={{0,24},{1,25},{2,26},{3,27},{4,28},{5,29},{6,30},{7,31},{8,0},{9,1... | collective-permute-start | bytes 344072 | tf_op jit(solution)/shard_map/ppermute | solution.py:122
  163.7 4.5 %collective-permute-start.4 = (bf16[8,224,256]{2,1,0:T(8,128)(2,1)S(1)}, bf16[8,224,256]{2,1,0:T(8,128)(2,1)S(1)}, u32[]{:S(2)}, u32[]{:S(2)}) collective-permute-start(bf16[8,224,256]{2,1,0:T(8,128)(2,1)S(1)} %all-to-all-done.5), channel_id=1, source_target_pairs={{0,32},{32,0},{64,96},{96,64},{128,160},{160,128},{192,224},{224,1... | collective-permute-start | bytes 2752520 | tf_op jit(solution)/shard_map/ppermute | solution.py:124
Sparse Core Ops, SparseCore 0:
  18.5 44.1 all-gather.1
  90.1 54.4 reduce-scatter.1

commit v7 on v6

--- a/solution.py
+++ b/solution.py
@@ -40,7 +40,7 @@
     out[...] = jnp.dot(left[...], right[...], preferred_element_type=jnp.float32).astype(out.dtype)
 
 
-def product(left, right, rows=896):
+def product(left, right, rows=1792):
     (count, depth), columns = left.shape, right.shape[1]
     return pl.pallas_call(
         product_kernel,

time: 178 us -> 177 us (level)
  no operation moved by 1% of the time
where the time goes in v7:
time: 177 us; the launch traced here: 176 us
  blocking collectives  60.5 us (34%)
  waiting for transfers between devices  37 us (21%)
  starting transfers between devices  35.1 us (20%)
  between operations  14.3 us (8%)
  local copies, waits for them, and re-layouts  13.7 us (8%)
  matrix products  5.78 us (3%)
  other arithmetic  5.71 us (3%)
  Pallas kernels  3.76 us (2%)
    all_to_all x3, blocking collectives, exchange(): lax.all_to_all(blocks, axis, 0, 0, tiled=True, axis_index_groups=groups)  60.5 us
    all_to_all x2, waiting for transfers between devices, exchange(): lax.all_to_all(blocks, axis, 0, 0, tiled=True, axis_index_groups=groups)  18.5 us
    ppermute x3, starting transfers between devices, body(): lax.ppermute(blocks[k], 'voc', X_SHIFTS[k])  10.5 us
    ppermute x1, starting transfers between devices, body(): came = lax.ppermute(given, 'tok', CORE_SWAP)  8.08 us
    all_to_all x2, starting transfers between devices, exchange(): lax.all_to_all(blocks, axis, 0, 0, tiled=True, axis_index_groups=groups)  7.25 us
    reduce_scatter x1, waiting for transfers between devices, body(): lax.psum_scatter(product(by_y, grad_later), 'voc', axis_index_groups=Y_GR...  7.03 us
    all_to_all x1, starting transfers between devices, body(): lax.all_to_all(jnp.broadcast_to(stats[None], (NX * NY,) + stats.shape), '...  6.84 us
    all_to_all x1, waiting for transfers between devices, body(): lax.all_to_all(jnp.broadcast_to(stats[None], (NX * NY,) + stats.shape), '...  5.92 us
  transfers between devices with their start and end apart: 10, of which 7 were waited for; matrix products, arithmetic and copies ran while one was open for 9% of the time, Pallas kernels for 0%

profile of v7, /device:TPU:1, one launch (start us, length us, event | category | flops | bytes accessed | tf_op | source)
XLA Modules:
  0.0 175.9 jit_solution(11012035756514714666)
XLA Ops:
  7.2 0.0 all-gather.2.cloned.1.call-start
  7.2 0.8 slice.34
  8.1 10.3 %all_to_all.30 = bf16[4,64,512]{2,1,0:T(8,128)(2,1)} all-to-all(bf16[4,64,512]{2,1,0:T(8,128)(2,1)S(1)} %broadcast_in_dim.26), channel_id=1, replica_groups={{0,8,16,24},{1,9,17,25},{2,10,18,26},{3,11,19,27},{4,12,20,28},{5,13,21..., dimensions={0} | all-to-all | bytes 524288 | tf_op jit(solution)/shard_map/all_to_all | solution.py:17
  18.4 0.0 all-gather.2.cloned.1.call-update
  18.4 0.8 slice.35
  19.2 18.2 %all_to_all.31 = bf16[8,48,512]{2,1,0:T(8,128)(2,1)S(1)} all-to-all(bf16[8,48,512]{2,1,0:T(8,128)(2,1)S(1)} %broadcast_in_dim.27), channel_id=1, replica_groups={{0,1,2,3,4,5,6,7},{8,9,10,11,12,13,14,15},{16,17,18,19,20,21,22,23},{24..., dimensions={0} | all-to-all | bytes 786432 | tf_op jit(solution)/shard_map/all_to_all | solution.py:17
  37.4 1.3 broadcast_in_dim.29
  38.7 0.0 copy-start
  38.7 3.7 %all-to-all-start.2 = ((bf16[4,384,512]{2,1,0:T(8,128)(2,1)}), bf16[4,384,512]{2,1,0:T(8,128)(2,1)S(1)}, u32[]{:S(2)}, u32[]{:S(2)}) async-start(bf16[4,384,512]{2,1,0:T(8,128)(2,1)} %broadcast_in_dim.29), calls=%async_computation.2 | async-start | bytes 3145728 | tf_op jit(solution)/shard_map/all_to_all | solution.py:17
  42.4 0.0 copy-done
  42.4 1.0 slice.36
  43.4 0.1 slice_bitcast_fusion
  43.5 1.0 copy.24
  44.6 1.8 %copy.25 = bf16[512,256]{0,1:T(8,128)(2,1)} copy(bf16[512,256]{1,0:T(8,128)(2,1)} %param.7) | data formatting | bytes 524288 | tf_op args[2]
  46.4 1.4 copy.28
  47.8 10.9 %all-to-all-done.2 = bf16[4,384,512]{2,1,0:T(8,128)(2,1)S(1)} async-done(((bf16[4,384,512]{2,1,0:T(8,128)(2,1)}), bf16[4,384,512]{2,1,0:T(8,128)(2,1)S(1)}, u32[]{:S(2)}, u32[]{:S(2)}) %all-to-all-start.2) | async-done | bytes 1572896 | tf_op jit(solution)/shard_map/all_to_all | solution.py:17
  58.7 1.8 convolution_bitcast_fusion
  60.5 2.2 %all-gather.2.cloned.1.call-done = bf16[2048,512]{1,0:T(8,128)(2,1)} async-done(((bf16[256,512]{1,0:T(8,128)(2,1)}), bf16[2048,512]{1,0:T(8,128)(2,1)}) %all-gather.2.cloned.1.call-update) | async-done | bytes 2097168 | tf_op jit(solution)/shard_map/all_gather | solution.py:70
  62.7 0.0 copy-start.4
  62.7 2.7 %fusion.6 = (f32[512]{0:T(512)S(1)}, f32[256,512]{1,0:T(8,128)S(1)}) fusion(f32[256,512]{1,0:T(8,128)S(1)} %convolution_bitcast_fusion, bf16[2048,256]{1,0:T(8,128)(2,1)} %bitcast.84, bf16[2048,512]{1,0:T(8,128)(2,1)} %all-gather.2.cloned.1.call-done), kind=kOutput, calls=%fused_computation.34 | convolution fusion | flops 537132544 | bytes 4196352 | tf_op jit(solution)/shard_map/dot_general | solution.py:36
  65.4 0.0 copy-done.4
  65.4 0.0 copy-done.5
  65.4 0.2 exponential_reduce_fusion
  65.7 0.8 broadcast_in_dim.30
  66.4 6.8 %all-to-all-start.3 = ((f32[32,4,512]{2,1,0:T(4,128)}), f32[32,4,512]{2,1,0:T(4,128)S(1)}, u32[]{:S(2)}, u32[]{:S(2)}) async-start(f32[32,4,512]{2,1,0:T(4,128)} %broadcast_in_dim.30), calls=%async_computation.3 | async-start | bytes 524288 | tf_op jit(solution)/shard_map/all_to_all | solution.py:89
  73.3 0.0 reduce-scatter.2.cloned.1.call-start
  73.3 1.8 %pad_maximum_fusion = bf16[4,8,112,512]{3,2,0,1:T(8,128)(2,1)S(1)} fusion(bf16[4,8,64,512]{3,2,0,1:T(8,128)(2,1)} %bitcast.82, bf16[4,8,48,512]{3,2,1,0:T(8,128)(2,1)S(1)} %bitcast.80), kind=kLoop, calls=%fused_computation | loop fusion | flops 7340032 | bytes 7340032 | tf_op jit(solution)/shard_map/concatenate | solution.py:90
  75.2 0.3 copy.27
  75.5 0.0 copy-start.6
  75.5 1.5 constant_dynamic-slice_fusion
  77.0 5.9 %all-to-all-done.3 = f32[32,4,512]{2,1,0:T(4,128)S(1)} async-done(((f32[32,4,512]{2,1,0:T(4,128)}), f32[32,4,512]{2,1,0:T(4,128)S(1)}, u32[]{:S(2)}, u32[]{:S(2)}) %all-to-all-start.3) | async-done | bytes 262176 | tf_op jit(solution)/shard_map/all_to_all | solution.py:89
  82.9 0.2 slice_reduce_fusion
  83.1 0.1 copy.31
  83.3 0.6 multiply_add_fusion
  83.9 0.0 copy-done.6
  83.9 0.2 multiply_convert_fusion.right
  84.1 0.4 copy-done.1
  84.4 0.7 convolution_convert_fusion
  85.1 0.0 copy-done.2
  85.1 3.8 %shard_map.76 = bf16[3584,512]{1,0:T(8,128)(2,1)} custom-call(bf16[3584,256]{1,0:T(8,128)(2,1)} %bitcast.76, bf16[256,512]{1,0:T(8,128)(2,1)} %copy-done.2), custom_call_target="tpu_custom_call" | custom-call | flops 939524096 | bytes 5767168 | tf_op jit(solution)/shard_map/pallas_call | solution.py:45
  88.9 0.0 reduce-scatter.2.cloned.1.call-update
  88.9 8.1 %collective-permute-start = (bf16[1792,256]{1,0:T(8,128)(2,1)S(1)}, bf16[1792,256]{1,0:T(8,128)(2,1)S(1)}, u32[]{:S(2)}, u32[]{:S(2)}) collective-permute-start(bf16[1792,256]{1,0:T(8,128)(2,1)S(1)} %convolution_convert_fusion), channel_id=1, source_target_pairs={{0,32},{32,0},{64,96},{96,64},{128,160},{160,128},{192,224},{224,1... | collective-permute-start | bytes 2752520 | tf_op jit(solution)/shard_map/ppermute | solution.py:110
  97.0 2.1 %collective-permute-done = bf16[1792,256]{1,0:T(8,128)(2,1)S(1)} collective-permute-done((bf16[1792,256]{1,0:T(8,128)(2,1)S(1)}, bf16[1792,256]{1,0:T(8,128)(2,1)S(1)}, u32[]{:S(2)}, u32[]{:S(2)}) %collective-permute-start) | collective-permute-done | bytes 917536 | tf_op jit(solution)/shard_map/ppermute | solution.py:110
  99.1 0.0 copy-done.3
  99.1 0.7 add_convert_fusion
  99.7 32.0 %all_to_all.32 = bf16[8,224,256]{2,1,0:T(8,128)(2,1)S(1)} all-to-all(bf16[8,224,256]{2,1,0:T(8,128)(2,1)S(1)} %bitcast.81), channel_id=1, replica_groups={{0,64,128,192,256,320,384,448},{32,96,160,224,288,352,416,480},{1,65,12..., dimensions={0} | all-to-all | bytes 1835008 | tf_op jit(solution)/shard_map/all_to_all | solution.py:17
  131.8 0.1 reduce_sum.72
  131.9 1.0 broadcast_in_dim.31
  132.9 3.6 %all-to-all-start.5 = ((bf16[8,224,256]{2,1,0:T(8,128)(2,1)}), bf16[8,224,256]{2,1,0:T(8,128)(2,1)S(1)}, u32[]{:S(2)}, u32[]{:S(2)}) async-start(bf16[8,224,256]{2,1,0:T(8,128)(2,1)} %broadcast_in_dim.31), calls=%async_computation.5 | async-start | bytes 1835008 | tf_op jit(solution)/shard_map/all_to_all | solution.py:17
  136.5 7.0 %reduce-scatter.2.cloned.1.call-done = bf16[448,512]{1,0:T(8,128)(2,1)} async-done(((bf16[3584,512]{1,0:T(8,128)(2,1)}), bf16[448,512]{1,0:T(8,128)(2,1)}) %reduce-scatter.2.cloned.1.call-update) | async-done | bytes 458768 | tf_op jit(solution)/shard_map/reduce_scatter | solution.py:113
  143.6 1.1 dynamic-slice_bitcast_fusion
  144.7 3.1 %collective-permute-start.1 = (bf16[112,512]{1,0:T(8,128)(2,1)S(1)}, bf16[112,512]{1,0:T(8,128)(2,1)S(1)}, u32[]{:S(2)}, u32[]{:S(2)}) collective-permute-start(bf16[112,512]{1,0:T(8,128)(2,1)S(1)} %get-tuple-element.36), channel_id=1, source_target_pairs={{0,8},{1,9},{2,10},{3,11},{4,12},{5,13},{6,14},{7,15},{8,16},{9,17... | collective-permute-start | bytes 344072 | tf_op jit(solution)/shard_map/ppermute | solution.py:122
  147.8 4.3 %collective-permute-start.2 = (bf16[112,512]{1,0:T(8,128)(2,1)S(1)}, bf16[112,512]{1,0:T(8,128)(2,1)S(1)}, u32[]{:S(2)}, u32[]{:S(2)}) collective-permute-start(bf16[112,512]{1,0:T(8,128)(2,1)S(1)} %get-tuple-element.35), channel_id=1, source_target_pairs={{0,16},{1,17},{2,18},{3,19},{4,20},{5,21},{6,22},{7,23},{8,24},{9,... | collective-permute-start | bytes 344072 | tf_op jit(solution)/shard_map/ppermute | solution.py:122
  152.1 3.1 %collective-permute-start.3 = (bf16[112,512]{1,0:T(8,128)(2,1)S(1)}, bf16[112,512]{1,0:T(8,128)(2,1)S(1)}, u32[]{:S(2)}, u32[]{:S(2)}) collective-permute-start(bf16[112,512]{1,0:T(8,128)(2,1)S(1)} %get-tuple-element.34), channel_id=1, source_target_pairs={{0,24},{1,25},{2,26},{3,27},{4,28},{5,29},{6,30},{7,31},{8,0},{9,1... | collective-permute-start | bytes 344072 | tf_op jit(solution)/shard_map/ppermute | solution.py:122
  155.2 7.6 %all-to-all-done.5 = bf16[8,224,256]{2,1,0:T(8,128)(2,1)S(1)} async-done(((bf16[8,224,256]{2,1,0:T(8,128)(2,1)}), bf16[8,224,256]{2,1,0:T(8,128)(2,1)S(1)}, u32[]{:S(2)}, u32[]{:S(2)}) %all-to-all-start.5) | async-done | bytes 917536 | tf_op jit(solution)/shard_map/all_to_all | solution.py:17
  162.8 0.0 collective-permute-done.1
  162.8 0.0 collective-permute-done.2
  162.8 0.0 collective-permute-done.3
  162.8 2.4 %collective-permute-start.4 = (bf16[8,224,256]{2,1,0:T(8,128)(2,1)S(1)}, bf16[8,224,256]{2,1,0:T(8,128)(2,1)S(1)}, u32[]{:S(2)}, u32[]{:S(2)}) collective-permute-start(bf16[8,224,256]{2,1,0:T(8,128)(2,1)S(1)} %all-to-all-done.5), channel_id=1, source_target_pairs={{0,32},{32,0},{64,96},{96,64},{128,160},{160,128},{192,224},{224,1... | collective-permute-start | bytes 2752520 | tf_op jit(solution)/shard_map/ppermute | solution.py:124
  165.2 0.1 iota.11
  165.3 0.1 iota.12
  165.4 0.7 fusion.3
  166.1 1.2 collective-permute-done.4
  167.3 1.8 %bitcast_select_fusion = bf16[3584,256]{1,0:T(8,128)(2,1)} fusion(pred[3584]{0:T(1024)(128)(4,1)S(1)} %iota.12, bf16[8,224,256]{2,1,0:T(8,128)(2,1)S(1)} %collective-permute-done.4, bf16[8,224,256]{2,1,0:T(8,128)(2,1)S(1)} %all-to-all-done.5), kind=kLoop, calls=%fused_computation.2 | loop fusion | flops 917504 | bytes 3673600 | tf_op jit(solution)/shard_map/jit(_where)/select_n | solution.py:128
  (10 shorter events, 0.1 us)
Async XLA Ops:
  7.2 55.5 %all-gather.2.cloned.1.call-start = ((), (), s32[]{:S(2)}) async-start(), calls=%async_computation.7 | async-start | bytes 2359296 | tf_op jit(solution)/shard_map/all_gather | solution.py:70
  38.7 3.7 %copy-start = (bf16[3584,256]{1,0:T(8,128)(2,1)S(1)}, bf16[3584,256]{1,0:T(8,128)(2,1)}, u32[]{:S(2)}) copy-start(bf16[3584,256]{1,0:T(8,128)(2,1)} %param.6) | copy-start | bytes 5505028
  38.7 20.0 %all-to-all-start.2 = ((bf16[4,384,512]{2,1,0:T(8,128)(2,1)}), bf16[4,384,512]{2,1,0:T(8,128)(2,1)S(1)}, u32[]{:S(2)}, u32[]{:S(2)}) async-start(bf16[4,384,512]{2,1,0:T(8,128)(2,1)} %broadcast_in_dim.29), calls=%async_computation.2 | async-start | bytes 3145728 | tf_op jit(solution)/shard_map/all_to_all | solution.py:17
  62.7 2.7 %copy-start.4 = (bf16[512,256]{0,1:T(8,128)(2,1)S(1)}, bf16[512,256]{0,1:T(8,128)(2,1)}, u32[]{:S(2)}) copy-start(bf16[512,256]{0,1:T(8,128)(2,1)} %copy.25) | copy-start | bytes 786436
  62.7 2.7 %copy-start.5 = (f32[512]{0:T(512)S(1)}, f32[512]{0:T(512)}, u32[]{:S(2)}) copy-start(f32[512]{0:T(512)} %param.8) | copy-start | bytes 6148
  66.4 16.5 %all-to-all-start.3 = ((f32[32,4,512]{2,1,0:T(4,128)}), f32[32,4,512]{2,1,0:T(4,128)S(1)}, u32[]{:S(2)}, u32[]{:S(2)}) async-start(f32[32,4,512]{2,1,0:T(4,128)} %broadcast_in_dim.30), calls=%async_computation.3 | async-start | bytes 524288 | tf_op jit(solution)/shard_map/all_to_all | solution.py:89
  73.3 70.3 %reduce-scatter.2.cloned.1.call-start = ((), (), s32[]{:S(2)}) async-start(), calls=%async_computation.8 | async-start | bytes 4128768 | tf_op jit(solution)/shard_map/reduce_scatter | solution.py:113
  75.5 8.4 %copy-start.6 = (f32[512]{0:T(512)S(1)}, f32[512]{0:T(512)}, u32[]{:S(2)}) copy-start(f32[512]{0:T(512)} %param.9) | copy-start | bytes 6148
  82.9 1.5 copy-start.1
  84.4 0.7 copy-start.2
  88.9 10.2 %copy-start.3 = (bf16[256,512]{1,0:T(8,128)(2,1)S(1)}, bf16[256,512]{1,0:T(8,128)(2,1)}, u32[]{:S(2)}) copy-start(bf16[256,512]{1,0:T(8,128)(2,1)} %copy-done.2) | copy-start | bytes 786436
  88.9 10.2 %collective-permute-start = (bf16[1792,256]{1,0:T(8,128)(2,1)S(1)}, bf16[1792,256]{1,0:T(8,128)(2,1)S(1)}, u32[]{:S(2)}, u32[]{:S(2)}) collective-permute-start(bf16[1792,256]{1,0:T(8,128)(2,1)S(1)} %convolution_convert_fusion), channel_id=1, source_target_pairs={{0,32},{32,0},{64,96},{96,64},{128,160},{160,128},{192,224},{224,1... | collective-permute-start | bytes 2752520 | tf_op jit(solution)/shard_map/ppermute | solution.py:110
  132.9 29.9 %all-to-all-start.5 = ((bf16[8,224,256]{2,1,0:T(8,128)(2,1)}), bf16[8,224,256]{2,1,0:T(8,128)(2,1)S(1)}, u32[]{:S(2)}, u32[]{:S(2)}) async-start(bf16[8,224,256]{2,1,0:T(8,128)(2,1)} %broadcast_in_dim.31), calls=%async_computation.5 | async-start | bytes 1835008 | tf_op jit(solution)/shard_map/all_to_all | solution.py:17
  144.7 18.1 %collective-permute-start.1 = (bf16[112,512]{1,0:T(8,128)(2,1)S(1)}, bf16[112,512]{1,0:T(8,128)(2,1)S(1)}, u32[]{:S(2)}, u32[]{:S(2)}) collective-permute-start(bf16[112,512]{1,0:T(8,128)(2,1)S(1)} %get-tuple-element.36), channel_id=1, source_target_pairs={{0,8},{1,9},{2,10},{3,11},{4,12},{5,13},{6,14},{7,15},{8,16},{9,17... | collective-permute-start | bytes 344072 | tf_op jit(solution)/shard_map/ppermute | solution.py:122
  147.8 15.0 %collective-permute-start.2 = (bf16[112,512]{1,0:T(8,128)(2,1)S(1)}, bf16[112,512]{1,0:T(8,128)(2,1)S(1)}, u32[]{:S(2)}, u32[]{:S(2)}) collective-permute-start(bf16[112,512]{1,0:T(8,128)(2,1)S(1)} %get-tuple-element.35), channel_id=1, source_target_pairs={{0,16},{1,17},{2,18},{3,19},{4,20},{5,21},{6,22},{7,23},{8,24},{9,... | collective-permute-start | bytes 344072 | tf_op jit(solution)/shard_map/ppermute | solution.py:122
  152.1 10.7 %collective-permute-start.3 = (bf16[112,512]{1,0:T(8,128)(2,1)S(1)}, bf16[112,512]{1,0:T(8,128)(2,1)S(1)}, u32[]{:S(2)}, u32[]{:S(2)}) collective-permute-start(bf16[112,512]{1,0:T(8,128)(2,1)S(1)} %get-tuple-element.34), channel_id=1, source_target_pairs={{0,24},{1,25},{2,26},{3,27},{4,28},{5,29},{6,30},{7,31},{8,0},{9,1... | collective-permute-start | bytes 344072 | tf_op jit(solution)/shard_map/ppermute | solution.py:122
  162.8 4.5 %collective-permute-start.4 = (bf16[8,224,256]{2,1,0:T(8,128)(2,1)S(1)}, bf16[8,224,256]{2,1,0:T(8,128)(2,1)S(1)}, u32[]{:S(2)}, u32[]{:S(2)}) collective-permute-start(bf16[8,224,256]{2,1,0:T(8,128)(2,1)S(1)} %all-to-all-done.5), channel_id=1, source_target_pairs={{0,32},{32,0},{64,96},{96,64},{128,160},{160,128},{192,224},{224,1... | collective-permute-start | bytes 2752520 | tf_op jit(solution)/shard_map/ppermute | solution.py:124
Sparse Core Ops, SparseCore 0:
  18.5 44.1 all-gather.1
  89.0 54.4 reduce-scatter.1

commit v8 on v7

--- a/solution.py
+++ b/solution.py
@@ -59,6 +59,54 @@
     )(left, right)
 
 
+def stats_kernel(columns, rows, part, teacher, lse, logits, stats):
+    step = pl.program_id(0)
+
+    @pl.when(step == 0)
+    def _():
+        logits[...] = part[...]
+
+    logits[...] += jnp.dot(columns[...], rows[...], preferred_element_type=jnp.float32)
+
+    @pl.when(step == pl.num_programs(0) - 1)
+    def _():
+        value = logits[...]
+        shifted = teacher[...].astype(jnp.float32) - lse[...]
+        probs = jnp.exp(shifted)
+        top = jnp.max(value, axis=0, keepdims=True)
+        total = jnp.sum(jnp.exp(value - top), axis=0, keepdims=True)
+        mass = jnp.sum(probs, axis=0, keepdims=True)
+        cross = jnp.sum(probs * (shifted - value), axis=0, keepdims=True)
+        for k, stat in enumerate((top, total, mass, cross)):
+            stats[:, k, :] = jnp.broadcast_to(stat, (stats.shape[0], stats.shape[2]))
+
+
+def logits_and_stats(columns, rows, part, teacher, lse, copies, depth=512):
+    (count, features), tokens = columns.shape, rows.shape[1]
+    whole = lambda shape: pl.BlockSpec(shape, lambda i: (0,) * len(shape))
+    return pl.pallas_call(
+        stats_kernel,
+        grid=(features // depth,),
+        in_specs=[
+            pl.BlockSpec((count, depth), lambda i: (0, i)),
+            pl.BlockSpec((depth, tokens), lambda i: (i, 0)),
+            whole((count, tokens)),
+            whole((count, tokens)),
+            whole((1, tokens)),
+        ],
+        out_specs=[whole((count, tokens)), whole((copies, 4, tokens))],
+        out_shape=[
+            jax.ShapeDtypeStruct((count, tokens), jnp.float32),
+            jax.ShapeDtypeStruct((copies, 4, tokens), jnp.float32),
+        ],
+        cost_estimate=pl.CostEstimate(
+            flops=2 * count * features * tokens,
+            bytes_accessed=2 * features * (count + tokens) + 12 * count * tokens,
+            transcendentals=2 * count * tokens,
+        ),
+    )(columns, rows, part, teacher, lse)
+
+
 def body(hidden, unembed, teacher, teacher_lse, cotangent):
     tokens, columns = teacher.shape
     features = unembed.shape[0]
@@ -77,16 +125,17 @@
     unembed_a = by_shard[:, :, GATHER_B:].reshape(-1, columns)
     by_y = by_shard.transpose(1, 0, 2, 3).reshape(features, columns)
 
-    teacher_t = teacher.T.astype(jnp.float32)
-    shifted = teacher_t - teacher_lse[None, :]
-    probs = jnp.exp(shifted)
-    logits = contract(unembed_b, gathered_b, ((0,), (0,))) + contract(unembed_a, gathered_a, ((0,), (0,)))
-    top = jnp.max(logits, axis=0)
-    total = jnp.sum(jnp.exp(logits - top[None, :]), axis=0)
-    mass = jnp.sum(probs, axis=0)
-    cross = jnp.sum(probs * (shifted - logits), axis=0)
-    stats = jnp.stack([top, total, mass, cross])
-    every = lax.all_to_all(jnp.broadcast_to(stats[None], (NX * NY,) + stats.shape), "voc", 0, 0, tiled=True)
+    columns_b, teacher_t = lax.optimization_barrier((unembed_b.T, teacher.T))
+    logits, stats = logits_and_stats(
+        columns_b,
+        gathered_b,
+        contract(unembed_a, gathered_a, ((0,), (0,))),
+        teacher_t,
+        teacher_lse[None, :],
+        NX * NY,
+    )
+    every = lax.all_to_all(stats, "voc", 0, 0, tiled=True)
+    probs = jnp.exp(teacher_t.astype(jnp.float32) - teacher_lse[None, :])
     natural = jnp.concatenate(
         [
             gathered_b.reshape(NY, NX, GATHER_B, tokens).transpose(1, 0, 2, 3),

time: 177 us -> 178 us (level)
  Pallas kernels: 3.76 us -> 8.55 us
  matrix products: 5.78 us -> 2.75 us
  local copies, waits for them, and re-layouts: 13.7 us -> 16.1 us
    pallas_call x0 -> x1, Pallas kernels: none -> 4.79 us  [logits_and_stats(): pl.pallas_call(stats_kernel, grid=(features // depth,), in_specs=[pl.Bloc...]
    dot_general x4 -> x3, matrix products: 5.78 us -> 2.75 us  [contract(): lax.dot_general(left, right, (dims, ((), ())), preferred_element_type=jnp...]
    all_to_all x1, waiting for transfers between devices: 5.92 us -> 3.25 us  [body(): every = lax.all_to_all(stats, 'voc', 0, 0, tiled=True)]
where the time goes in v8:
time: 178 us; the launch traced here: 177 us
  blocking collectives  60.5 us (34%)
  waiting for transfers between devices  35.5 us (20%)
  starting transfers between devices  35.1 us (20%)
  local copies, waits for them, and re-layouts  16.1 us (9%)
  between operations  14.3 us (8%)
  Pallas kernels  8.55 us (5%)
  other arithmetic  3.96 us (2%)
  matrix products  2.75 us (2%)
    all_to_all x3, blocking collectives, exchange(): lax.all_to_all(blocks, axis, 0, 0, tiled=True, axis_index_groups=groups)  60.5 us
    all_to_all x2, waiting for transfers between devices, exchange(): lax.all_to_all(blocks, axis, 0, 0, tiled=True, axis_index_groups=groups)  18.6 us
    ppermute x3, starting transfers between devices, body(): lax.ppermute(blocks[k], 'voc', X_SHIFTS[k])  10.5 us
    ppermute x1, starting transfers between devices, body(): came = lax.ppermute(given, 'tok', CORE_SWAP)  8.07 us
    reduce_scatter x1, waiting for transfers between devices, body(): lax.psum_scatter(product(by_y, grad_later), 'voc', axis_index_groups=Y_GR...  7.79 us
    all_to_all x2, starting transfers between devices, exchange(): lax.all_to_all(blocks, axis, 0, 0, tiled=True, axis_index_groups=groups)  7.25 us
    all_to_all x1, starting transfers between devices, body(): every = lax.all_to_all(stats, 'voc', 0, 0, tiled=True)  6.84 us
    pallas_call x1, Pallas kernels, logits_and_stats(): pl.pallas_call(stats_kernel, grid=(features // depth,), in_specs=[pl.Bloc...  4.79 us
  transfers between devices with their start and end apart: 10, of which 7 were waited for; matrix products, arithmetic and copies ran while one was open for 9% of the time, Pallas kernels for 0%

profile of v8, /device:TPU:1, one launch (start us, length us, event | category | flops | bytes accessed | tf_op | source)
XLA Modules:
  0.0 176.9 jit_solution(3218061261746306637)
XLA Ops:
  7.2 0.0 all-gather.2.cloned.1.call-start
  7.2 0.8 slice.34
  8.1 10.3 %all_to_all.30 = bf16[4,64,512]{2,1,0:T(8,128)(2,1)} all-to-all(bf16[4,64,512]{2,1,0:T(8,128)(2,1)S(1)} %broadcast_in_dim.26), channel_id=1, replica_groups={{0,8,16,24},{1,9,17,25},{2,10,18,26},{3,11,19,27},{4,12,20,28},{5,13,21..., dimensions={0} | all-to-all | bytes 524288 | tf_op jit(solution)/shard_map/all_to_all | solution.py:17
  18.4 0.0 all-gather.2.cloned.1.call-update
  18.4 0.8 slice.35
  19.2 18.2 %all_to_all.31 = bf16[8,48,512]{2,1,0:T(8,128)(2,1)S(1)} all-to-all(bf16[8,48,512]{2,1,0:T(8,128)(2,1)S(1)} %broadcast_in_dim.27), channel_id=1, replica_groups={{0,1,2,3,4,5,6,7},{8,9,10,11,12,13,14,15},{16,17,18,19,20,21,22,23},{24..., dimensions={0} | all-to-all | bytes 786432 | tf_op jit(solution)/shard_map/all_to_all | solution.py:17
  37.4 1.3 broadcast_in_dim.57
  38.7 3.7 %all-to-all-start.2 = ((bf16[4,384,512]{2,1,0:T(8,128)(2,1)}), bf16[4,384,512]{2,1,0:T(8,128)(2,1)S(1)}, u32[]{:S(2)}, u32[]{:S(2)}) async-start(bf16[4,384,512]{2,1,0:T(8,128)(2,1)} %broadcast_in_dim.57), calls=%async_computation.2 | async-start | bytes 3145728 | tf_op jit(solution)/shard_map/all_to_all | solution.py:17
  42.4 0.0 copy-done.1
  42.4 1.0 slice.36
  43.4 0.1 slice_bitcast_fusion
  43.5 0.1 copy.18
  43.6 0.0 copy-start.8
  43.6 1.4 copy.19
  45.1 1.8 %copy.20 = bf16[512,256]{0,1:T(8,128)(2,1)} copy(bf16[512,256]{1,0:T(8,128)(2,1)} %param.7) | data formatting | bytes 524288 | tf_op args[2]
  46.9 11.8 %all-to-all-done.2 = bf16[4,384,512]{2,1,0:T(8,128)(2,1)S(1)} async-done(((bf16[4,384,512]{2,1,0:T(8,128)(2,1)}), bf16[4,384,512]{2,1,0:T(8,128)(2,1)S(1)}, u32[]{:S(2)}, u32[]{:S(2)}) %all-to-all-start.2) | async-done | bytes 1572896 | tf_op jit(solution)/shard_map/all_to_all | solution.py:17
  58.7 0.0 copy-done.8
  58.7 1.4 convolution_bitcast_fusion.part
  60.1 0.0 copy-done.3
  60.1 2.5 %all-gather.2.cloned.1.call-done.rows = bf16[2048,512]{1,0:T(8,128)(2,1)} async-done(((bf16[256,512]{1,0:T(8,128)(2,1)}), bf16[2048,512]{1,0:T(8,128)(2,1)}) %all-gather.2.cloned.1.call-update) | async-done | bytes 2097168 | tf_op jit(solution)/shard_map/all_gather | solution.py:118
  62.7 4.8 %shard_map.76 = (f32[256,512]{1,0:T(8,128)}, f32[32,4,512]{2,1,0:T(4,128)}) custom-call(bf16[256,2048]{1,0:T(8,128)(2,1)} %bitcast.68, bf16[2048,512]{1,0:T(8,128)(2,1)} %all-gather.2.cloned.1.call-done.rows, f32[256,512]{1,0:T(8,128)} %convolution_bitcast_fusion.part, bf16[256,512]{1,0:T(8,128)(2,1)} %bitcast.71, f32[1,512]{1,0:T(1,128)} %bitcast.79), custom_call_target="tpu_custom_call" | custom-call | flops 536870912 | bytes 4718592 | tf_op jit(solution)/shard_map/pallas_call | solution.py:87
  67.5 6.8 %all-to-all-start.3 = ((f32[32,4,512]{2,1,0:T(4,128)}), f32[32,4,512]{2,1,0:T(4,128)S(1)}, u32[]{:S(2)}, u32[]{:S(2)}) async-start(f32[32,4,512]{2,1,0:T(4,128)} %get-tuple-element.21), calls=%async_computation.3 | async-start | bytes 524288 | tf_op jit(solution)/shard_map/all_to_all | solution.py:137
  74.3 0.0 reduce-scatter.2.cloned.1.call-start
  74.4 3.0 %copy.23 = bf16[8,4,112,256]{3,2,1,0:T(8,128)(2,1)} copy(bf16[8,4,112,256]{3,2,0,1:T(8,128)(2,1)} %bitcast.60) | data formatting | bytes 3670016 | tf_op jit(solution)/shard_map/transpose | solution.py:126
  77.4 0.1 copy.29
  77.6 1.3 copy-done.4
  78.8 0.3 pad_maximum_fusion
  79.2 0.0 copy-start.10
  79.2 0.0 copy-start.11
  79.2 1.5 constant_dynamic-slice_fusion
  80.7 3.2 %all-to-all-done.3 = f32[32,4,512]{2,1,0:T(4,128)S(1)} async-done(((f32[32,4,512]{2,1,0:T(4,128)}), f32[32,4,512]{2,1,0:T(4,128)S(1)}, u32[]{:S(2)}, u32[]{:S(2)}) %all-to-all-start.3) | async-done | bytes 262176 | tf_op jit(solution)/shard_map/all_to_all | solution.py:137
  84.0 0.2 slice_reduce_fusion
  84.2 0.1 copy.24
  84.3 0.6 multiply_add_fusion
  84.9 0.0 copy-done.7
  84.9 0.0 copy-done.10
  84.9 0.2 multiply_convert_fusion.right
  85.1 0.4 copy-done.2
  85.5 0.7 convolution_convert_fusion
  86.1 0.0 copy-done.5
  86.2 3.8 %shard_map.77 = bf16[3584,512]{1,0:T(8,128)(2,1)} custom-call(bf16[3584,256]{1,0:T(8,128)(2,1)} %bitcast.63, bf16[256,512]{1,0:T(8,128)(2,1)} %copy-done.5), custom_call_target="tpu_custom_call" | custom-call | flops 939524096 | bytes 5767168 | tf_op jit(solution)/shard_map/pallas_call | solution.py:45
  89.9 0.0 reduce-scatter.2.cloned.1.call-update
  90.0 8.1 %collective-permute-start = (bf16[1792,256]{1,0:T(8,128)(2,1)S(1)}, bf16[1792,256]{1,0:T(8,128)(2,1)S(1)}, u32[]{:S(2)}, u32[]{:S(2)}) collective-permute-start(bf16[1792,256]{1,0:T(8,128)(2,1)S(1)} %convolution_convert_fusion), channel_id=1, source_target_pairs={{0,32},{32,0},{64,96},{96,64},{128,160},{160,128},{192,224},{224,1... | collective-permute-start | bytes 2752520 | tf_op jit(solution)/shard_map/ppermute | solution.py:159
  98.0 2.1 %collective-permute-done = bf16[1792,256]{1,0:T(8,128)(2,1)S(1)} collective-permute-done((bf16[1792,256]{1,0:T(8,128)(2,1)S(1)}, bf16[1792,256]{1,0:T(8,128)(2,1)S(1)}, u32[]{:S(2)}, u32[]{:S(2)}) %collective-permute-start) | collective-permute-done | bytes 917536 | tf_op jit(solution)/shard_map/ppermute | solution.py:159
  100.1 0.7 add_convert_fusion
  100.8 32.0 %all_to_all.32 = bf16[8,224,256]{2,1,0:T(8,128)(2,1)S(1)} all-to-all(bf16[8,224,256]{2,1,0:T(8,128)(2,1)S(1)} %bitcast.70), channel_id=1, replica_groups={{0,64,128,192,256,320,384,448},{32,96,160,224,288,352,416,480},{1,65,12..., dimensions={0} | all-to-all | bytes 1835008 | tf_op jit(solution)/shard_map/all_to_all | solution.py:17
  132.8 0.1 reduce_sum.42
  133.0 1.0 broadcast_in_dim.59
  134.0 3.6 %all-to-all-start.5 = ((bf16[8,224,256]{2,1,0:T(8,128)(2,1)}), bf16[8,224,256]{2,1,0:T(8,128)(2,1)S(1)}, u32[]{:S(2)}, u32[]{:S(2)}) async-start(bf16[8,224,256]{2,1,0:T(8,128)(2,1)} %broadcast_in_dim.59), calls=%async_computation.5 | async-start | bytes 1835008 | tf_op jit(solution)/shard_map/all_to_all | solution.py:17
  137.6 7.8 %reduce-scatter.2.cloned.1.call-done = bf16[448,512]{1,0:T(8,128)(2,1)} async-done(((bf16[3584,512]{1,0:T(8,128)(2,1)}), bf16[448,512]{1,0:T(8,128)(2,1)}) %reduce-scatter.2.cloned.1.call-update) | async-done | bytes 458768 | tf_op jit(solution)/shard_map/reduce_scatter | solution.py:162
  145.4 1.1 dynamic-slice_bitcast_fusion
  146.5 3.1 %collective-permute-start.1 = (bf16[112,512]{1,0:T(8,128)(2,1)S(1)}, bf16[112,512]{1,0:T(8,128)(2,1)S(1)}, u32[]{:S(2)}, u32[]{:S(2)}) collective-permute-start(bf16[112,512]{1,0:T(8,128)(2,1)S(1)} %get-tuple-element.41), channel_id=1, source_target_pairs={{0,8},{1,9},{2,10},{3,11},{4,12},{5,13},{6,14},{7,15},{8,16},{9,17... | collective-permute-start | bytes 344072 | tf_op jit(solution)/shard_map/ppermute | solution.py:171
  149.6 4.3 %collective-permute-start.2 = (bf16[112,512]{1,0:T(8,128)(2,1)S(1)}, bf16[112,512]{1,0:T(8,128)(2,1)S(1)}, u32[]{:S(2)}, u32[]{:S(2)}) collective-permute-start(bf16[112,512]{1,0:T(8,128)(2,1)S(1)} %get-tuple-element.40), channel_id=1, source_target_pairs={{0,16},{1,17},{2,18},{3,19},{4,20},{5,21},{6,22},{7,23},{8,24},{9,... | collective-permute-start | bytes 344072 | tf_op jit(solution)/shard_map/ppermute | solution.py:171
  153.9 3.1 %collective-permute-start.3 = (bf16[112,512]{1,0:T(8,128)(2,1)S(1)}, bf16[112,512]{1,0:T(8,128)(2,1)S(1)}, u32[]{:S(2)}, u32[]{:S(2)}) collective-permute-start(bf16[112,512]{1,0:T(8,128)(2,1)S(1)} %get-tuple-element.39), channel_id=1, source_target_pairs={{0,24},{1,25},{2,26},{3,27},{4,28},{5,29},{6,30},{7,31},{8,0},{9,1... | collective-permute-start | bytes 344072 | tf_op jit(solution)/shard_map/ppermute | solution.py:171
  157.0 6.8 %all-to-all-done.5 = bf16[8,224,256]{2,1,0:T(8,128)(2,1)S(1)} async-done(((bf16[8,224,256]{2,1,0:T(8,128)(2,1)}), bf16[8,224,256]{2,1,0:T(8,128)(2,1)S(1)}, u32[]{:S(2)}, u32[]{:S(2)}) %all-to-all-start.5) | async-done | bytes 917536 | tf_op jit(solution)/shard_map/all_to_all | solution.py:17
  163.8 0.0 collective-permute-done.1
  163.8 0.0 collective-permute-done.2
  163.8 0.0 collective-permute-done.3
  163.8 2.4 %collective-permute-start.4 = (bf16[8,224,256]{2,1,0:T(8,128)(2,1)S(1)}, bf16[8,224,256]{2,1,0:T(8,128)(2,1)S(1)}, u32[]{:S(2)}, u32[]{:S(2)}) collective-permute-start(bf16[8,224,256]{2,1,0:T(8,128)(2,1)S(1)} %all-to-all-done.5), channel_id=1, source_target_pairs={{0,32},{32,0},{64,96},{96,64},{128,160},{160,128},{192,224},{224,1... | collective-permute-start | bytes 2752520 | tf_op jit(solution)/shard_map/ppermute | solution.py:173
  166.3 0.1 iota.11
  166.3 0.1 iota.12
  166.4 0.7 fusion
  167.1 1.2 collective-permute-done.4
  168.3 1.8 %bitcast_select_fusion = bf16[3584,256]{1,0:T(8,128)(2,1)} fusion(pred[3584]{0:T(1024)(128)(4,1)S(1)} %iota.12, bf16[8,224,256]{2,1,0:T(8,128)(2,1)S(1)} %collective-permute-done.4, bf16[8,224,256]{2,1,0:T(8,128)(2,1)S(1)} %all-to-all-done.5), kind=kLoop, calls=%fused_computation.3 | loop fusion | flops 917504 | bytes 3673600 | tf_op jit(solution)/shard_map/jit(_where)/select_n | solution.py:177
  (18 shorter events, 0.1 us)
Async XLA Ops:
  7.2 55.5 %all-gather.2.cloned.1.call-start = ((), (), s32[]{:S(2)}) async-start(), calls=%async_computation.7 | async-start | bytes 2359296 | tf_op jit(solution)/shard_map/all_gather | solution.py:118
  38.7 3.7 %copy-start.1 = (bf16[3584,256]{1,0:T(8,128)(2,1)S(1)}, bf16[3584,256]{1,0:T(8,128)(2,1)}, u32[]{:S(2)}) copy-start(bf16[3584,256]{1,0:T(8,128)(2,1)} %param.6) | copy-start | bytes 5505028
  38.7 20.0 %all-to-all-start.2 = ((bf16[4,384,512]{2,1,0:T(8,128)(2,1)}), bf16[4,384,512]{2,1,0:T(8,128)(2,1)S(1)}, u32[]{:S(2)}, u32[]{:S(2)}) async-start(bf16[4,384,512]{2,1,0:T(8,128)(2,1)} %broadcast_in_dim.57), calls=%async_computation.2 | async-start | bytes 3145728 | tf_op jit(solution)/shard_map/all_to_all | solution.py:17
  43.6 15.1 %copy-start.8 = (bf16[4,8,48,256]{3,2,1,0:T(8,128)(2,1)S(1)}, bf16[4,8,48,256]{3,2,1,0:T(8,128)(2,1)}, u32[]{:S(2)}) copy-start(bf16[4,8,48,256]{3,2,1,0:T(8,128)(2,1)} %slice.36) | copy-start | bytes 2359300
  58.7 1.4 copy-start.3
  67.5 16.5 %all-to-all-start.3 = ((f32[32,4,512]{2,1,0:T(4,128)}), f32[32,4,512]{2,1,0:T(4,128)S(1)}, u32[]{:S(2)}, u32[]{:S(2)}) async-start(f32[32,4,512]{2,1,0:T(4,128)} %get-tuple-element.21), calls=%async_computation.3 | async-start | bytes 524288 | tf_op jit(solution)/shard_map/all_to_all | solution.py:137
  74.3 71.1 %reduce-scatter.2.cloned.1.call-start = ((), (), s32[]{:S(2)}) async-start(), calls=%async_computation.8 | async-start | bytes 4128768 | tf_op jit(solution)/shard_map/reduce_scatter | solution.py:162
  74.4 3.0 %copy-start = (bf16[2048,512]{1,0:T(8,128)(2,1)S(1)}, bf16[2048,512]{1,0:T(8,128)(2,1)}, u32[]{:S(2)}) copy-start(bf16[2048,512]{1,0:T(8,128)(2,1)} %all-gather.2.cloned.1.call-done.rows) | copy-start | bytes 6291460
  77.4 1.4 copy-start.4
  79.2 5.7 %copy-start.7 = (bf16[512,256]{0,1:T(8,128)(2,1)S(1)}, bf16[512,256]{0,1:T(8,128)(2,1)}, u32[]{:S(2)}) copy-start(bf16[512,256]{0,1:T(8,128)(2,1)} %copy.20) | copy-start | bytes 786436
  79.2 5.7 %copy-start.9 = (f32[256,512]{1,0:T(8,128)S(1)}, f32[256,512]{1,0:T(8,128)}, u32[]{:S(2)}) copy-start(f32[256,512]{1,0:T(8,128)} %get-tuple-element.24) | copy-start | bytes 1572868
  79.2 5.7 %copy-start.10 = (f32[512]{0:T(512)S(1)}, f32[512]{0:T(512)}, u32[]{:S(2)}) copy-start(f32[512]{0:T(512)} %param.8) | copy-start | bytes 6148
  79.2 5.7 %copy-start.11 = (f32[512]{0:T(512)S(1)}, f32[512]{0:T(512)}, u32[]{:S(2)}) copy-start(f32[512]{0:T(512)} %param.9) | copy-start | bytes 6148
  84.0 1.5 copy-start.2
  85.5 0.7 copy-start.5
  89.9 10.2 %copy-start.6 = (bf16[256,512]{1,0:T(8,128)(2,1)S(1)}, bf16[256,512]{1,0:T(8,128)(2,1)}, u32[]{:S(2)}) copy-start(bf16[256,512]{1,0:T(8,128)(2,1)} %copy-done.5) | copy-start | bytes 786436
  90.0 10.2 %collective-permute-start = (bf16[1792,256]{1,0:T(8,128)(2,1)S(1)}, bf16[1792,256]{1,0:T(8,128)(2,1)S(1)}, u32[]{:S(2)}, u32[]{:S(2)}) collective-permute-start(bf16[1792,256]{1,0:T(8,128)(2,1)S(1)} %convolution_convert_fusion), channel_id=1, source_target_pairs={{0,32},{32,0},{64,96},{96,64},{128,160},{160,128},{192,224},{224,1... | collective-permute-start | bytes 2752520 | tf_op jit(solution)/shard_map/ppermute | solution.py:159
  134.0 29.9 %all-to-all-start.5 = ((bf16[8,224,256]{2,1,0:T(8,128)(2,1)}), bf16[8,224,256]{2,1,0:T(8,128)(2,1)S(1)}, u32[]{:S(2)}, u32[]{:S(2)}) async-start(bf16[8,224,256]{2,1,0:T(8,128)(2,1)} %broadcast_in_dim.59), calls=%async_computation.5 | async-start | bytes 1835008 | tf_op jit(solution)/shard_map/all_to_all | solution.py:17
  146.5 17.3 %collective-permute-start.1 = (bf16[112,512]{1,0:T(8,128)(2,1)S(1)}, bf16[112,512]{1,0:T(8,128)(2,1)S(1)}, u32[]{:S(2)}, u32[]{:S(2)}) collective-permute-start(bf16[112,512]{1,0:T(8,128)(2,1)S(1)} %get-tuple-element.41), channel_id=1, source_target_pairs={{0,8},{1,9},{2,10},{3,11},{4,12},{5,13},{6,14},{7,15},{8,16},{9,17... | collective-permute-start | bytes 344072 | tf_op jit(solution)/shard_map/ppermute | solution.py:171
  149.6 14.3 %collective-permute-start.2 = (bf16[112,512]{1,0:T(8,128)(2,1)S(1)}, bf16[112,512]{1,0:T(8,128)(2,1)S(1)}, u32[]{:S(2)}, u32[]{:S(2)}) collective-permute-start(bf16[112,512]{1,0:T(8,128)(2,1)S(1)} %get-tuple-element.40), channel_id=1, source_target_pairs={{0,16},{1,17},{2,18},{3,19},{4,20},{5,21},{6,22},{7,23},{8,24},{9,... | collective-permute-start | bytes 344072 | tf_op jit(solution)/shard_map/ppermute | solution.py:171
  153.9 9.9 %collective-permute-start.3 = (bf16[112,512]{1,0:T(8,128)(2,1)S(1)}, bf16[112,512]{1,0:T(8,128)(2,1)S(1)}, u32[]{:S(2)}, u32[]{:S(2)}) collective-permute-start(bf16[112,512]{1,0:T(8,128)(2,1)S(1)} %get-tuple-element.39), channel_id=1, source_target_pairs={{0,24},{1,25},{2,26},{3,27},{4,28},{5,29},{6,30},{7,31},{8,0},{9,1... | collective-permute-start | bytes 344072 | tf_op jit(solution)/shard_map/ppermute | solution.py:171
  163.8 4.5 %collective-permute-start.4 = (bf16[8,224,256]{2,1,0:T(8,128)(2,1)S(1)}, bf16[8,224,256]{2,1,0:T(8,128)(2,1)S(1)}, u32[]{:S(2)}, u32[]{:S(2)}) collective-permute-start(bf16[8,224,256]{2,1,0:T(8,128)(2,1)S(1)} %all-to-all-done.5), channel_id=1, source_target_pairs={{0,32},{32,0},{64,96},{96,64},{128,160},{160,128},{192,224},{224,1... | collective-permute-start | bytes 2752520 | tf_op jit(solution)/shard_map/ppermute | solution.py:173
Sparse Core Ops, SparseCore 0:
  18.5 44.1 all-gather.1
  90.1 55.2 reduce-scatter.1

commit v9 on v7

--- a/solution.py
+++ b/solution.py
@@ -110,9 +110,8 @@
     came = lax.ppermute(given, "tok", CORE_SWAP)
 
     grad_later = lax.optimization_barrier((grad_logits, given))[0]
-    line = lax.psum_scatter(
-        product(by_y, grad_later), "voc", axis_index_groups=Y_GROUPS, scatter_dimension=0, tiled=True
-    )
+    came, terms = lax.optimization_barrier((came, product(by_y, grad_later)))
+    line = lax.psum_scatter(terms, "voc", axis_index_groups=Y_GROUPS, scatter_dimension=0, tiled=True)
     chip_terms = (contract(rows_kept, grad_logits, ((1,), (1,))) + came.astype(jnp.float32)).astype(jnp.bfloat16)
     summed = add_up(exchange(chip_terms.reshape(NZ, -1, columns), "tok", Z_GROUPS))
     own = spread(summed, "tok", Z_GROUPS)

time: 177 us -> 178 us (level)
  waiting for transfers between devices: 37 us -> 32.6 us
  starting transfers between devices: 35.1 us -> 37.2 us
    all_to_all x2, waiting for transfers between devices: 18.5 us -> 14.4 us  [exchange(): lax.all_to_all(blocks, axis, 0, 0, tiled=True, axis_index_groups=groups)]
    ppermute x1, starting transfers between devices: 2.4 us -> 4.64 us  [body(): other = lax.ppermute(own, 'tok', CORE_SWAP)]
    ppermute x1, waiting for transfers between devices: 2.08 us -> 0.01 us  [body(): came = lax.ppermute(given, 'tok', CORE_SWAP)]
    reduce_scatter x1, waiting for transfers between devices: 7.03 us -> 8.85 us  [body(): lax.psum_scatter(terms, 'voc', axis_index_groups=Y_GROUPS, scatter_dimens...]
  transfers between devices with their start and end apart: 10 -> 10, of which waited for: 7 -> 6; matrix products, arithmetic and copies ran while one was open for 9% -> 10% of each run, Pallas kernels for 0% -> 2%
where the time goes in v9:
time: 178 us; the launch traced here: 177 us
  blocking collectives  61.8 us (35%)
  starting transfers between devices  37.2 us (21%)
  waiting for transfers between devices  32.6 us (18%)
  local copies, waits for them, and re-layouts  14.6 us (8%)
  between operations  14.3 us (8%)
  matrix products  6.69 us (4%)
  other arithmetic  6 us (3%)
  Pallas kernels  3.76 us (2%)
    all_to_all x3, blocking collectives, exchange(): lax.all_to_all(blocks, axis, 0, 0, tiled=True, axis_index_groups=groups)  61.8 us
    all_to_all x2, waiting for transfers between devices, exchange(): lax.all_to_all(blocks, axis, 0, 0, tiled=True, axis_index_groups=groups)  14.4 us
    ppermute x3, starting transfers between devices, body(): lax.ppermute(blocks[k], 'voc', X_SHIFTS[k])  10.5 us
    reduce_scatter x1, waiting for transfers between devices, body(): lax.psum_scatter(terms, 'voc', axis_index_groups=Y_GROUPS, scatter_dimens...  8.85 us
    ppermute x1, starting transfers between devices, body(): came = lax.ppermute(given, 'tok', CORE_SWAP)  7.93 us
    all_to_all x2, starting transfers between devices, exchange(): lax.all_to_all(blocks, axis, 0, 0, tiled=True, axis_index_groups=groups)  7.25 us
    all_to_all x1, starting transfers between devices, body(): lax.all_to_all(jnp.broadcast_to(stats[None], (NX * NY,) + stats.shape), '...  6.84 us
    dot_general x4, matrix products, contract(): lax.dot_general(left, right, (dims, ((), ())), preferred_element_type=jnp...  6.69 us
  transfers between devices with their start and end apart: 10, of which 6 were waited for; matrix products, arithmetic and copies ran while one was open for 10% of the time, Pallas kernels for 2%

profile of v9, /device:TPU:1, one launch (start us, length us, event | category | flops | bytes accessed | tf_op | source)
XLA Modules:
  0.0 177.0 jit_solution(8419006800296759636)
XLA Ops:
  7.2 0.0 all-gather.2.cloned.1.call-start
  7.2 0.8 slice.34
  8.1 10.3 %all_to_all.30 = bf16[4,64,512]{2,1,0:T(8,128)(2,1)} all-to-all(bf16[4,64,512]{2,1,0:T(8,128)(2,1)S(1)} %broadcast_in_dim.26), channel_id=1, replica_groups={{0,8,16,24},{1,9,17,25},{2,10,18,26},{3,11,19,27},{4,12,20,28},{5,13,21..., dimensions={0} | all-to-all | bytes 524288 | tf_op jit(solution)/shard_map/all_to_all | solution.py:17
  18.4 0.0 all-gather.2.cloned.1.call-update
  18.4 0.8 slice.35
  19.2 18.2 %all_to_all.31 = bf16[8,48,512]{2,1,0:T(8,128)(2,1)S(1)} all-to-all(bf16[8,48,512]{2,1,0:T(8,128)(2,1)S(1)} %broadcast_in_dim.27), channel_id=1, replica_groups={{0,1,2,3,4,5,6,7},{8,9,10,11,12,13,14,15},{16,17,18,19,20,21,22,23},{24..., dimensions={0} | all-to-all | bytes 786432 | tf_op jit(solution)/shard_map/all_to_all | solution.py:17
  37.4 1.3 broadcast_in_dim.29
  38.7 0.0 copy-start
  38.7 3.7 %all-to-all-start.2 = ((bf16[4,384,512]{2,1,0:T(8,128)(2,1)}), bf16[4,384,512]{2,1,0:T(8,128)(2,1)S(1)}, u32[]{:S(2)}, u32[]{:S(2)}) async-start(bf16[4,384,512]{2,1,0:T(8,128)(2,1)} %broadcast_in_dim.29), calls=%async_computation.2 | async-start | bytes 3145728 | tf_op jit(solution)/shard_map/all_to_all | solution.py:17
  42.4 0.0 copy-done
  42.4 1.0 slice.36
  43.4 0.1 slice_bitcast_fusion
  43.5 1.0 copy.24
  44.6 1.8 %copy.25 = bf16[512,256]{0,1:T(8,128)(2,1)} copy(bf16[512,256]{1,0:T(8,128)(2,1)} %param.7) | data formatting | bytes 524288 | tf_op args[2]
  46.4 1.4 copy.28
  47.8 10.9 %all-to-all-done.2 = bf16[4,384,512]{2,1,0:T(8,128)(2,1)S(1)} async-done(((bf16[4,384,512]{2,1,0:T(8,128)(2,1)}), bf16[4,384,512]{2,1,0:T(8,128)(2,1)S(1)}, u32[]{:S(2)}, u32[]{:S(2)}) %all-to-all-start.2) | async-done | bytes 1572896 | tf_op jit(solution)/shard_map/all_to_all | solution.py:17
  58.7 1.8 convolution_bitcast_fusion
  60.5 2.2 %all-gather.2.cloned.1.call-done = bf16[2048,512]{1,0:T(8,128)(2,1)} async-done(((bf16[256,512]{1,0:T(8,128)(2,1)}), bf16[2048,512]{1,0:T(8,128)(2,1)}) %all-gather.2.cloned.1.call-update) | async-done | bytes 2097168 | tf_op jit(solution)/shard_map/all_gather | solution.py:70
  62.7 2.7 %fusion.6 = (f32[512]{0:T(512)S(1)}, f32[256,512]{1,0:T(8,128)S(1)}) fusion(f32[256,512]{1,0:T(8,128)S(1)} %convolution_bitcast_fusion, bf16[2048,256]{1,0:T(8,128)(2,1)} %bitcast.84, bf16[2048,512]{1,0:T(8,128)(2,1)} %all-gather.2.cloned.1.call-done), kind=kOutput, calls=%fused_computation.34 | convolution fusion | flops 537132544 | bytes 4196352 | tf_op jit(solution)/shard_map/dot_general | solution.py:36
  65.4 0.0 copy-done.4
  65.4 0.0 copy-done.5
  65.4 0.2 exponential_reduce_fusion
  65.7 0.8 broadcast_in_dim.30
  66.4 6.8 %all-to-all-start.3 = ((f32[32,4,512]{2,1,0:T(4,128)}), f32[32,4,512]{2,1,0:T(4,128)S(1)}, u32[]{:S(2)}, u32[]{:S(2)}) async-start(f32[32,4,512]{2,1,0:T(4,128)} %broadcast_in_dim.30), calls=%async_computation.3 | async-start | bytes 524288 | tf_op jit(solution)/shard_map/all_to_all | solution.py:89
  73.3 0.0 reduce-scatter.2.cloned.1.call-start
  73.3 1.8 %pad_maximum_fusion = bf16[4,8,112,512]{3,2,0,1:T(8,128)(2,1)S(1)} fusion(bf16[4,8,64,512]{3,2,0,1:T(8,128)(2,1)} %bitcast.82, bf16[4,8,48,512]{3,2,1,0:T(8,128)(2,1)S(1)} %bitcast.80), kind=kLoop, calls=%fused_computation | loop fusion | flops 7340032 | bytes 7340032 | tf_op jit(solution)/shard_map/concatenate | solution.py:90
  75.2 0.3 copy.27
  75.5 0.0 copy-start.6
  75.5 1.5 constant_dynamic-slice_fusion
  77.0 5.9 %all-to-all-done.3 = f32[32,4,512]{2,1,0:T(4,128)S(1)} async-done(((f32[32,4,512]{2,1,0:T(4,128)}), f32[32,4,512]{2,1,0:T(4,128)S(1)}, u32[]{:S(2)}, u32[]{:S(2)}) %all-to-all-start.3) | async-done | bytes 262176 | tf_op jit(solution)/shard_map/all_to_all | solution.py:89
  82.9 0.2 slice_reduce_fusion
  83.1 0.1 copy.31
  83.3 0.6 multiply_add_fusion
  83.9 0.0 copy-done.6
  83.9 0.2 multiply_convert_fusion.right
  84.1 0.4 copy-done.1
  84.4 1.6 convolution_convert_fusion
  86.0 7.9 %collective-permute-start = (bf16[1792,256]{1,0:T(8,128)(2,1)}, bf16[1792,256]{1,0:T(8,128)(2,1)S(1)}, u32[]{:S(2)}, u32[]{:S(2)}) collective-permute-start(bf16[1792,256]{1,0:T(8,128)(2,1)} %convolution_convert_fusion), channel_id=1, source_target_pairs={{0,32},{32,0},{64,96},{96,64},{128,160},{160,128},{192,224},{224,1... | collective-permute-start | bytes 2752520 | tf_op jit(solution)/shard_map/ppermute | solution.py:110
  94.0 0.0 copy-done.2
  94.0 3.8 %shard_map.76 = bf16[3584,512]{1,0:T(8,128)(2,1)} custom-call(bf16[3584,256]{1,0:T(8,128)(2,1)} %bitcast.76, bf16[256,512]{1,0:T(8,128)(2,1)} %copy-done.2), custom_call_target="tpu_custom_call" | custom-call | flops 939524096 | bytes 5767168 | tf_op jit(solution)/shard_map/pallas_call | solution.py:45
  97.7 0.0 collective-permute-done
  97.7 0.0 reduce-scatter.2.cloned.1.call-update
  97.8 0.9 copy-done.3
  98.7 0.7 fusion.7
  99.4 0.3 add_convert_fusion
  99.7 33.3 %all_to_all.32 = bf16[8,224,256]{2,1,0:T(8,128)(2,1)S(1)} all-to-all(bf16[8,224,256]{2,1,0:T(8,128)(2,1)S(1)} %bitcast.81), channel_id=1, replica_groups={{0,64,128,192,256,320,384,448},{32,96,160,224,288,352,416,480},{1,65,12..., dimensions={0} | all-to-all | bytes 1835008 | tf_op jit(solution)/shard_map/all_to_all | solution.py:17
  133.0 0.1 reduce_sum.72
  133.1 1.0 broadcast_in_dim.31
  134.1 3.6 %all-to-all-start.5 = ((bf16[8,224,256]{2,1,0:T(8,128)(2,1)}), bf16[8,224,256]{2,1,0:T(8,128)(2,1)S(1)}, u32[]{:S(2)}, u32[]{:S(2)}) async-start(bf16[8,224,256]{2,1,0:T(8,128)(2,1)} %broadcast_in_dim.31), calls=%async_computation.5 | async-start | bytes 1835008 | tf_op jit(solution)/shard_map/all_to_all | solution.py:17
  137.7 8.8 %reduce-scatter.2.cloned.1.call-done = bf16[448,512]{1,0:T(8,128)(2,1)} async-done(((bf16[3584,512]{1,0:T(8,128)(2,1)}), bf16[448,512]{1,0:T(8,128)(2,1)}) %reduce-scatter.2.cloned.1.call-update) | async-done | bytes 458768 | tf_op jit(solution)/shard_map/reduce_scatter | solution.py:114
  146.5 1.1 dynamic-slice_bitcast_fusion
  147.6 3.1 %collective-permute-start.1 = (bf16[112,512]{1,0:T(8,128)(2,1)S(1)}, bf16[112,512]{1,0:T(8,128)(2,1)S(1)}, u32[]{:S(2)}, u32[]{:S(2)}) collective-permute-start(bf16[112,512]{1,0:T(8,128)(2,1)S(1)} %get-tuple-element.40), channel_id=1, source_target_pairs={{0,8},{1,9},{2,10},{3,11},{4,12},{5,13},{6,14},{7,15},{8,16},{9,17... | collective-permute-start | bytes 344072 | tf_op jit(solution)/shard_map/ppermute | solution.py:121
  150.8 4.3 %collective-permute-start.2 = (bf16[112,512]{1,0:T(8,128)(2,1)S(1)}, bf16[112,512]{1,0:T(8,128)(2,1)S(1)}, u32[]{:S(2)}, u32[]{:S(2)}) collective-permute-start(bf16[112,512]{1,0:T(8,128)(2,1)S(1)} %get-tuple-element.39), channel_id=1, source_target_pairs={{0,16},{1,17},{2,18},{3,19},{4,20},{5,21},{6,22},{7,23},{8,24},{9,... | collective-permute-start | bytes 344072 | tf_op jit(solution)/shard_map/ppermute | solution.py:121
  155.1 3.1 %collective-permute-start.3 = (bf16[112,512]{1,0:T(8,128)(2,1)S(1)}, bf16[112,512]{1,0:T(8,128)(2,1)S(1)}, u32[]{:S(2)}, u32[]{:S(2)}) collective-permute-start(bf16[112,512]{1,0:T(8,128)(2,1)S(1)} %get-tuple-element.38), channel_id=1, source_target_pairs={{0,24},{1,25},{2,26},{3,27},{4,28},{5,29},{6,30},{7,31},{8,0},{9,1... | collective-permute-start | bytes 344072 | tf_op jit(solution)/shard_map/ppermute | solution.py:121
  158.2 3.5 %all-to-all-done.5 = bf16[8,224,256]{2,1,0:T(8,128)(2,1)S(1)} async-done(((bf16[8,224,256]{2,1,0:T(8,128)(2,1)}), bf16[8,224,256]{2,1,0:T(8,128)(2,1)S(1)}, u32[]{:S(2)}, u32[]{:S(2)}) %all-to-all-start.5) | async-done | bytes 917536 | tf_op jit(solution)/shard_map/all_to_all | solution.py:17
  161.7 0.0 collective-permute-done.1
  161.7 0.0 collective-permute-done.2
  161.7 0.0 collective-permute-done.3
  161.7 4.6 %collective-permute-start.4 = (bf16[8,224,256]{2,1,0:T(8,128)(2,1)S(1)}, bf16[8,224,256]{2,1,0:T(8,128)(2,1)S(1)}, u32[]{:S(2)}, u32[]{:S(2)}) collective-permute-start(bf16[8,224,256]{2,1,0:T(8,128)(2,1)S(1)} %all-to-all-done.5), channel_id=1, source_target_pairs={{0,32},{32,0},{64,96},{96,64},{128,160},{160,128},{192,224},{224,1... | collective-permute-start | bytes 2752520 | tf_op jit(solution)/shard_map/ppermute | solution.py:123
  166.4 0.1 iota.11
  166.4 0.1 iota.12
  166.5 0.7 fusion.3
  167.2 1.2 collective-permute-done.4
  168.4 1.8 bitcast_select_fusion
  (11 shorter events, 0.1 us)
Async XLA Ops:
  7.2 55.5 %all-gather.2.cloned.1.call-start = ((), (), s32[]{:S(2)}) async-start(), calls=%async_computation.7 | async-start | bytes 2359296 | tf_op jit(solution)/shard_map/all_gather | solution.py:70
  38.7 3.7 %copy-start = (bf16[3584,256]{1,0:T(8,128)(2,1)S(1)}, bf16[3584,256]{1,0:T(8,128)(2,1)}, u32[]{:S(2)}) copy-start(bf16[3584,256]{1,0:T(8,128)(2,1)} %param.6) | copy-start | bytes 5505028
  38.7 20.0 %all-to-all-start.2 = ((bf16[4,384,512]{2,1,0:T(8,128)(2,1)}), bf16[4,384,512]{2,1,0:T(8,128)(2,1)S(1)}, u32[]{:S(2)}, u32[]{:S(2)}) async-start(bf16[4,384,512]{2,1,0:T(8,128)(2,1)} %broadcast_in_dim.29), calls=%async_computation.2 | async-start | bytes 3145728 | tf_op jit(solution)/shard_map/all_to_all | solution.py:17
  62.7 2.7 %copy-start.4 = (bf16[512,256]{0,1:T(8,128)(2,1)S(1)}, bf16[512,256]{0,1:T(8,128)(2,1)}, u32[]{:S(2)}) copy-start(bf16[512,256]{0,1:T(8,128)(2,1)} %copy.25) | copy-start | bytes 786436
  62.7 2.7 %copy-start.5 = (f32[512]{0:T(512)S(1)}, f32[512]{0:T(512)}, u32[]{:S(2)}) copy-start(f32[512]{0:T(512)} %param.8) | copy-start | bytes 6148
  66.4 16.5 %all-to-all-start.3 = ((f32[32,4,512]{2,1,0:T(4,128)}), f32[32,4,512]{2,1,0:T(4,128)S(1)}, u32[]{:S(2)}, u32[]{:S(2)}) async-start(f32[32,4,512]{2,1,0:T(4,128)} %broadcast_in_dim.30), calls=%async_computation.3 | async-start | bytes 524288 | tf_op jit(solution)/shard_map/all_to_all | solution.py:89
  73.3 73.3 %reduce-scatter.2.cloned.1.call-start = ((), (), s32[]{:S(2)}) async-start(), calls=%async_computation.8 | async-start | bytes 4128768 | tf_op jit(solution)/shard_map/reduce_scatter | solution.py:114
  75.5 8.4 %copy-start.6 = (f32[512]{0:T(512)S(1)}, f32[512]{0:T(512)}, u32[]{:S(2)}) copy-start(f32[512]{0:T(512)} %param.9) | copy-start | bytes 6148
  82.9 1.5 copy-start.1
  84.4 9.5 %copy-start.2 = (bf16[256,512]{1,0:T(8,128)(2,1)}, bf16[256,512]{1,0:T(8,128)(2,1)S(1)}, u32[]{:S(2)}) copy-start(bf16[256,512]{1,0:T(8,128)(2,1)S(1)} %multiply_convert_fusion.right) | copy-start | bytes 786436
  86.0 11.7 %collective-permute-start = (bf16[1792,256]{1,0:T(8,128)(2,1)}, bf16[1792,256]{1,0:T(8,128)(2,1)S(1)}, u32[]{:S(2)}, u32[]{:S(2)}) collective-permute-start(bf16[1792,256]{1,0:T(8,128)(2,1)} %convolution_convert_fusion), channel_id=1, source_target_pairs={{0,32},{32,0},{64,96},{96,64},{128,160},{160,128},{192,224},{224,1... | collective-permute-start | bytes 2752520 | tf_op jit(solution)/shard_map/ppermute | solution.py:110
  97.7 0.9 copy-start.3
  134.1 27.6 %all-to-all-start.5 = ((bf16[8,224,256]{2,1,0:T(8,128)(2,1)}), bf16[8,224,256]{2,1,0:T(8,128)(2,1)S(1)}, u32[]{:S(2)}, u32[]{:S(2)}) async-start(bf16[8,224,256]{2,1,0:T(8,128)(2,1)} %broadcast_in_dim.31), calls=%async_computation.5 | async-start | bytes 1835008 | tf_op jit(solution)/shard_map/all_to_all | solution.py:17
  147.6 14.1 %collective-permute-start.1 = (bf16[112,512]{1,0:T(8,128)(2,1)S(1)}, bf16[112,512]{1,0:T(8,128)(2,1)S(1)}, u32[]{:S(2)}, u32[]{:S(2)}) collective-permute-start(bf16[112,512]{1,0:T(8,128)(2,1)S(1)} %get-tuple-element.40), channel_id=1, source_target_pairs={{0,8},{1,9},{2,10},{3,11},{4,12},{5,13},{6,14},{7,15},{8,16},{9,17... | collective-permute-start | bytes 344072 | tf_op jit(solution)/shard_map/ppermute | solution.py:121
  150.8 10.9 %collective-permute-start.2 = (bf16[112,512]{1,0:T(8,128)(2,1)S(1)}, bf16[112,512]{1,0:T(8,128)(2,1)S(1)}, u32[]{:S(2)}, u32[]{:S(2)}) collective-permute-start(bf16[112,512]{1,0:T(8,128)(2,1)S(1)} %get-tuple-element.39), channel_id=1, source_target_pairs={{0,16},{1,17},{2,18},{3,19},{4,20},{5,21},{6,22},{7,23},{8,24},{9,... | collective-permute-start | bytes 344072 | tf_op jit(solution)/shard_map/ppermute | solution.py:121
  155.1 6.6 %collective-permute-start.3 = (bf16[112,512]{1,0:T(8,128)(2,1)S(1)}, bf16[112,512]{1,0:T(8,128)(2,1)S(1)}, u32[]{:S(2)}, u32[]{:S(2)}) collective-permute-start(bf16[112,512]{1,0:T(8,128)(2,1)S(1)} %get-tuple-element.38), channel_id=1, source_target_pairs={{0,24},{1,25},{2,26},{3,27},{4,28},{5,29},{6,30},{7,31},{8,0},{9,1... | collective-permute-start | bytes 344072 | tf_op jit(solution)/shard_map/ppermute | solution.py:121
  161.7 6.7 %collective-permute-start.4 = (bf16[8,224,256]{2,1,0:T(8,128)(2,1)S(1)}, bf16[8,224,256]{2,1,0:T(8,128)(2,1)S(1)}, u32[]{:S(2)}, u32[]{:S(2)}) collective-permute-start(bf16[8,224,256]{2,1,0:T(8,128)(2,1)S(1)} %all-to-all-done.5), channel_id=1, source_target_pairs={{0,32},{32,0},{64,96},{96,64},{128,160},{160,128},{192,224},{224,1... | collective-permute-start | bytes 2752520 | tf_op jit(solution)/shard_map/ppermute | solution.py:123
Sparse Core Ops, SparseCore 0:
  18.5 44.1 all-gather.1
  97.9 48.6 reduce-scatter.1

commit v10 on v7

--- a/solution.py
+++ b/solution.py
@@ -10,7 +10,7 @@
 Z_GROUPS = [[z * NC + c for z in range(NZ)] for c in range(NC)]
 CORE_SWAP = [(z * NC + c, z * NC + 1 - c) for z in range(NZ) for c in range(NC)]
 X_SHIFTS = [[(x * NY + y, (x + k) % NX * NY + y) for x in range(NX) for y in range(NY)] for k in range(NX)]
-GATHER_B = 64
+GATHER_B = 80
 
 
 def exchange(blocks, axis, groups):

time: 177 us -> 181 us (1.023)
  waiting for transfers between devices: 37 us -> 44.8 us
    all_gather x1, waiting for transfers between devices: 2.2 us -> 21.2 us  [body(): lax.all_gather(line, 'voc', axis_index_groups=Y_GROUPS, axis=0, tiled=True)]
    all_to_all x2, waiting for transfers between devices: 18.5 us -> 7.57 us  [exchange(): lax.all_to_all(blocks, axis, 0, 0, tiled=True, axis_index_groups=groups)]
    unnamed x15 -> x21, local copies, waits for them, and re-layouts: 2.23 us -> 0.32 us
  transfers between devices with their start and end apart: 10 -> 10, of which waited for: 7 -> 6; matrix products, arithmetic and copies ran while one was open for 9% -> 9% of each run, Pallas kernels for 0% -> 0%
where the time goes in v10:
time: 181 us
  blocking collectives  58.9 us (33%)
  waiting for transfers between devices  44.8 us (25%)
  starting transfers between devices  34.2 us (19%)
  between operations  14.4 us (8%)
  local copies, waits for them, and re-layouts  12.5 us (7%)
  other arithmetic  7.12 us (4%)
  matrix products  4.88 us (3%)
  Pallas kernels  3.77 us (2%)
    all_to_all x3, blocking collectives, exchange(): lax.all_to_all(blocks, axis, 0, 0, tiled=True, axis_index_groups=groups)  58.9 us
    all_gather x1, waiting for transfers between devices, body(): lax.all_gather(line, 'voc', axis_index_groups=Y_GROUPS, axis=0, tiled=True)  21.2 us
    ppermute x3, starting transfers between devices, body(): lax.ppermute(blocks[k], 'voc', X_SHIFTS[k])  10.5 us
    all_to_all x2, waiting for transfers between devices, exchange(): lax.all_to_all(blocks, axis, 0, 0, tiled=True, axis_index_groups=groups)  7.57 us
    ppermute x1, starting transfers between devices, body(): came = lax.ppermute(given, 'tok', CORE_SWAP)  7.16 us
    all_to_all x2, starting transfers between devices, exchange(): lax.all_to_all(blocks, axis, 0, 0, tiled=True, axis_index_groups=groups)  7.07 us
    reduce_scatter x1, waiting for transfers between devices, body(): lax.psum_scatter(product(by_y, grad_later), 'voc', axis_index_groups=Y_GR...  7.05 us
    all_to_all x1, starting transfers between devices, body(): lax.all_to_all(jnp.broadcast_to(stats[None], (NX * NY,) + stats.shape), '...  7.01 us
  transfers between devices with their start and end apart: 10, of which 6 were waited for; matrix products, arithmetic and copies ran while one was open for 9% of the time, Pallas kernels for 0%

profile of v10, /device:TPU:1, one launch (start us, length us, event | category | flops | bytes accessed | tf_op | source)
XLA Modules:
  0.0 180.6 jit_solution(5002126493650171388)
XLA Ops:
  7.2 0.0 all-gather.2.cloned.1.call-start
  7.2 0.9 slice.34
  8.1 10.6 %all_to_all.30 = bf16[4,80,512]{2,1,0:T(8,128)(2,1)} all-to-all(bf16[4,80,512]{2,1,0:T(8,128)(2,1)S(1)} %broadcast_in_dim.26), channel_id=1, replica_groups={{0,8,16,24},{1,9,17,25},{2,10,18,26},{3,11,19,27},{4,12,20,28},{5,13,21..., dimensions={0} | all-to-all | bytes 655360 | tf_op jit(solution)/shard_map/all_to_all | solution.py:17
  18.8 0.0 all-gather.2.cloned.1.call-update
  18.8 0.8 slice.35
  19.6 16.3 %all_to_all.31 = bf16[8,32,512]{2,1,0:T(8,128)(2,1)S(1)} all-to-all(bf16[8,32,512]{2,1,0:T(8,128)(2,1)S(1)} %broadcast_in_dim.27), channel_id=1, replica_groups={{0,1,2,3,4,5,6,7},{8,9,10,11,12,13,14,15},{16,17,18,19,20,21,22,23},{24..., dimensions={0} | all-to-all | bytes 524288 | tf_op jit(solution)/shard_map/all_to_all | solution.py:17
  35.9 1.1 broadcast_in_dim.29
  37.0 3.5 %all-to-all-start.2 = ((bf16[4,256,512]{2,1,0:T(8,128)(2,1)}), bf16[4,256,512]{2,1,0:T(8,128)(2,1)S(1)}, u32[]{:S(2)}, u32[]{:S(2)}) async-start(bf16[4,256,512]{2,1,0:T(8,128)(2,1)} %broadcast_in_dim.29), calls=%async_computation.2 | async-start | bytes 2097152 | tf_op jit(solution)/shard_map/all_to_all | solution.py:17
  40.5 0.0 copy-done
  40.5 0.9 slice.36
  41.4 0.1 slice_bitcast_fusion
  41.5 0.0 copy-start.7
  41.5 1.2 copy.24
  42.7 0.0 copy-done.7
  42.7 0.1 copy.25
  42.8 1.4 copy.28
  44.2 21.2 %all-gather.2.cloned.1.call-done = bf16[2560,512]{1,0:T(8,128)(2,1)} async-done(((bf16[320,512]{1,0:T(8,128)(2,1)}), bf16[2560,512]{1,0:T(8,128)(2,1)}) %all-gather.2.cloned.1.call-update) | async-done | bytes 2621456 | tf_op jit(solution)/shard_map/all_gather | solution.py:70
  65.4 3.0 %fusion.8 = f32[256,512]{1,0:T(8,128)S(1)} fusion(bf16[2560,256]{1,0:T(8,128)(2,1)} %bitcast.86, bf16[2560,512]{1,0:T(8,128)(2,1)} %all-gather.2.cloned.1.call-done), kind=kOutput, calls=%fused_computation.35 | convolution fusion | flops 671088640 | bytes 4456448 | tf_op jit(solution)/shard_map/dot_general | solution.py:36
  68.4 0.0 copy-start.8
  68.4 0.0 all-to-all-done.2
  68.5 0.5 fusion.7
  69.0 0.1 copy-done.8
  69.1 0.2 exponential_reduce_fusion
  69.4 0.8 broadcast_in_dim.30
  70.1 7.0 %all-to-all-start.3 = ((f32[32,4,512]{2,1,0:T(4,128)}), f32[32,4,512]{2,1,0:T(4,128)}, u32[]{:S(2)}, u32[]{:S(2)}) async-start(f32[32,4,512]{2,1,0:T(4,128)} %broadcast_in_dim.30), calls=%async_computation.3 | async-start | bytes 524288 | tf_op jit(solution)/shard_map/all_to_all | solution.py:89
  77.1 0.0 reduce-scatter.2.cloned.1.call-start
  77.2 2.0 %pad_maximum_fusion = bf16[4,8,112,512]{3,2,0,1:T(8,128)(2,1)S(1)} fusion(bf16[4,8,80,512]{3,2,0,1:T(8,128)(2,1)} %bitcast.84, bf16[4,8,32,512]{3,2,1,0:T(8,128)(2,1)S(1)} %bitcast.76), kind=kLoop, calls=%fused_computation | loop fusion | flops 7340032 | bytes 7340032 | tf_op jit(solution)/shard_map/concatenate | solution.py:90
  79.2 0.3 copy.27
  79.5 0.0 copy-start.5
  79.5 0.0 copy-start.9
  79.5 1.5 constant_dynamic-slice_fusion
  81.0 5.7 %all-to-all-done.3 = f32[32,4,512]{2,1,0:T(4,128)} async-done(((f32[32,4,512]{2,1,0:T(4,128)}), f32[32,4,512]{2,1,0:T(4,128)}, u32[]{:S(2)}, u32[]{:S(2)}) %all-to-all-start.3) | async-done | bytes 262176 | tf_op jit(solution)/shard_map/all_to_all | solution.py:89
  86.8 1.4 slice_reduce_fusion
  88.2 1.0 copy.31
  89.3 0.6 multiply_add_fusion
  89.9 0.0 copy-done.9
  89.9 0.2 multiply_convert_fusion.right
  90.1 0.0 copy-done.1
  90.1 0.7 convolution_convert_fusion
  90.8 0.0 copy-done.2
  90.8 3.8 %shard_map.76 = bf16[3584,512]{1,0:T(8,128)(2,1)} custom-call(bf16[3584,256]{1,0:T(8,128)(2,1)} %bitcast.80, bf16[256,512]{1,0:T(8,128)(2,1)} %copy-done.2), custom_call_target="tpu_custom_call" | custom-call | flops 939524096 | bytes 5767168 | tf_op jit(solution)/shard_map/pallas_call | solution.py:45
  94.6 0.0 reduce-scatter.2.cloned.1.call-update
  94.6 7.2 %collective-permute-start = (bf16[1792,256]{1,0:T(8,128)(2,1)S(1)}, bf16[1792,256]{1,0:T(8,128)(2,1)S(1)}, u32[]{:S(2)}, u32[]{:S(2)}) collective-permute-start(bf16[1792,256]{1,0:T(8,128)(2,1)S(1)} %convolution_convert_fusion), channel_id=1, source_target_pairs={{0,32},{32,0},{64,96},{96,64},{128,160},{160,128},{192,224},{224,1... | collective-permute-start | bytes 2752520 | tf_op jit(solution)/shard_map/ppermute | solution.py:110
  101.8 2.1 %collective-permute-done = bf16[1792,256]{1,0:T(8,128)(2,1)S(1)} collective-permute-done((bf16[1792,256]{1,0:T(8,128)(2,1)S(1)}, bf16[1792,256]{1,0:T(8,128)(2,1)S(1)}, u32[]{:S(2)}, u32[]{:S(2)}) %collective-permute-start) | collective-permute-done | bytes 917536 | tf_op jit(solution)/shard_map/ppermute | solution.py:110
  103.9 0.7 add_convert_fusion
  104.5 31.9 %all_to_all.32 = bf16[8,224,256]{2,1,0:T(8,128)(2,1)S(1)} all-to-all(bf16[8,224,256]{2,1,0:T(8,128)(2,1)S(1)} %bitcast.83), channel_id=1, replica_groups={{0,64,128,192,256,320,384,448},{32,96,160,224,288,352,416,480},{1,65,12..., dimensions={0} | all-to-all | bytes 1835008 | tf_op jit(solution)/shard_map/all_to_all | solution.py:17
  136.5 0.1 reduce_sum.72
  136.6 1.0 broadcast_in_dim.31
  137.6 3.6 %all-to-all-start.5 = ((bf16[8,224,256]{2,1,0:T(8,128)(2,1)}), bf16[8,224,256]{2,1,0:T(8,128)(2,1)S(1)}, u32[]{:S(2)}, u32[]{:S(2)}) async-start(bf16[8,224,256]{2,1,0:T(8,128)(2,1)} %broadcast_in_dim.31), calls=%async_computation.5 | async-start | bytes 1835008 | tf_op jit(solution)/shard_map/all_to_all | solution.py:17
  141.2 7.0 %reduce-scatter.2.cloned.1.call-done = bf16[448,512]{1,0:T(8,128)(2,1)} async-done(((bf16[3584,512]{1,0:T(8,128)(2,1)}), bf16[448,512]{1,0:T(8,128)(2,1)}) %reduce-scatter.2.cloned.1.call-update) | async-done | bytes 458768 | tf_op jit(solution)/shard_map/reduce_scatter | solution.py:113
  148.3 1.1 dynamic-slice_bitcast_fusion
  149.4 3.1 %collective-permute-start.1 = (bf16[112,512]{1,0:T(8,128)(2,1)S(1)}, bf16[112,512]{1,0:T(8,128)(2,1)S(1)}, u32[]{:S(2)}, u32[]{:S(2)}) collective-permute-start(bf16[112,512]{1,0:T(8,128)(2,1)S(1)} %get-tuple-element.36), channel_id=1, source_target_pairs={{0,8},{1,9},{2,10},{3,11},{4,12},{5,13},{6,14},{7,15},{8,16},{9,17... | collective-permute-start | bytes 344072 | tf_op jit(solution)/shard_map/ppermute | solution.py:122
  152.5 4.3 %collective-permute-start.2 = (bf16[112,512]{1,0:T(8,128)(2,1)S(1)}, bf16[112,512]{1,0:T(8,128)(2,1)S(1)}, u32[]{:S(2)}, u32[]{:S(2)}) collective-permute-start(bf16[112,512]{1,0:T(8,128)(2,1)S(1)} %get-tuple-element.35), channel_id=1, source_target_pairs={{0,16},{1,17},{2,18},{3,19},{4,20},{5,21},{6,22},{7,23},{8,24},{9,... | collective-permute-start | bytes 344072 | tf_op jit(solution)/shard_map/ppermute | solution.py:122
  156.8 3.1 %collective-permute-start.3 = (bf16[112,512]{1,0:T(8,128)(2,1)S(1)}, bf16[112,512]{1,0:T(8,128)(2,1)S(1)}, u32[]{:S(2)}, u32[]{:S(2)}) collective-permute-start(bf16[112,512]{1,0:T(8,128)(2,1)S(1)} %get-tuple-element.34), channel_id=1, source_target_pairs={{0,24},{1,25},{2,26},{3,27},{4,28},{5,29},{6,30},{7,31},{8,0},{9,1... | collective-permute-start | bytes 344072 | tf_op jit(solution)/shard_map/ppermute | solution.py:122
  159.9 7.6 %all-to-all-done.5 = bf16[8,224,256]{2,1,0:T(8,128)(2,1)S(1)} async-done(((bf16[8,224,256]{2,1,0:T(8,128)(2,1)}), bf16[8,224,256]{2,1,0:T(8,128)(2,1)S(1)}, u32[]{:S(2)}, u32[]{:S(2)}) %all-to-all-start.5) | async-done | bytes 917536 | tf_op jit(solution)/shard_map/all_to_all | solution.py:17
  167.4 0.0 collective-permute-done.1
  167.4 0.0 collective-permute-done.2
  167.5 0.0 collective-permute-done.3
  167.5 2.4 %collective-permute-start.4 = (bf16[8,224,256]{2,1,0:T(8,128)(2,1)S(1)}, bf16[8,224,256]{2,1,0:T(8,128)(2,1)S(1)}, u32[]{:S(2)}, u32[]{:S(2)}) collective-permute-start(bf16[8,224,256]{2,1,0:T(8,128)(2,1)S(1)} %all-to-all-done.5), channel_id=1, source_target_pairs={{0,32},{32,0},{64,96},{96,64},{128,160},{160,128},{192,224},{224,1... | collective-permute-start | bytes 2752520 | tf_op jit(solution)/shard_map/ppermute | solution.py:124
  169.9 0.1 iota.11
  170.0 0.1 iota.12
  170.1 0.7 fusion.4
  170.8 1.2 collective-permute-done.4
  171.9 1.8 bitcast_select_fusion
  (16 shorter events, 0.1 us)
Async XLA Ops:
  7.2 58.2 %all-gather.2.cloned.1.call-start = ((), (), s32[]{:S(2)}) async-start(), calls=%async_computation.7 | async-start | bytes 2949120 | tf_op jit(solution)/shard_map/all_gather | solution.py:70
  35.9 4.6 %copy-start = (bf16[3584,256]{1,0:T(8,128)(2,1)S(1)}, bf16[3584,256]{1,0:T(8,128)(2,1)}, u32[]{:S(2)}) copy-start(bf16[3584,256]{1,0:T(8,128)(2,1)} %param.6) | copy-start | bytes 5505028
  37.0 31.5 %all-to-all-start.2 = ((bf16[4,256,512]{2,1,0:T(8,128)(2,1)}), bf16[4,256,512]{2,1,0:T(8,128)(2,1)S(1)}, u32[]{:S(2)}, u32[]{:S(2)}) async-start(bf16[4,256,512]{2,1,0:T(8,128)(2,1)} %broadcast_in_dim.29), calls=%async_computation.2 | async-start | bytes 2097152 | tf_op jit(solution)/shard_map/all_to_all | solution.py:17
  41.5 1.2 copy-start.7
  42.8 26.2 %copy-start.4 = (bf16[512,256]{0,1:T(8,128)(2,1)}, bf16[512,256]{0,1:T(8,128)(2,1)S(1)}, u32[]{:S(2)}) copy-start(bf16[512,256]{0,1:T(8,128)(2,1)S(1)} %copy.25) | copy-start | bytes 786436
  65.4 3.1 %copy-start.6 = (bf16[4,8,32,256]{3,2,1,0:T(8,128)(2,1)S(1)}, bf16[4,8,32,256]{3,2,1,0:T(8,128)(2,1)}, u32[]{:S(2)}) copy-start(bf16[4,8,32,256]{3,2,1,0:T(8,128)(2,1)} %slice.36) | copy-start | bytes 1572868
  68.4 0.7 copy-start.8
  70.1 16.6 %all-to-all-start.3 = ((f32[32,4,512]{2,1,0:T(4,128)}), f32[32,4,512]{2,1,0:T(4,128)}, u32[]{:S(2)}, u32[]{:S(2)}) async-start(f32[32,4,512]{2,1,0:T(4,128)} %broadcast_in_dim.30), calls=%async_computation.3 | async-start | bytes 524288 | tf_op jit(solution)/shard_map/all_to_all | solution.py:89
  77.1 71.1 %reduce-scatter.2.cloned.1.call-start = ((), (), s32[]{:S(2)}) async-start(), calls=%async_computation.8 | async-start | bytes 4128768 | tf_op jit(solution)/shard_map/reduce_scatter | solution.py:113
  79.5 10.4 %copy-start.5 = (bf16[512,256]{0,1:T(8,128)(2,1)S(1)}, bf16[512,256]{0,1:T(8,128)(2,1)}, u32[]{:S(2)}) copy-start(bf16[512,256]{0,1:T(8,128)(2,1)} %copy-done.4) | copy-start | bytes 786436
  79.5 10.4 %copy-start.9 = (f32[512]{0:T(512)S(1)}, f32[512]{0:T(512)}, u32[]{:S(2)}) copy-start(f32[512]{0:T(512)} %param.9) | copy-start | bytes 6148
  86.8 3.3 %copy-start.1 = (bf16[8,1,224,512]{3,2,1,0:T(8,128)(2,1)S(1)}, bf16[8,1,224,512]{3,2,1,0:T(8,128)(2,1)}, u32[]{:S(2)}) copy-start(bf16[8,1,224,512]{3,2,1,0:T(8,128)(2,1)} %get-tuple-element.32) | copy-start | bytes 5505028
  90.1 0.7 copy-start.2
  94.6 9.3 %copy-start.3 = (bf16[256,512]{1,0:T(8,128)(2,1)S(1)}, bf16[256,512]{1,0:T(8,128)(2,1)}, u32[]{:S(2)}) copy-start(bf16[256,512]{1,0:T(8,128)(2,1)} %copy-done.2) | copy-start | bytes 786436
  94.6 9.2 %collective-permute-start = (bf16[1792,256]{1,0:T(8,128)(2,1)S(1)}, bf16[1792,256]{1,0:T(8,128)(2,1)S(1)}, u32[]{:S(2)}, u32[]{:S(2)}) collective-permute-start(bf16[1792,256]{1,0:T(8,128)(2,1)S(1)} %convolution_convert_fusion), channel_id=1, source_target_pairs={{0,32},{32,0},{64,96},{96,64},{128,160},{160,128},{192,224},{224,1... | collective-permute-start | bytes 2752520 | tf_op jit(solution)/shard_map/ppermute | solution.py:110
  137.6 29.9 %all-to-all-start.5 = ((bf16[8,224,256]{2,1,0:T(8,128)(2,1)}), bf16[8,224,256]{2,1,0:T(8,128)(2,1)S(1)}, u32[]{:S(2)}, u32[]{:S(2)}) async-start(bf16[8,224,256]{2,1,0:T(8,128)(2,1)} %broadcast_in_dim.31), calls=%async_computation.5 | async-start | bytes 1835008 | tf_op jit(solution)/shard_map/all_to_all | solution.py:17
  149.4 18.1 %collective-permute-start.1 = (bf16[112,512]{1,0:T(8,128)(2,1)S(1)}, bf16[112,512]{1,0:T(8,128)(2,1)S(1)}, u32[]{:S(2)}, u32[]{:S(2)}) collective-permute-start(bf16[112,512]{1,0:T(8,128)(2,1)S(1)} %get-tuple-element.36), channel_id=1, source_target_pairs={{0,8},{1,9},{2,10},{3,11},{4,12},{5,13},{6,14},{7,15},{8,16},{9,17... | collective-permute-start | bytes 344072 | tf_op jit(solution)/shard_map/ppermute | solution.py:122
  152.5 15.0 %collective-permute-start.2 = (bf16[112,512]{1,0:T(8,128)(2,1)S(1)}, bf16[112,512]{1,0:T(8,128)(2,1)S(1)}, u32[]{:S(2)}, u32[]{:S(2)}) collective-permute-start(bf16[112,512]{1,0:T(8,128)(2,1)S(1)} %get-tuple-element.35), channel_id=1, source_target_pairs={{0,16},{1,17},{2,18},{3,19},{4,20},{5,21},{6,22},{7,23},{8,24},{9,... | collective-permute-start | bytes 344072 | tf_op jit(solution)/shard_map/ppermute | solution.py:122
  156.8 10.7 %collective-permute-start.3 = (bf16[112,512]{1,0:T(8,128)(2,1)S(1)}, bf16[112,512]{1,0:T(8,128)(2,1)S(1)}, u32[]{:S(2)}, u32[]{:S(2)}) collective-permute-start(bf16[112,512]{1,0:T(8,128)(2,1)S(1)} %get-tuple-element.34), channel_id=1, source_target_pairs={{0,24},{1,25},{2,26},{3,27},{4,28},{5,29},{6,30},{7,31},{8,0},{9,1... | collective-permute-start | bytes 344072 | tf_op jit(solution)/shard_map/ppermute | solution.py:122
  167.5 4.5 %collective-permute-start.4 = (bf16[8,224,256]{2,1,0:T(8,128)(2,1)S(1)}, bf16[8,224,256]{2,1,0:T(8,128)(2,1)S(1)}, u32[]{:S(2)}, u32[]{:S(2)}) collective-permute-start(bf16[8,224,256]{2,1,0:T(8,128)(2,1)S(1)} %all-to-all-done.5), channel_id=1, source_target_pairs={{0,32},{32,0},{64,96},{96,64},{128,160},{160,128},{192,224},{224,1... | collective-permute-start | bytes 2752520 | tf_op jit(solution)/shard_map/ppermute | solution.py:124
Sparse Core Ops, SparseCore 0:
  18.9 46.4 all-gather.1
  94.7 53.4 reduce-scatter.1

commit v11 on v10

--- a/solution.py
+++ b/solution.py
@@ -10,7 +10,7 @@
 Z_GROUPS = [[z * NC + c for z in range(NZ)] for c in range(NC)]
 CORE_SWAP = [(z * NC + c, z * NC + 1 - c) for z in range(NZ) for c in range(NC)]
 X_SHIFTS = [[(x * NY + y, (x + k) % NX * NY + y) for x in range(NX) for y in range(NY)] for k in range(NX)]
-GATHER_B = 80
+GATHER_B = 56
 
 
 def exchange(blocks, axis, groups):

time: 181 us -> 179 us (0.989)
  waiting for transfers between devices: 44.8 us -> 37 us
  blocking collectives: 58.9 us -> 61.7 us
  local copies, waits for them, and re-layouts: 12.5 us -> 15.3 us
    all_gather x1, waiting for transfers between devices: 21.2 us -> 12.9 us  [body(): lax.all_gather(line, 'voc', axis_index_groups=Y_GROUPS, axis=0, tiled=True)]
    all_to_all x3, blocking collectives: 58.9 us -> 61.7 us  [exchange(): lax.all_to_all(blocks, axis, 0, 0, tiled=True, axis_index_groups=groups)]
    unnamed x21 -> x17, local copies, waits for them, and re-layouts: 0.32 us -> 2.66 us
where the time goes in v11:
time: 179 us; the launch traced here: 178 us
  blocking collectives  61.7 us (34%)
  waiting for transfers between devices  37 us (21%)
  starting transfers between devices  34.6 us (19%)
  local copies, waits for them, and re-layouts  15.3 us (9%)
  between operations  14.3 us (8%)
  matrix products  6.05 us (3%)
  other arithmetic  5.52 us (3%)
  Pallas kernels  3.75 us (2%)
    all_to_all x3, blocking collectives, exchange(): lax.all_to_all(blocks, axis, 0, 0, tiled=True, axis_index_groups=groups)  61.7 us
    all_gather x1, waiting for transfers between devices, body(): lax.all_gather(line, 'voc', axis_index_groups=Y_GROUPS, axis=0, tiled=True)  12.9 us
    ppermute x3, starting transfers between devices, body(): lax.ppermute(blocks[k], 'voc', X_SHIFTS[k])  10.5 us
    ppermute x1, starting transfers between devices, body(): came = lax.ppermute(given, 'tok', CORE_SWAP)  8.49 us
    all_to_all x2, waiting for transfers between devices, exchange(): lax.all_to_all(blocks, axis, 0, 0, tiled=True, axis_index_groups=groups)  7.5 us
    all_to_all x2, starting transfers between devices, exchange(): lax.all_to_all(blocks, axis, 0, 0, tiled=True, axis_index_groups=groups)  7.14 us
    reduce_scatter x1, waiting for transfers between devices, body(): lax.psum_scatter(product(by_y, grad_later), 'voc', axis_index_groups=Y_GR...  7.11 us
    all_to_all x1, waiting for transfers between devices, body(): lax.all_to_all(jnp.broadcast_to(stats[None], (NX * NY,) + stats.shape), '...  6.12 us
  transfers between devices with their start and end apart: 10, of which 6 were waited for; matrix products, arithmetic and copies ran while one was open for 9% of the time, Pallas kernels for 0%

profile of v11, /device:TPU:1, one launch (start us, length us, event | category | flops | bytes accessed | tf_op | source)
XLA Modules:
  0.0 178.3 jit_solution(621227588889830917)
XLA Ops:
  7.2 0.0 all-gather.2.cloned.1.call-start
  7.2 0.9 fusion.8
  8.1 10.1 %all_to_all.30 = bf16[4,56,512]{2,1,0:T(8,128)(2,1)} all-to-all(bf16[4,56,512]{2,1,0:T(8,128)(2,1)S(1)} %broadcast_in_dim.26), channel_id=1, replica_groups={{0,8,16,24},{1,9,17,25},{2,10,18,26},{3,11,19,27},{4,12,20,28},{5,13,21..., dimensions={0} | all-to-all | bytes 458752 | tf_op jit(solution)/shard_map/all_to_all | solution.py:17
  18.2 0.0 all-gather.2.cloned.1.call-update
  18.3 19.4 %all_to_all.31 = bf16[8,56,512]{2,1,0:T(8,128)(2,1)S(1)} all-to-all(bf16[8,56,512]{2,1,0:T(8,128)(2,1)S(1)} %broadcast_in_dim.27), channel_id=1, replica_groups={{0,1,2,3,4,5,6,7},{8,9,10,11,12,13,14,15},{16,17,18,19,20,21,22,23},{24..., dimensions={0} | all-to-all | bytes 917504 | tf_op jit(solution)/shard_map/all_to_all | solution.py:17
  37.7 1.4 broadcast_in_dim.29
  39.0 3.6 %all-to-all-start.2 = ((bf16[4,448,512]{2,1,0:T(8,128)(2,1)}), bf16[4,448,512]{2,1,0:T(8,128)(2,1)S(1)}, u32[]{:S(2)}, u32[]{:S(2)}) async-start(bf16[4,448,512]{2,1,0:T(8,128)(2,1)} %broadcast_in_dim.29), calls=%async_computation.2 | async-start | bytes 3670016 | tf_op jit(solution)/shard_map/all_to_all | solution.py:17
  42.6 2.5 %fusion.7 = (bf16[4,8,56,256]{3,2,1,0:T(8,128)(2,1)}, bf16[8,4,56,256]{3,2,0,1:T(8,128)(2,1)S(1)}) fusion(bf16[4,8,112,256]{3,2,1,0:T(8,128)(2,1)} %bitcast.78), kind=kLoop, calls=%fused_computation.34 | loop fusion | bytes 3670016 | tf_op jit(solution)/shard_map/slice | solution.py:77
  45.2 0.0 copy-start.5
  45.2 0.1 copy.24
  45.2 0.9 copy-done.5
  46.1 0.1 copy.25
  46.3 2.9 %copy.28 = bf16[8,4,112,256]{3,2,1,0:T(8,128)(2,1)} copy(bf16[8,4,112,256]{3,2,0,1:T(8,128)(2,1)} %bitcast.79) | data formatting | bytes 3670016 | tf_op jit(solution)/shard_map/transpose | solution.py:78
  49.2 12.9 %all-gather.2.cloned.1.call-done = bf16[1792,512]{1,0:T(8,128)(2,1)} async-done(((bf16[224,512]{1,0:T(8,128)(2,1)}), bf16[1792,512]{1,0:T(8,128)(2,1)}) %all-gather.2.cloned.1.call-update) | async-done | bytes 1835024 | tf_op jit(solution)/shard_map/all_gather | solution.py:70
  62.1 2.1 %fusion.10 = f32[256,512]{1,0:T(8,128)S(1)} fusion(bf16[1792,256]{1,0:T(8,128)(2,1)S(1)} %bitcast.83, bf16[1792,512]{1,0:T(8,128)(2,1)} %all-gather.2.cloned.1.call-done), kind=kOutput, calls=%fused_computation.37 | convolution fusion | flops 469762048 | bytes 3276800 | tf_op jit(solution)/shard_map/dot_general | solution.py:36
  64.3 0.0 all-to-all-done.2
  64.3 0.0 copy-start.1
  64.3 1.2 copy-done.1
  65.5 0.0 copy-start.6
  65.5 2.6 %fusion.9 = (f32[512]{0:T(512)S(1)}, f32[256,512]{1,0:T(8,128)S(1)}) fusion(f32[256,512]{1,0:T(8,128)S(1)} %fusion.10, bf16[1792,512]{1,0:T(8,128)(2,1)} %bitcast.76, bf16[1792,256]{1,0:T(8,128)(2,1)} %bitcast.86), kind=kOutput, calls=%fused_computation.36 | convolution fusion | flops 470023680 | bytes 3803136 | tf_op jit(solution)/shard_map/dot_general | solution.py:36
  68.1 0.0 copy-done.6
  68.1 0.2 exponential_reduce_fusion
  68.4 0.7 broadcast_in_dim.30
  69.1 6.0 %all-to-all-start.3 = ((f32[32,4,512]{2,1,0:T(4,128)}), f32[32,4,512]{2,1,0:T(4,128)S(1)}, u32[]{:S(2)}, u32[]{:S(2)}) async-start(f32[32,4,512]{2,1,0:T(4,128)} %broadcast_in_dim.30), calls=%async_computation.3 | async-start | bytes 524288 | tf_op jit(solution)/shard_map/all_to_all | solution.py:89
  75.1 0.0 reduce-scatter.2.cloned.1.call-start
  75.1 0.0 copy-done
  75.1 1.7 pad_maximum_fusion
  76.8 0.3 copy.27
  77.1 0.0 copy-start.7
  77.1 1.5 constant_dynamic-slice_fusion
  78.6 6.1 %all-to-all-done.3 = f32[32,4,512]{2,1,0:T(4,128)S(1)} async-done(((f32[32,4,512]{2,1,0:T(4,128)}), f32[32,4,512]{2,1,0:T(4,128)S(1)}, u32[]{:S(2)}, u32[]{:S(2)}) %all-to-all-start.3) | async-done | bytes 262176 | tf_op jit(solution)/shard_map/all_to_all | solution.py:89
  84.7 0.2 slice_reduce_fusion
  84.9 0.1 copy.31
  85.1 0.6 multiply_add_fusion
  85.7 0.0 copy-done.7
  85.7 0.2 multiply_convert_fusion.right
  85.9 0.4 copy-done.2
  86.2 0.7 convolution_convert_fusion
  86.9 0.0 copy-done.3
  87.0 3.8 %shard_map.76 = bf16[3584,512]{1,0:T(8,128)(2,1)} custom-call(bf16[3584,256]{1,0:T(8,128)(2,1)} %bitcast.80, bf16[256,512]{1,0:T(8,128)(2,1)} %copy-done.3), custom_call_target="tpu_custom_call" | custom-call | flops 939524096 | bytes 5767168 | tf_op jit(solution)/shard_map/pallas_call | solution.py:45
  90.7 0.0 reduce-scatter.2.cloned.1.call-update
  90.7 8.5 %collective-permute-start = (bf16[1792,256]{1,0:T(8,128)(2,1)S(1)}, bf16[1792,256]{1,0:T(8,128)(2,1)S(1)}, u32[]{:S(2)}, u32[]{:S(2)}) collective-permute-start(bf16[1792,256]{1,0:T(8,128)(2,1)S(1)} %convolution_convert_fusion), channel_id=1, source_target_pairs={{0,32},{32,0},{64,96},{96,64},{128,160},{160,128},{192,224},{224,1... | collective-permute-start | bytes 2752520 | tf_op jit(solution)/shard_map/ppermute | solution.py:110
  99.2 2.1 %collective-permute-done = bf16[1792,256]{1,0:T(8,128)(2,1)S(1)} collective-permute-done((bf16[1792,256]{1,0:T(8,128)(2,1)S(1)}, bf16[1792,256]{1,0:T(8,128)(2,1)S(1)}, u32[]{:S(2)}, u32[]{:S(2)}) %collective-permute-start) | collective-permute-done | bytes 917536 | tf_op jit(solution)/shard_map/ppermute | solution.py:110
  101.3 0.0 copy-done.4
  101.3 0.7 add_convert_fusion
  102.0 32.2 %all_to_all.32 = bf16[8,224,256]{2,1,0:T(8,128)(2,1)S(1)} all-to-all(bf16[8,224,256]{2,1,0:T(8,128)(2,1)S(1)} %bitcast.84), channel_id=1, replica_groups={{0,64,128,192,256,320,384,448},{32,96,160,224,288,352,416,480},{1,65,12..., dimensions={0} | all-to-all | bytes 1835008 | tf_op jit(solution)/shard_map/all_to_all | solution.py:17
  134.2 0.1 reduce_sum.72
  134.4 1.0 broadcast_in_dim.31
  135.3 3.6 %all-to-all-start.5 = ((bf16[8,224,256]{2,1,0:T(8,128)(2,1)}), bf16[8,224,256]{2,1,0:T(8,128)(2,1)S(1)}, u32[]{:S(2)}, u32[]{:S(2)}) async-start(bf16[8,224,256]{2,1,0:T(8,128)(2,1)} %broadcast_in_dim.31), calls=%async_computation.5 | async-start | bytes 1835008 | tf_op jit(solution)/shard_map/all_to_all | solution.py:17
  139.0 7.1 %reduce-scatter.2.cloned.1.call-done = bf16[448,512]{1,0:T(8,128)(2,1)} async-done(((bf16[3584,512]{1,0:T(8,128)(2,1)}), bf16[448,512]{1,0:T(8,128)(2,1)}) %reduce-scatter.2.cloned.1.call-update) | async-done | bytes 458768 | tf_op jit(solution)/shard_map/reduce_scatter | solution.py:113
  146.1 1.1 dynamic-slice_bitcast_fusion
  147.2 3.1 %collective-permute-start.1 = (bf16[112,512]{1,0:T(8,128)(2,1)S(1)}, bf16[112,512]{1,0:T(8,128)(2,1)S(1)}, u32[]{:S(2)}, u32[]{:S(2)}) collective-permute-start(bf16[112,512]{1,0:T(8,128)(2,1)S(1)} %get-tuple-element.38), channel_id=1, source_target_pairs={{0,8},{1,9},{2,10},{3,11},{4,12},{5,13},{6,14},{7,15},{8,16},{9,17... | collective-permute-start | bytes 344072 | tf_op jit(solution)/shard_map/ppermute | solution.py:122
  150.3 4.3 %collective-permute-start.2 = (bf16[112,512]{1,0:T(8,128)(2,1)S(1)}, bf16[112,512]{1,0:T(8,128)(2,1)S(1)}, u32[]{:S(2)}, u32[]{:S(2)}) collective-permute-start(bf16[112,512]{1,0:T(8,128)(2,1)S(1)} %get-tuple-element.37), channel_id=1, source_target_pairs={{0,16},{1,17},{2,18},{3,19},{4,20},{5,21},{6,22},{7,23},{8,24},{9,... | collective-permute-start | bytes 344072 | tf_op jit(solution)/shard_map/ppermute | solution.py:122
  154.6 3.1 %collective-permute-start.3 = (bf16[112,512]{1,0:T(8,128)(2,1)S(1)}, bf16[112,512]{1,0:T(8,128)(2,1)S(1)}, u32[]{:S(2)}, u32[]{:S(2)}) collective-permute-start(bf16[112,512]{1,0:T(8,128)(2,1)S(1)} %get-tuple-element.36), channel_id=1, source_target_pairs={{0,24},{1,25},{2,26},{3,27},{4,28},{5,29},{6,30},{7,31},{8,0},{9,1... | collective-permute-start | bytes 344072 | tf_op jit(solution)/shard_map/ppermute | solution.py:122
  157.7 7.5 %all-to-all-done.5 = bf16[8,224,256]{2,1,0:T(8,128)(2,1)S(1)} async-done(((bf16[8,224,256]{2,1,0:T(8,128)(2,1)}), bf16[8,224,256]{2,1,0:T(8,128)(2,1)S(1)}, u32[]{:S(2)}, u32[]{:S(2)}) %all-to-all-start.5) | async-done | bytes 917536 | tf_op jit(solution)/shard_map/all_to_all | solution.py:17
  165.2 0.0 collective-permute-done.1
  165.2 0.0 collective-permute-done.2
  165.2 0.0 collective-permute-done.3
  165.2 2.4 %collective-permute-start.4 = (bf16[8,224,256]{2,1,0:T(8,128)(2,1)S(1)}, bf16[8,224,256]{2,1,0:T(8,128)(2,1)S(1)}, u32[]{:S(2)}, u32[]{:S(2)}) collective-permute-start(bf16[8,224,256]{2,1,0:T(8,128)(2,1)S(1)} %all-to-all-done.5), channel_id=1, source_target_pairs={{0,32},{32,0},{64,96},{96,64},{128,160},{160,128},{192,224},{224,1... | collective-permute-start | bytes 2752520 | tf_op jit(solution)/shard_map/ppermute | solution.py:124
  167.6 0.1 iota.11
  167.7 0.1 iota.12
  167.8 0.7 fusion.4
  168.5 1.2 collective-permute-done.4
  169.7 1.8 bitcast_select_fusion
  (10 shorter events, 0.1 us)
Async XLA Ops:
  7.2 55.0 %all-gather.2.cloned.1.call-start = ((), (), s32[]{:S(2)}) async-start(), calls=%async_computation.7 | async-start | bytes 2064384 | tf_op jit(solution)/shard_map/all_gather | solution.py:70
  39.0 25.3 %all-to-all-start.2 = ((bf16[4,448,512]{2,1,0:T(8,128)(2,1)}), bf16[4,448,512]{2,1,0:T(8,128)(2,1)S(1)}, u32[]{:S(2)}, u32[]{:S(2)}) async-start(bf16[4,448,512]{2,1,0:T(8,128)(2,1)} %broadcast_in_dim.29), calls=%async_computation.2 | async-start | bytes 3670016 | tf_op jit(solution)/shard_map/all_to_all | solution.py:17
  45.2 1.0 copy-start.5
  64.3 1.2 copy-start.1
  65.5 2.6 %copy-start.6 = (f32[512]{0:T(512)S(1)}, f32[512]{0:T(512)}, u32[]{:S(2)}) copy-start(f32[512]{0:T(512)} %param.8) | copy-start | bytes 6148
  65.5 9.6 %copy-start = (bf16[1792,512]{1,0:T(8,128)(2,1)S(1)}, bf16[1792,512]{1,0:T(8,128)(2,1)}, u32[]{:S(2)}) copy-start(bf16[1792,512]{1,0:T(8,128)(2,1)} %all-gather.2.cloned.1.call-done) | copy-start | bytes 5505028
  69.1 15.6 %all-to-all-start.3 = ((f32[32,4,512]{2,1,0:T(4,128)}), f32[32,4,512]{2,1,0:T(4,128)S(1)}, u32[]{:S(2)}, u32[]{:S(2)}) async-start(f32[32,4,512]{2,1,0:T(4,128)} %broadcast_in_dim.30), calls=%async_computation.3 | async-start | bytes 524288 | tf_op jit(solution)/shard_map/all_to_all | solution.py:89
  75.1 71.0 %reduce-scatter.2.cloned.1.call-start = ((), (), s32[]{:S(2)}) async-start(), calls=%async_computation.8 | async-start | bytes 4128768 | tf_op jit(solution)/shard_map/reduce_scatter | solution.py:113
  77.1 8.5 %copy-start.7 = (f32[512]{0:T(512)S(1)}, f32[512]{0:T(512)}, u32[]{:S(2)}) copy-start(f32[512]{0:T(512)} %param.9) | copy-start | bytes 6148
  84.7 1.5 copy-start.2
  86.2 0.7 copy-start.3
  90.7 10.6 %copy-start.4 = (bf16[256,512]{1,0:T(8,128)(2,1)S(1)}, bf16[256,512]{1,0:T(8,128)(2,1)}, u32[]{:S(2)}) copy-start(bf16[256,512]{1,0:T(8,128)(2,1)} %copy-done.3) | copy-start | bytes 786436
  90.7 10.6 %collective-permute-start = (bf16[1792,256]{1,0:T(8,128)(2,1)S(1)}, bf16[1792,256]{1,0:T(8,128)(2,1)S(1)}, u32[]{:S(2)}, u32[]{:S(2)}) collective-permute-start(bf16[1792,256]{1,0:T(8,128)(2,1)S(1)} %convolution_convert_fusion), channel_id=1, source_target_pairs={{0,32},{32,0},{64,96},{96,64},{128,160},{160,128},{192,224},{224,1... | collective-permute-start | bytes 2752520 | tf_op jit(solution)/shard_map/ppermute | solution.py:110
  135.3 29.9 %all-to-all-start.5 = ((bf16[8,224,256]{2,1,0:T(8,128)(2,1)}), bf16[8,224,256]{2,1,0:T(8,128)(2,1)S(1)}, u32[]{:S(2)}, u32[]{:S(2)}) async-start(bf16[8,224,256]{2,1,0:T(8,128)(2,1)} %broadcast_in_dim.31), calls=%async_computation.5 | async-start | bytes 1835008 | tf_op jit(solution)/shard_map/all_to_all | solution.py:17
  147.2 18.0 %collective-permute-start.1 = (bf16[112,512]{1,0:T(8,128)(2,1)S(1)}, bf16[112,512]{1,0:T(8,128)(2,1)S(1)}, u32[]{:S(2)}, u32[]{:S(2)}) collective-permute-start(bf16[112,512]{1,0:T(8,128)(2,1)S(1)} %get-tuple-element.38), channel_id=1, source_target_pairs={{0,8},{1,9},{2,10},{3,11},{4,12},{5,13},{6,14},{7,15},{8,16},{9,17... | collective-permute-start | bytes 344072 | tf_op jit(solution)/shard_map/ppermute | solution.py:122
  150.3 14.9 %collective-permute-start.2 = (bf16[112,512]{1,0:T(8,128)(2,1)S(1)}, bf16[112,512]{1,0:T(8,128)(2,1)S(1)}, u32[]{:S(2)}, u32[]{:S(2)}) collective-permute-start(bf16[112,512]{1,0:T(8,128)(2,1)S(1)} %get-tuple-element.37), channel_id=1, source_target_pairs={{0,16},{1,17},{2,18},{3,19},{4,20},{5,21},{6,22},{7,23},{8,24},{9,... | collective-permute-start | bytes 344072 | tf_op jit(solution)/shard_map/ppermute | solution.py:122
  154.6 10.6 %collective-permute-start.3 = (bf16[112,512]{1,0:T(8,128)(2,1)S(1)}, bf16[112,512]{1,0:T(8,128)(2,1)S(1)}, u32[]{:S(2)}, u32[]{:S(2)}) collective-permute-start(bf16[112,512]{1,0:T(8,128)(2,1)S(1)} %get-tuple-element.36), channel_id=1, source_target_pairs={{0,24},{1,25},{2,26},{3,27},{4,28},{5,29},{6,30},{7,31},{8,0},{9,1... | collective-permute-start | bytes 344072 | tf_op jit(solution)/shard_map/ppermute | solution.py:122
  165.2 4.5 %collective-permute-start.4 = (bf16[8,224,256]{2,1,0:T(8,128)(2,1)S(1)}, bf16[8,224,256]{2,1,0:T(8,128)(2,1)S(1)}, u32[]{:S(2)}, u32[]{:S(2)}) collective-permute-start(bf16[8,224,256]{2,1,0:T(8,128)(2,1)S(1)} %all-to-all-done.5), channel_id=1, source_target_pairs={{0,32},{32,0},{64,96},{96,64},{128,160},{160,128},{192,224},{224,1... | collective-permute-start | bytes 2752520 | tf_op jit(solution)/shard_map/ppermute | solution.py:124
Sparse Core Ops, SparseCore 0:
  18.3 43.7 all-gather.1
  90.8 55.1 reduce-scatter.1
